TPU v7x, 512 devices: a whole 4x4x16 slice. The times are simulated.
512 devices in a mesh: event: 32 (over z, core), mesh: 16 (over x, y).
Axes of the slice: x: 4, y: 4, z: 16, core: 2. Of those that a mesh axis runs over, the one named last changes fastest.
Arguments:
- forward_start: float32 [32, 3, 125, 2048], P('event', None, None, 'mesh'), may hold values from -6 to 6
- adjoint_start: float32 [32, 3, 125, 2048], P('event', None, None, 'mesh'), may hold values from -6 to 6
- stiffness: float32 [125, 125], replicated
- projection: float32 [125, 64], replicated, may hold values from -0.5 to 0.5
- material: float32 [32, 2048], P('event', 'mesh'), may hold values from 0.5 to 2
- neighbours: int32 [32, 6, 2048], P('event', None, 'mesh'), may hold values from 0 to 2047, as said below
- destinations: int32 [32, 2048], P('event', 'mesh'), may hold values from 0 to 2047
- counts: int32 [32, 16], P('event', 'mesh'), may hold values from 32 to 128, as said below
- smoothing: float32 [4, 2048], P(None, ('event', 'mesh')), may hold values from 0.02 to 0.12
Outputs:
- forward_final: float32 [32, 3, 125, 2048], P('event', None, None, 'mesh')
- tiles: float32 [64, 2048], P(None, ('event', 'mesh'))
Inputs may be any that keep to these rules, and one draw needn't show every extreme that they name: `counts`: in every event one partition holds exactly 128 live elements and another exactly 32; live elements fill a partition's first slots. `neighbours`: A neighbour slot lies in the element's own partition, or in the previous or next partition of the same event (wrapping around), and then among that partition's first 32 slots.
All inputs are finite; a program needn't handle non-finite values.
Results may differ from a plain program's by a relative error of at most 0.0003.
Values sent between devices are 32-bit elements; how exact they have to be, the bound alone decides.
No kernel may reach another device: no remote copies, remote signals or barrier semaphores. Data moves between devices by JAX's collectives and lax.ppermute only.
A program may use at most 64 MiB of HBM per device.

v0:
```python
import math

import jax
import jax.numpy as jnp
from jax import lax
from jax.sharding import PartitionSpec as P

STEPS = 2


time_square = 0.4
penalty = 0.5
partner_face = (1, 0, 3, 2, 5, 4)


def padded_2(x, sides, width, wrap):
    for axis, dim in sides:
        count, length = (lax.axis_size(axis), x.shape[dim])
        up = [(i, (i + 1) % count) for i in range(count if wrap else count - 1)]
        down = [(j, i) for i, j in up]
        last = lax.slice_in_dim(x, length - width, length, axis=dim)
        first = lax.slice_in_dim(x, 0, width, axis=dim)
        before = lax.ppermute(last, axis, up)
        after = lax.ppermute(first, axis, down)
        x = jnp.concatenate([before, x, after], axis=dim)
    return x


def element_faces(field):
    elements = field.shape[-1]
    cube = field.reshape(3, 5, 5, 5, elements)
    sheets = [
        cube[:, 0],
        cube[:, 4],
        cube[:, :, 0],
        cube[:, :, 4],
        cube[:, :, :, 0],
        cube[:, :, :, 4],
    ]
    return jnp.stack(sheets).reshape(6, 3, 25, elements)


def lift_faces(jumps):
    elements = jumps.shape[-1]
    sheets = jumps.reshape(6, 3, 5, 5, elements)
    keep = (0, 0)
    lifted = jnp.pad(sheets[0][:, None], (keep, (0, 4), keep, keep, keep))
    lifted = lifted + jnp.pad(sheets[1][:, None], (keep, (4, 0), keep, keep, keep))
    lifted = lifted + jnp.pad(sheets[2][:, :, None], (keep, keep, (0, 4), keep, keep))
    lifted = lifted + jnp.pad(sheets[3][:, :, None], (keep, keep, (4, 0), keep, keep))
    lifted = lifted + jnp.pad(sheets[4][:, :, :, None], (keep, keep, keep, (0, 4), keep))
    lifted = lifted + jnp.pad(sheets[5][:, :, :, None], (keep, keep, keep, (4, 0), keep))
    return lifted.reshape(3, 125, elements)


def node_laplace(values, coefs):
    width = values.shape[-1]
    cube = values.reshape(4, 4, 4, width)
    padded = jnp.pad(cube, ((1, 1), (1, 1), (1, 1), (0, 0)))
    first_dir = padded[2:, 1:-1, 1:-1] + padded[:-2, 1:-1, 1:-1] - 2.0 * cube
    second_dir = padded[1:-1, 2:, 1:-1] + padded[1:-1, :-2, 1:-1] - 2.0 * cube
    third_dir = padded[1:-1, 1:-1, 2:] + padded[1:-1, 1:-1, :-2] - 2.0 * cube
    summed = coefs[0] * first_dir + coefs[1] * second_dir + coefs[2] * third_dir
    return summed.reshape(64, width)


def smooth_columns(values, coefs):
    middle = values[:, 1:-1]
    chain = values[:, :-2] + values[:, 2:] - 2.0 * middle
    return middle + coefs[0] * chain + node_laplace(middle, coefs[1:])


def per_device(
    forward_start,
    adjoint_start,
    stiffness,
    projection,
    material,
    neighbours,
    destinations,
    counts,
    smoothing,
):
    elements = forward_start.shape[-1]
    boundary = elements // 4
    tile_width = smoothing.shape[1]
    mesh_size = lax.axis_size("mesh")
    event_size = lax.axis_size("event")
    my_partition = lax.axis_index("mesh")
    slots = jnp.arange(elements, dtype=jnp.int32)
    live = (slots < counts[0, 0]).astype(jnp.float32)
    fields = jnp.stack([forward_start[0], adjoint_start[0]]) * live
    previous = fields
    target = neighbours[0] // elements
    local_slot = neighbours[0] % elements
    relative = (target - my_partition + mesh_size) % mesh_size
    pool_index = jnp.where(
        relative == 0,
        local_slot,
        jnp.where(relative == 1, elements + 2 * boundary + local_slot, elements + local_slot),
    )
    material_row = material[0]
    kernel = jnp.zeros((stiffness.shape[0], elements), jnp.float32)
    for step_index in range(STEPS):
        strain = jnp.einsum("nm,fcme->fcne", stiffness, fields, precision=lax.Precision.HIGHEST)
        kernel = kernel + jnp.sum(fields[0] * strain[1], axis=0)
        faces = jax.vmap(element_faces)(fields)
        rim_faces = padded_2(faces[..., :boundary], (("mesh", 4),), boundary, True)
        pool = jnp.concatenate([faces, rim_faces], axis=4)
        across = jnp.stack(
            [jnp.take(pool[:, partner_face[face]], pool_index[face], axis=3) for face in range(6)],
            axis=1,
        )
        force = -material_row * strain + penalty * jax.vmap(lift_faces)(across - faces)
        following = live * (2.0 * fields - previous + time_square * force)
        previous, fields = (fields, following)
    scale = math.sqrt(tile_width / elements) / STEPS
    blocks = jnp.dot(projection.T, kernel, precision=lax.Precision.HIGHEST) * scale
    total_tiles = tile_width * event_size * mesh_size
    destination_row = destinations[0]
    dense = (
        jnp.zeros((projection.shape[1], total_tiles), jnp.float32)
        .at[:, destination_row]
        .add(blocks)
    )
    tiles = lax.psum_scatter(dense, ("event", "mesh"), scatter_dimension=1, tiled=True)
    for pass_index in range(2):
        padded = padded_2(tiles, ((("event", "mesh"), 1),), 1, False)
        tiles = smooth_columns(padded, smoothing)
    return (fields[0][None], tiles)


def solution(mesh):
    in_specs = (
        P("event", None, None, "mesh"),
        P("event", None, None, "mesh"),
        P(),
        P(),
        P("event", "mesh"),
        P("event", None, "mesh"),
        P("event", "mesh"),
        P("event", "mesh"),
        P(None, ("event", "mesh")),
    )
    out_specs = (P("event", None, None, "mesh"), P(None, ("event", "mesh")))
    return jax.shard_map(
        per_device, mesh=mesh, in_specs=in_specs, out_specs=out_specs, check_vma=False
    )
```

profile of v0, /device:TPU:1, one launch (start us, length us, event | category | flops | bytes accessed | tf_op | source)
XLA Modules:
  0.0 600.0 jit_solution(9176218650003830220)
XLA Ops:
  7.9 1.4 maximum_multiply_fusion.1
  9.4 4.0 collective-permute-start
  13.5 5.6 collective-permute-start.1
  19.1 0.9 copy-done.3
  23.0 1.5 collective-permute-done.1
  24.5 1.2 pad_maximum_fusion
  26.8 1.1 gather_fusion
  29.3 1.1 gather_fusion.1
  31.8 1.1 gather_fusion.2
  34.3 1.1 gather_fusion.3
  36.8 1.1 gather_fusion.4
  39.3 1.1 gather_fusion.5
  42.9 5.2 collective-permute-start.2
  48.1 4.0 collective-permute-start.3
  52.6 3.3 collective-permute-done.2
  55.9 2.5 collective-permute-done.3
  58.3 1.2 pad_maximum_fusion.1
  60.7 1.8 gather_fusion.10
  63.4 1.8 gather_fusion.11
  65.2 1.7 select_bitcast_fusion
  68.7 1.9 gather_fusion.8
  71.4 1.8 gather_fusion.9
  73.3 1.7 select_bitcast_fusion.2
  76.7 1.8 gather_fusion.6
  79.4 1.8 gather_fusion.7
  81.3 1.7 select_bitcast_fusion.4
  89.7 2.0 scatter_custom_fusion
  93.3 477.9 %all-reduce.17.cloned.1.call-done = f32[64,2048]{0,1:T(8,128)} async-done(((f32[64,2048]{0,1:T(8,128)}), f32[64,2048]{0,1:T(8,128)}) %all-reduce.17.cloned.1.call-update) | async-done | bytes 524304
  571.9 3.0 collective-permute-start.4
  575.0 5.8 collective-permute-start.5
  582.4 1.9 collective-permute-start.6
  584.3 7.5 %collective-permute-start.7 = (f32[64,1]{0,1:T(1,128)S(1)}, f32[64,1]{0,1:T(1,128)S(1)}, u32[]{:S(2)}, u32[]{:S(2)}) collective-permute-start(f32[64,1]{0,1:T(1,128)S(1)} %get-tuple-element.63), channel_id=1, source_target_pairs={{1,0},{2,1},{3,2},{4,3},{5,4},{6,5},{7,6},{8,7},{9,8},{10,9},{11,1... | collective-permute-start | bytes 776 | tf_op jit(solution)/shard_map/ppermute | solution.py:24
  (138 shorter events, 32.8 us)
Async XLA Ops:
  7.2 34.6 %copy-start = (f32[125,125]{1,0:T(8,128)S(1)}, f32[125,125]{1,0:T(8,128)}, u32[]{:S(2)}) copy-start(f32[125,125]{1,0:T(8,128)} %param.13) | copy-start | bytes 187504
  7.2 563.9 %all-reduce.17.cloned.1.call-start = ((), (), s32[]{:S(2)}) async-start(), calls=%async_computation | async-start | bytes 2097152
  9.3 9.7 %copy-start.2 = (f32[1,3,125,128]{3,0,2,1:T(1,128)S(1)}, f32[1,3,125,128]{3,0,2,1:T(1,128)}, u32[]{:S(2)}) copy-start(f32[1,3,125,128]{3,0,2,1:T(1,128)} %param.11) | copy-start | bytes 576004
  9.4 13.6 %collective-permute-start = (f32[2,6,3,25,32]{4,0,3,2,1:T(2,128)S(1)}, f32[2,6,3,25,32]{4,0,3,2,1:T(2,128)S(1)}, u32[]{:S(2)}, u32[]{:S(2)}) collective-permute-start(f32[2,6,3,25,32]{4,0,3,2,1:T(2,128)S(1)} %bitcast.252), channel_id=1, source_target_pairs={{0,1},{1,2},{2,3},{3,4},{4,5},{5,6},{6,7},{7,8},{8,9},{9,10},{10,1... | collective-permute-start | bytes 345608 | tf_op jit(solution)/shard_map/ppermute | solution.py:23
  13.5 11.0 %collective-permute-start.1 = (f32[2,6,3,25,32]{4,0,3,2,1:T(2,128)S(1)}, f32[2,6,3,25,32]{4,0,3,2,1:T(2,128)S(1)}, u32[]{:S(2)}, u32[]{:S(2)}) collective-permute-start(f32[2,6,3,25,32]{4,0,3,2,1:T(2,128)S(1)} %bitcast.253), channel_id=1, source_target_pairs={{1,0},{2,1},{3,2},{4,3},{5,4},{6,5},{7,6},{8,7},{9,8},{10,9},{11,1... | collective-permute-start | bytes 345608 | tf_op jit(solution)/shard_map/ppermute | solution.py:24
  19.1 0.9 copy-start.3
  20.0 0.7 copy-start.8
  20.8 0.7 copy-start.10
  21.4 0.7 copy-start.11
  42.9 13.0 %collective-permute-start.2 = (f32[2,6,3,25,32]{4,0,3,2,1:T(2,128)S(1)}, f32[2,6,3,25,32]{4,0,3,2,1:T(2,128)S(1)}, u32[]{:S(2)}, u32[]{:S(2)}) collective-permute-start(f32[2,6,3,25,32]{4,0,3,2,1:T(2,128)S(1)} %bitcast.256), channel_id=1, source_target_pairs={{0,1},{1,2},{2,3},{3,4},{4,5},{5,6},{6,7},{7,8},{8,9},{9,10},{10,1... | collective-permute-start | bytes 345608 | tf_op jit(solution)/shard_map/ppermute | solution.py:23
  48.1 10.2 %collective-permute-start.3 = (f32[2,6,3,25,32]{4,0,3,2,1:T(2,128)S(1)}, f32[2,6,3,25,32]{4,0,3,2,1:T(2,128)S(1)}, u32[]{:S(2)}, u32[]{:S(2)}) collective-permute-start(f32[2,6,3,25,32]{4,0,3,2,1:T(2,128)S(1)} %bitcast.257), channel_id=1, source_target_pairs={{1,0},{2,1},{3,2},{4,3},{5,4},{6,5},{7,6},{8,7},{9,8},{10,9},{11,1... | collective-permute-start | bytes 345608 | tf_op jit(solution)/shard_map/ppermute | solution.py:24
  84.1 1.0 copy-start.4
  85.1 0.9 copy-start.6
  86.0 0.9 copy-start.5
  87.6 1.0 copy-start.1
  88.6 0.8 copy-start.7
  91.7 0.7 copy-start.9
  571.9 9.1 %collective-permute-start.4 = (f32[64,1]{0,1:T(1,128)S(1)}, f32[64,1]{0,1:T(1,128)S(1)}, u32[]{:S(2)}, u32[]{:S(2)}) collective-permute-start(f32[64,1]{0,1:T(1,128)S(1)} %get-tuple-element.70), channel_id=1, source_target_pairs={{0,1},{1,2},{2,3},{3,4},{4,5},{5,6},{6,7},{7,8},{8,9},{9,10},{10,1... | collective-permute-start | bytes 776 | tf_op jit(solution)/shard_map/ppermute | solution.py:23
  575.0 6.6 %collective-permute-start.5 = (f32[64,1]{0,1:T(1,128)S(1)}, f32[64,1]{0,1:T(1,128)S(1)}, u32[]{:S(2)}, u32[]{:S(2)}) collective-permute-start(f32[64,1]{0,1:T(1,128)S(1)} %get-tuple-element.71), channel_id=1, source_target_pairs={{1,0},{2,1},{3,2},{4,3},{5,4},{6,5},{7,6},{8,7},{9,8},{10,9},{11,1... | collective-permute-start | bytes 776 | tf_op jit(solution)/shard_map/ppermute | solution.py:24
  582.4 9.6 %collective-permute-start.6 = (f32[64,1]{0,1:T(1,128)S(1)}, f32[64,1]{0,1:T(1,128)S(1)}, u32[]{:S(2)}, u32[]{:S(2)}) collective-permute-start(f32[64,1]{0,1:T(1,128)S(1)} %get-tuple-element.62), channel_id=1, source_target_pairs={{0,1},{1,2},{2,3},{3,4},{4,5},{5,6},{6,7},{7,8},{8,9},{9,10},{10,1... | collective-permute-start | bytes 776 | tf_op jit(solution)/shard_map/ppermute | solution.py:23
  584.3 8.2 %collective-permute-start.7 = (f32[64,1]{0,1:T(1,128)S(1)}, f32[64,1]{0,1:T(1,128)S(1)}, u32[]{:S(2)}, u32[]{:S(2)}) collective-permute-start(f32[64,1]{0,1:T(1,128)S(1)} %get-tuple-element.63), channel_id=1, source_target_pairs={{1,0},{2,1},{3,2},{4,3},{5,4},{6,5},{7,6},{8,7},{9,8},{10,9},{11,1... | collective-permute-start | bytes 776 | tf_op jit(solution)/shard_map/ppermute | solution.py:24
Sparse Core Ops, SparseCore 0:
  91.8 479.2 all-reduce.16
where the time goes:
time: 603 us; the launch traced here: 600 us
  waiting for transfers between devices  486 us (81%)
  local copies, waits for them, and re-layouts  44.2 us (7%)
  starting transfers between devices  37.2 us (6%)
  other arithmetic  15.8 us (3%)
  between operations  15.5 us (3%)
    unnamed x2, waiting for transfers between devices  478 us
    ppermute x4, starting transfers between devices, padded_2(): after = lax.ppermute(first, axis, down)  22.9 us
    gather x12, local copies, waits for them, and re-layouts, per_device(): jnp.take(pool[:, partner_face[face]], pool_index[face], axis=3)  17.8 us
    ppermute x4, starting transfers between devices, padded_2(): before = lax.ppermute(last, axis, up)  14.2 us
  transfers between devices with their start and end apart: 9, of which 7 were waited for; matrix products, arithmetic and copies ran while one was open for 0% of the time, Pallas kernels for 0%

commit v1 on v0

v1 whole, which is shorter than its diff:
```python
import math

import jax
import jax.numpy as jnp
from jax import lax
from jax.experimental import pallas as pl
from jax.experimental.pallas import tpu as pltpu
from jax.sharding import PartitionSpec as P

STEPS = 2
NODES = 125
RIM = 32
SHEET = 32
FACES = 6
F32, BF16, I32 = jnp.float32, jnp.bfloat16, jnp.int32
partner_face = (1, 0, 3, 2, 5, 4)

VMEM = pl.BlockSpec(memory_space=pltpu.VMEM)
SMEM = pl.BlockSpec(memory_space=pltpu.SMEM)
PARAMS = pltpu.CompilerParams(vmem_limit_bytes=40 * 2**20)


def shape(*dims):
    return jax.ShapeDtypeStruct(dims, F32)


def iota(dims, axis):
    return lax.broadcasted_iota(I32, dims, axis)


def halves(x):
    high = x.astype(BF16)
    return high, (x - high.astype(F32)).astype(BF16)


def dot(a, b):
    return lax.dot_general(a, b, (((1,), (0,)), ((), ())), preferred_element_type=F32)


def face_nodes(dims, axis):
    row = iota(dims, axis)
    face, q = row // SHEET, row % SHEET
    a = sum((q >= 5 * i).astype(I32) for i in range(1, 5))
    b = q - 5 * a
    node = jnp.where(face == 0, q, q + 100)
    node = jnp.where(face == 2, 25 * a + b, node)
    node = jnp.where(face == 3, 25 * a + 20 + b, node)
    node = jnp.where(face == 4, 5 * q, node)
    node = jnp.where(face == 5, 5 * q + 4, node)
    return jnp.where(q < 25, node, -1)


def picker():
    dims = (FACES * SHEET, 128)
    return jnp.where(face_nodes(dims, 0) == iota(dims, 1), 1.0, 0.0).astype(BF16)


def lifter():
    dims = (128, FACES * SHEET)
    return jnp.where(face_nodes(dims, 1) == iota(dims, 0), 1.0, 0.0).astype(BF16)


def padded(ref, index):
    return jnp.concatenate([ref[index], jnp.zeros((128 - NODES, 128), F32)], axis=0)


def stacked(fields):
    high, low = halves(jnp.concatenate(fields, axis=1))
    return jnp.concatenate([high, low], axis=0)


def pack_rim(fields):
    lane = iota((128, 128), 1)
    out = fields[0]
    for k in range(1, 4):
        if k < len(fields):
            out = jnp.where(lane < RIM * k, out, pltpu.roll(fields[k], RIM * k, 1))
    return jnp.where(lane < RIM * len(fields), out, 0.0)


def pack_kernel(count_ref, forward_ref, adjoint_ref, rim_ref):
    live = (iota((128, 128), 1) < count_ref[0, 0]).astype(F32)
    fields = [padded(ref, c) * live for ref in (forward_ref, adjoint_ref) for c in range(3)]
    rim_ref[0] = pack_rim(fields[:4])
    rim_ref[1] = pack_rim(fields[4:])


def own_kernel(count_ref, forward_ref, adjoint_ref, stiff_ref, strain_ref, face_ref, kernel_ref):
    live = (iota((128, 128), 1) < count_ref[0, 0]).astype(F32)
    fields = [padded(ref, c) * live for ref in (forward_ref, adjoint_ref) for c in range(3)]
    strain, faces = products(stiff_ref, fields, fields)
    for k in range(6):
        strain_ref[k] = strain[k]
        face_ref[k] = faces[k]
    kernel_ref[...] = sum(fields[c] * strain[3 + c] for c in range(3))


def padded_stiffness(stiff_ref):
    wide = jnp.concatenate([stiff_ref[...], jnp.zeros((NODES, 128 - NODES), F32)], axis=1)
    return jnp.concatenate([wide, jnp.zeros((128 - NODES, 128), F32)], axis=0)


def products(stiff_ref, fields, faced):
    n, m = len(fields), len(faced)
    high, low = halves(padded_stiffness(stiff_ref))
    x = stacked(fields)
    both = dot(jnp.concatenate([high, high], axis=1), x)
    strain = both + dot(low, x[:128])
    pick = picker()
    faces = dot(jnp.concatenate([pick, pick], axis=1), x[:, : 128 * m])
    return (
        [strain[:, 128 * k : 128 * (k + 1)] for k in range(n)],
        [faces[:, 128 * k : 128 * (k + 1)] for k in range(m)],
    )


def rim_faces(groups):
    x = stacked(groups)
    pick = picker()
    faces = dot(jnp.concatenate([pick, pick], axis=1), x)
    return [faces[:, 128 * k : 128 * (k + 1)] for k in range(len(groups))]


def lifted(place_ref, near_ref, own, before, after):
    mine, parts = place_ref[0], place_ref[1]
    jumps = [[] for _ in own]
    for face in range(FACES):
        p = partner_face[face]
        near = jnp.broadcast_to(near_ref[face : face + 1, :], (SHEET, 128))
        target, slot = near // 128, near % 128
        relative = target - mine
        relative = jnp.where(relative < 0, relative + parts, relative)
        at_home, is_next = relative == 0, relative == 1
        rim_slot = slot % RIM
        for k in range(len(own)):
            group, q = k // 4, k % 4
            rows = slice(SHEET * p, SHEET * (p + 1))
            here = jnp.take_along_axis(own[k][rows], slot, axis=1, mode="promise_in_bounds")
            prev = jnp.take_along_axis(before[group][rows], rim_slot + RIM * q, axis=1, mode="promise_in_bounds")
            foll = jnp.take_along_axis(after[group][rows], rim_slot + RIM * q, axis=1, mode="promise_in_bounds")
            across = jnp.where(at_home, here, jnp.where(is_next, foll, prev))
            jumps[k].append(across - own[k][SHEET * face : SHEET * (face + 1)])
    high, low = halves(jnp.concatenate([jnp.concatenate(j, axis=0) for j in jumps], axis=1))
    lift = lifter()
    out = dot(lift, high) + dot(lift, low)
    return [out[:, 128 * k : 128 * (k + 1)] for k in range(len(own))]


def step_kernel(
    n_event, n_mesh, tile_width, scale,
    count_ref, place_ref, forward_ref, adjoint_ref, strain_ref, face_ref, kernel_ref, before_ref, after_ref,
    near_ref, material_ref, stiff_ref, project_ref, destination_ref,
    forward_one_ref, strain_one_ref, face_one_ref, rim_ref, dense_ref,
):
    live = (iota((128, 128), 1) < count_ref[0, 0]).astype(F32)
    material = jnp.broadcast_to(material_ref[...], (128, 128))
    before = rim_faces([before_ref[0], before_ref[1]])
    after = rim_faces([after_ref[0], after_ref[1]])
    lift = lifted(place_ref, near_ref, [face_ref[k] for k in range(6)], before, after)
    fields = []
    for k in range(6):
        start = padded(forward_ref if k < 3 else adjoint_ref, k % 3) * live
        force = 0.5 * lift[k] - material * strain_ref[k]
        fields.append(live * (start + 0.4 * force))
    rim_ref[...] = pack_rim(fields[:3])
    strain, faces = products(stiff_ref, fields, fields[:3])
    for c in range(3):
        forward_one_ref[c] = fields[c]
        strain_one_ref[c] = strain[c]
        face_one_ref[c] = faces[c]
    kernel = kernel_ref[...] + sum(fields[c] * strain[3 + c] for c in range(3))
    k_high, k_low = halves(kernel.T)
    project = jnp.concatenate([project_ref[...], jnp.zeros((128 - NODES, 64), F32)], axis=0)
    p_high, p_low = halves(project)
    blocks = (dot(k_high, p_high) + (dot(k_high, p_low) + dot(k_low, p_high))) * scale
    b_high, b_low = halves(blocks)
    none = jnp.zeros((128, 64), BF16)
    right = jnp.concatenate(
        [
            jnp.concatenate([b_high, none, b_low, none], axis=1),
            jnp.concatenate([none, b_high, none, b_low], axis=1),
        ],
        axis=0,
    )
    rows = 4 * n_event
    row = iota((rows, 128), 0)
    tile = (row // 4) * (n_mesh * tile_width) - 2 + row % 4
    wanted = jnp.broadcast_to(destination_ref[...], (rows, 128))
    offset = wanted - tile
    for m in range(n_mesh):
        hit = [jnp.where(offset == m * tile_width + 4 * h, 1.0, 0.0).astype(BF16) for h in range(2)]
        out = dot(jnp.concatenate(hit, axis=1), right)
        dense_ref[m] = out[:, :128] + out[:, 128:]


def last_kernel(
    count_ref, place_ref, forward_ref, one_ref, strain_ref, face_ref, before_ref, after_ref, near_ref, material_ref,
    final_ref,
):
    live = (iota((128, 128), 1) < count_ref[0, 0]).astype(F32)
    material = jnp.broadcast_to(material_ref[...], (128, 128))
    before = rim_faces([before_ref[...]])
    after = rim_faces([after_ref[...]])
    lift = lifted(place_ref, near_ref, [face_ref[k] for k in range(3)], before, after)
    for c in range(3):
        force = 0.5 * lift[c] - material * strain_ref[c]
        out = live * (2.0 * one_ref[c] - padded(forward_ref, c) * live + 0.4 * force)
        final_ref[c] = out[:NODES]


def sum_kernel(x_ref, o_ref):
    total = x_ref[0]
    for i in range(1, x_ref.shape[0]):
        total = total + x_ref[i]
    o_ref[...] = total


def smooth_kernel(x_ref, coef_ref, o_ref):
    total = x_ref[0]
    for i in range(1, x_ref.shape[0]):
        total = total + x_ref[i]
    both = jnp.concatenate([total, pltpu.roll(total, 64, 1)], axis=0)
    x = both.T[:64]
    node = iota((64, 8), 0)
    tile = iota((64, 8), 1)
    for _ in range(2):
        right = jnp.where(tile < 7, pltpu_shift(x, -1, 1), 0.0)
        left = jnp.where(tile > 0, pltpu_shift(x, 1, 1), 0.0)
        out = x + coef_ref[0:1, :] * (left + right - 2.0 * x)
        for d, stride in ((1, 16), (2, 4), (3, 1)):
            place = (node // stride) % 4
            up = jnp.where(place < 3, pltpu_shift(x, -stride, 0), 0.0)
            down = jnp.where(place > 0, pltpu_shift(x, stride, 0), 0.0)
            out = out + coef_ref[d : d + 1, :] * (up + down - 2.0 * x)
        x = out
    o_ref[...] = x[:, 2:6]


def pltpu_shift(x, by, axis):
    n = x.shape[axis]
    cut = (n - by) % n
    return jnp.concatenate([lax.slice_in_dim(x, cut, n, axis=axis), lax.slice_in_dim(x, 0, cut, axis=axis)], axis=axis)


def exchange(x, axis, wrap):
    count = lax.axis_size(axis)
    up = [(i, (i + 1) % count) for i in range(count if wrap else count - 1)]
    down = [(j, i) for i, j in up]
    return up, down


def per_device(
    forward_start, adjoint_start, stiffness, projection, material, neighbours, destinations, counts, smoothing
):
    elements = forward_start.shape[-1]
    tile_width = smoothing.shape[1]
    n_mesh, n_event = lax.axis_size("mesh"), lax.axis_size("event")
    scale = math.sqrt(tile_width / elements) / STEPS
    forward, adjoint, near = forward_start[0], adjoint_start[0], neighbours[0]
    place = jnp.stack([lax.axis_index("mesh"), jnp.int32(n_mesh)]).astype(I32)

    rim = pl.pallas_call(
        pack_kernel, out_shape=shape(2, 128, 128), in_specs=[SMEM, VMEM, VMEM], out_specs=VMEM, compiler_params=PARAMS
    )(counts, forward, adjoint)
    up, down = exchange(rim, "mesh", True)
    before, after = lax.ppermute(rim, "mesh", up), lax.ppermute(rim, "mesh", down)
    all_up, all_down = exchange(smoothing, ("event", "mesh"), False)
    coef_before = lax.ppermute(smoothing[:, tile_width - 1 :], ("event", "mesh"), all_up)
    coef_after = lax.ppermute(smoothing[:, :1], ("event", "mesh"), all_down)
    edge = jnp.zeros((4, 1), F32)
    coefs = jnp.concatenate([edge, coef_before, smoothing, coef_after, edge], axis=1)

    strain, faces, kernel = pl.pallas_call(
        own_kernel,
        out_shape=(shape(6, 128, 128), shape(6, 192, 128), shape(128, 128)),
        in_specs=[SMEM, VMEM, VMEM, VMEM],
        out_specs=(VMEM,) * 3,
        compiler_params=PARAMS,
    )(counts, forward, adjoint, stiffness)

    def one_step(*refs):
        step_kernel(n_event, n_mesh, tile_width, scale, *refs)

    one, strain_one, face_one, rim_one, dense = pl.pallas_call(
        one_step,
        out_shape=(
            shape(3, 128, 128),
            shape(3, 128, 128),
            shape(3, 192, 128),
            shape(128, 128),
            shape(n_mesh, 4 * n_event, 128),
        ),
        in_specs=[SMEM, SMEM] + [VMEM] * 12,
        out_specs=(VMEM,) * 5,
        compiler_params=PARAMS,
    )(
        counts, place, forward, adjoint, strain, faces, kernel, before, after,
        near, material, stiffness, projection, destinations,
    )
    before, after = lax.ppermute(rim_one, "mesh", up), lax.ppermute(rim_one, "mesh", down)

    parts = lax.all_to_all(dense, "mesh", 0, 0, tiled=True)
    partial = pl.pallas_call(
        sum_kernel, out_shape=shape(4 * n_event, 128), in_specs=[VMEM], out_specs=VMEM, compiler_params=PARAMS
    )(parts)
    final = pl.pallas_call(
        last_kernel,
        out_shape=shape(3, NODES, 128),
        in_specs=[SMEM, SMEM] + [VMEM] * 8,
        out_specs=VMEM,
        compiler_params=PARAMS,
    )(counts, place, forward, one, strain_one, face_one, before, after, near, material)
    pieces = lax.all_to_all(partial.reshape(n_event, 4, 128), "event", 0, 0, tiled=True)
    tiles = pl.pallas_call(
        smooth_kernel, out_shape=shape(64, tile_width), in_specs=[VMEM, VMEM], out_specs=VMEM, compiler_params=PARAMS
    )(pieces, coefs)
    return final[None], tiles


def solution(mesh):
    in_specs = (
        P("event", None, None, "mesh"),
        P("event", None, None, "mesh"),
        P(),
        P(),
        P("event", "mesh"),
        P("event", None, "mesh"),
        P("event", "mesh"),
        P("event", "mesh"),
        P(None, ("event", "mesh")),
    )
    out_specs = (P("event", None, None, "mesh"), P(None, ("event", "mesh")))
    return jax.shard_map(per_device, mesh=mesh, in_specs=in_specs, out_specs=out_specs, check_vma=False)
```

time: 603 us -> 83.9 us (0.14)
  the two profiles are of different devices: /device:TPU:1 before, /device:TPU:127 now
where the time goes in v1:
time: 83.9 us; the launch traced here: 83.4 us
  starting transfers between devices  41.9 us (50%)
  blocking collectives  17 us (20%)
  waiting for transfers between devices  13.5 us (16%)
  Pallas kernels  5.62 us (7%)
  local copies, waits for them, and re-layouts  3.94 us (5%)
  between operations  1.42 us (2%)
    all_to_all x1, starting transfers between devices, per_device(): lax.all_to_all(partial.reshape(n_event, 4, 128), 'event', 0, 0, tiled=True)  17.3 us
    all_to_all x1, blocking collectives, per_device(): parts = lax.all_to_all(dense, 'mesh', 0, 0, tiled=True)  17 us
    ppermute x1, starting transfers between devices, per_device(): lax.ppermute(smoothing[:, tile_width - 1:], ('event', 'mesh'), all_up)  9.59 us
    ppermute x1, waiting for transfers between devices, per_device(): coef_after = lax.ppermute(smoothing[:, :1], ('event', 'mesh'), all_down)  8.39 us
    ppermute x1, starting transfers between devices, per_device(): lax.ppermute(rim_one, 'mesh', up)  5.8 us
    ppermute x1, waiting for transfers between devices, per_device(): lax.ppermute(rim, 'mesh', down)  5.09 us
    unnamed x17, local copies, waits for them, and re-layouts  3.77 us
    ppermute x1, starting transfers between devices, per_device(): lax.ppermute(rim, 'mesh', down)  3.36 us
  transfers between devices with their start and end apart: 7, of which 2 were waited for; matrix products, arithmetic and copies ran while one was open for 1% of the time, Pallas kernels for 2%

profile of v1, /device:TPU:127, one launch (start us, length us, event | category | flops | bytes accessed | tf_op | source)
XLA Modules:
  0.0 83.4 jit_solution(12337609442746705260)
XLA Ops:
  1.3 1.0 %copy_bitcast_fusion = (f32[3,125,128]{2,1,0:T(8,128)S(1)}, f32[3,125,128]{2,1,0:T(8,128)S(1)}) fusion(f32[1,3,125,128]{3,0,2,1:T(1,128)} %param.10, f32[1,3,125,128]{3,0,2,1:T(1,128)} %param.9), kind=kLoop, calls=%fused_computation | loop fusion | bytes 768000
  2.3 0.0 copy-start
  2.3 0.1 shard_map.105
  2.5 1.9 %collective-permute-start = (f32[2,128,128]{2,1,0:T(8,128)S(1)}, f32[2,128,128]{2,1,0:T(8,128)S(1)}, u32[]{:S(2)}, u32[]{:S(2)}) collective-permute-start(f32[2,128,128]{2,1,0:T(8,128)S(1)} %shard_map.105), channel_id=1, source_target_pairs={{0,1},{1,2},{2,3},{3,4},{4,5},{5,6},{6,7},{7,8},{8,9},{9,10},{10,1... | collective-permute-start | bytes 393224 | tf_op jit(solution)/shard_map/ppermute | solution.py:266
  4.4 3.4 %collective-permute-start.1 = (f32[2,128,128]{2,1,0:T(8,128)S(1)}, f32[2,128,128]{2,1,0:T(8,128)S(1)}, u32[]{:S(2)}, u32[]{:S(2)}) collective-permute-start(f32[2,128,128]{2,1,0:T(8,128)S(1)} %shard_map.105), channel_id=1, source_target_pairs={{1,0},{2,1},{3,2},{4,3},{5,4},{6,5},{7,6},{8,7},{9,8},{10,9},{11,1... | collective-permute-start | bytes 393224 | tf_op jit(solution)/shard_map/ppermute | solution.py:266
  7.8 0.0 copy-start.5
  7.8 0.0 copy-start.3
  7.8 0.3 shard_map.104
  8.2 0.3 copy-done.5
  8.5 0.1 copy-done.3
  8.6 0.1 copy.11.refs_12_
  8.7 0.1 pad_add_fusion.refs_1_.place_ref
  8.8 5.1 %collective-permute-done.1.refs_8_ = f32[2,128,128]{2,1,0:T(8,128)S(1)} collective-permute-done((f32[2,128,128]{2,1,0:T(8,128)S(1)}, f32[2,128,128]{2,1,0:T(8,128)S(1)}, u32[]{:S(2)}, u32[]{:S(2)}) %collective-permute-start.1) | collective-permute-done | bytes 131104 | tf_op jit(solution)/shard_map/ppermute | solution.py:266
  13.9 0.7 copy-done.1
  14.5 0.0 copy-done.2
  14.5 2.7 %shard_map.106 = (f32[3,128,128]{2,1,0:T(8,128)S(1)}, f32[3,128,128]{2,1,0:T(8,128)S(1)}, f32[3,192,128]{2,1,0:T(8,128)S(1)}, f32[128,128]{1,0:T(8,128)S(1)}, f32[16,128,128]{2,1,0:T(8,128)S(1)}) custom-call(s32[1,1]{1,0:T(1,128)S(6)} %copy.21.count_ref.refs_0_, s32[2]{0:T(128)S(1)} %pad_add_fusion.refs_1_.place_ref, ...), custom_call_target="tpu_custom_call" | custom-call | tf_op jit(solution)/shard_map/pallas_call | solution.py:284
  17.2 17.0 %all_to_all.10.x_ref = f32[16,128,128]{2,1,0:T(8,128)S(1)} all-to-all(f32[16,128,128]{2,1,0:T(8,128)S(1)} %get-tuple-element.17), channel_id=1, replica_groups=mesh['event'=32,'mesh'=16] {'mesh'}, dimensions={0} | all-to-all | bytes 2097152 | tf_op jit(solution)/shard_map/all_to_all | solution.py:302
  34.3 0.7 shard_map.108
  34.9 17.3 %all-to-all-start.1 = ((f32[32,4,128]{2,1,0:T(4,128)}), f32[32,4,128]{2,1,0:T(4,128)S(1)}, u32[]{:S(2)}, u32[]{:S(2)}) async-start(f32[32,4,128]{2,1,0:T(4,128)} %bitcast.2), calls=%async_computation.1 | async-start | bytes 131072 | tf_op jit(solution)/shard_map/all_to_all | solution.py:313
  52.3 5.8 %collective-permute-start.2 = (f32[128,128]{1,0:T(8,128)S(1)}, f32[128,128]{1,0:T(8,128)S(1)}, u32[]{:S(2)}, u32[]{:S(2)}) collective-permute-start(f32[128,128]{1,0:T(8,128)S(1)} %get-tuple-element.16), channel_id=1, source_target_pairs={{0,1},{1,2},{2,3},{3,4},{4,5},{5,6},{6,7},{7,8},{8,9},{9,10},{10,1... | collective-permute-start | bytes 196616 | tf_op jit(solution)/shard_map/ppermute | solution.py:300
  58.1 1.9 %collective-permute-start.3 = (f32[128,128]{1,0:T(8,128)S(1)}, f32[128,128]{1,0:T(8,128)S(1)}, u32[]{:S(2)}, u32[]{:S(2)}) collective-permute-start(f32[128,128]{1,0:T(8,128)S(1)} %get-tuple-element.16), channel_id=1, source_target_pairs={{1,0},{2,1},{3,2},{4,3},{5,4},{6,5},{7,6},{8,7},{9,8},{10,9},{11,1... | collective-permute-start | bytes 196616 | tf_op jit(solution)/shard_map/ppermute | solution.py:300
  60.0 0.1 fusion
  60.1 9.6 %collective-permute-start.4 = (f32[4,1]{1,0:T(4,128)S(1)}, f32[4,1]{1,0:T(4,128)S(1)}, u32[]{:S(2)}, u32[]{:S(2)}) collective-permute-start(f32[4,1]{1,0:T(4,128)S(1)} %get-tuple-element.21), channel_id=1, source_target_pairs={{0,1},{1,2},{2,3},{3,4},{4,5},{5,6},{6,7},{7,8},{8,9},{9,10},{10,1... | collective-permute-start | bytes 56 | tf_op jit(solution)/shard_map/ppermute | solution.py:268
  69.7 1.9 %collective-permute-start.5 = (f32[4,1]{1,0:T(4,128)S(1)}, f32[4,1]{1,0:T(4,128)S(1)}, u32[]{:S(2)}, u32[]{:S(2)}) collective-permute-start(f32[4,1]{1,0:T(4,128)S(1)} %get-tuple-element.20), channel_id=1, source_target_pairs={{1,0},{2,1},{3,2},{4,3},{5,4},{6,5},{7,6},{8,7},{9,8},{10,9},{11,1... | collective-permute-start | bytes 56 | tf_op jit(solution)/shard_map/ppermute | solution.py:269
  71.6 8.4 %collective-permute-done.5 = f32[4,1]{1,0:T(4,128)S(1)} collective-permute-done((f32[4,1]{1,0:T(4,128)S(1)}, f32[4,1]{1,0:T(4,128)S(1)}, u32[]{:S(2)}, u32[]{:S(2)}) %collective-permute-start.5) | collective-permute-done | bytes 48 | tf_op jit(solution)/shard_map/ppermute | solution.py:269
  80.0 0.1 concatenate.3.coef_ref
  80.1 0.0 collective-permute-done.2.before_ref
  80.1 0.0 collective-permute-done.3.after_ref
  80.1 1.3 %shard_map.107 = f32[3,125,128]{2,1,0:T(8,128)S(1)} custom-call(s32[1,1]{1,0:T(1,128)S(6)} %copy.21.count_ref.refs_0_, s32[2]{0:T(128)S(1)} %pad_add_fusion.refs_1_.place_ref, f32[3,125,128]{2,1,0:T(8,128)S(1)} %get-tuple-element.23.forward_ref.refs_2_, f32[3,128,128]{2,1,0:T(8,128)S(1)} %get-tuple-element.13.one_ref, ...), custom_call_target="tpu_custom_call" | custom-call | tf_op jit(solution)/shard_map/pallas_call | solution.py:306
  81.4 0.9 %copy.12 = f32[1,3,125,128]{3,0,2,1:T(1,128)} copy(f32[1,3,125,128]{3,2,1,0:T(8,128)S(1)} %bitcast.10) | data formatting | bytes 384000
  82.3 0.4 shard_map.109
  82.8 0.7 copy.13
  (10 shorter events, 0.0 us)
Async XLA Ops:
  2.3 5.5 %copy-start = (f32[125,125]{1,0:T(8,128)S(1)}, f32[125,125]{1,0:T(8,128)}, u32[]{:S(2)}) copy-start(f32[125,125]{1,0:T(8,128)} %refs_11_.1) | copy-start | bytes 187504
  2.5 6.3 %collective-permute-start = (f32[2,128,128]{2,1,0:T(8,128)S(1)}, f32[2,128,128]{2,1,0:T(8,128)S(1)}, u32[]{:S(2)}, u32[]{:S(2)}) collective-permute-start(f32[2,128,128]{2,1,0:T(8,128)S(1)} %shard_map.105), channel_id=1, source_target_pairs={{0,1},{1,2},{2,3},{3,4},{4,5},{5,6},{6,7},{7,8},{8,9},{9,10},{10,1... | collective-permute-start | bytes 393224 | tf_op jit(solution)/shard_map/ppermute | solution.py:266
  4.4 9.4 %collective-permute-start.1 = (f32[2,128,128]{2,1,0:T(8,128)S(1)}, f32[2,128,128]{2,1,0:T(8,128)S(1)}, u32[]{:S(2)}, u32[]{:S(2)}) collective-permute-start(f32[2,128,128]{2,1,0:T(8,128)S(1)} %shard_map.105), channel_id=1, source_target_pairs={{1,0},{2,1},{3,2},{4,3},{5,4},{6,5},{7,6},{8,7},{9,8},{10,9},{11,1... | collective-permute-start | bytes 393224 | tf_op jit(solution)/shard_map/ppermute | solution.py:266
  7.8 0.7 copy-start.5
  7.8 0.8 copy-start.3
  13.8 0.7 copy-start.1
  13.8 0.7 copy-start.2
  34.9 25.1 %copy-start.4 = (f32[4,4]{1,0:T(4,128)S(1)}, f32[4,4]{1,0:T(4,128)}, u32[]{:S(2)}) copy-start(f32[4,4]{1,0:T(4,128)} %param.17) | copy-start | bytes 196
  34.9 47.4 %all-to-all-start.1 = ((f32[32,4,128]{2,1,0:T(4,128)}), f32[32,4,128]{2,1,0:T(4,128)S(1)}, u32[]{:S(2)}, u32[]{:S(2)}) async-start(f32[32,4,128]{2,1,0:T(4,128)} %bitcast.2), calls=%async_computation.1 | async-start | bytes 131072 | tf_op jit(solution)/shard_map/all_to_all | solution.py:313
  52.3 27.9 %collective-permute-start.2 = (f32[128,128]{1,0:T(8,128)S(1)}, f32[128,128]{1,0:T(8,128)S(1)}, u32[]{:S(2)}, u32[]{:S(2)}) collective-permute-start(f32[128,128]{1,0:T(8,128)S(1)} %get-tuple-element.16), channel_id=1, source_target_pairs={{0,1},{1,2},{2,3},{3,4},{4,5},{5,6},{6,7},{7,8},{8,9},{9,10},{10,1... | collective-permute-start | bytes 196616 | tf_op jit(solution)/shard_map/ppermute | solution.py:300
  58.1 22.0 %collective-permute-start.3 = (f32[128,128]{1,0:T(8,128)S(1)}, f32[128,128]{1,0:T(8,128)S(1)}, u32[]{:S(2)}, u32[]{:S(2)}) collective-permute-start(f32[128,128]{1,0:T(8,128)S(1)} %get-tuple-element.16), channel_id=1, source_target_pairs={{1,0},{2,1},{3,2},{4,3},{5,4},{6,5},{7,6},{8,7},{9,8},{10,9},{11,1... | collective-permute-start | bytes 196616 | tf_op jit(solution)/shard_map/ppermute | solution.py:300
  60.1 11.5 %collective-permute-start.4 = (f32[4,1]{1,0:T(4,128)S(1)}, f32[4,1]{1,0:T(4,128)S(1)}, u32[]{:S(2)}, u32[]{:S(2)}) collective-permute-start(f32[4,1]{1,0:T(4,128)S(1)} %get-tuple-element.21), channel_id=1, source_target_pairs={{0,1},{1,2},{2,3},{3,4},{4,5},{5,6},{6,7},{7,8},{8,9},{9,10},{10,1... | collective-permute-start | bytes 56 | tf_op jit(solution)/shard_map/ppermute | solution.py:268
  69.7 10.3 %collective-permute-start.5 = (f32[4,1]{1,0:T(4,128)S(1)}, f32[4,1]{1,0:T(4,128)S(1)}, u32[]{:S(2)}, u32[]{:S(2)}) collective-permute-start(f32[4,1]{1,0:T(4,128)S(1)} %get-tuple-element.20), channel_id=1, source_target_pairs={{1,0},{2,1},{3,2},{4,3},{5,4},{6,5},{7,6},{8,7},{9,8},{10,9},{11,1... | collective-permute-start | bytes 56 | tf_op jit(solution)/shard_map/ppermute | solution.py:269

commit v2 on v1

v2 whole, which is shorter than its diff:
```python
import math

import jax
import jax.numpy as jnp
from jax import lax
from jax.experimental import pallas as pl
from jax.experimental.pallas import tpu as pltpu
from jax.sharding import PartitionSpec as P

STEPS = 2
NODES = 125
RIM = 32
SHEET = 32
FACES = 6
F32, BF16, I32 = jnp.float32, jnp.bfloat16, jnp.int32
partner_face = (1, 0, 3, 2, 5, 4)

VMEM = pl.BlockSpec(memory_space=pltpu.VMEM)
SMEM = pl.BlockSpec(memory_space=pltpu.SMEM)
ANY = pl.BlockSpec(memory_space=pl.ANY)
PARAMS = pltpu.CompilerParams(vmem_limit_bytes=40 * 2**20)


def shape(*dims):
    return jax.ShapeDtypeStruct(dims, F32)


def iota(dims, axis):
    return lax.broadcasted_iota(I32, dims, axis)


def halves(x):
    high = x.astype(BF16)
    return high, (x - high.astype(F32)).astype(BF16)


def dot(a, b):
    return lax.dot_general(a, b, (((1,), (0,)), ((), ())), preferred_element_type=F32)


def face_nodes(dims, axis):
    row = iota(dims, axis)
    face, q = row // SHEET, row % SHEET
    a = sum((q >= 5 * i).astype(I32) for i in range(1, 5))
    b = q - 5 * a
    node = jnp.where(face == 0, q, q + 100)
    node = jnp.where(face == 2, 25 * a + b, node)
    node = jnp.where(face == 3, 25 * a + 20 + b, node)
    node = jnp.where(face == 4, 5 * q, node)
    node = jnp.where(face == 5, 5 * q + 4, node)
    return jnp.where(q < 25, node, -1)


def picker():
    dims = (FACES * SHEET, 128)
    return jnp.where(face_nodes(dims, 0) == iota(dims, 1), 1.0, 0.0).astype(BF16)


def lifter():
    dims = (128, FACES * SHEET)
    return jnp.where(face_nodes(dims, 1) == iota(dims, 0), 1.0, 0.0).astype(BF16)


def padded(ref, index):
    return jnp.concatenate([ref[index], jnp.zeros((128 - NODES, 128), F32)], axis=0)


def stacked(fields):
    high, low = halves(jnp.concatenate(fields, axis=1))
    return jnp.concatenate([high, low], axis=0)


def pack_rim(fields):
    lane = iota((128, 128), 1)
    out = fields[0]
    for k in range(1, len(fields)):
        out = jnp.where(lane < RIM * k, out, pltpu.roll(fields[k], RIM * k, 1))
    return jnp.where(lane < RIM * len(fields), out, 0.0)


def fold(x):
    return jnp.where(iota((64, 128), 1) < 64, x[:64], pltpu.roll(x[64:], 64, 1))


def live_mask(count_ref):
    return (iota((128, 128), 1) < count_ref[0, 0]).astype(F32)


def pack_kernel(count_ref, forward_ref, adjoint_ref, rim_ref):
    live = live_mask(count_ref)
    fields = [padded(ref, c) * live for ref in (forward_ref, adjoint_ref) for c in range(3)]
    rim_ref[:128] = pack_rim(fields[:4])
    rim_ref[128:] = fold(pack_rim(fields[4:]))


def split_stiffness(stiff_ref):
    wide = jnp.concatenate([stiff_ref[...], jnp.zeros((NODES, 128 - NODES), F32)], axis=1)
    return halves(jnp.concatenate([wide, jnp.zeros((128 - NODES, 128), F32)], axis=0))


def columns(x):
    return [x[:, 128 * k : 128 * (k + 1)] for k in range(x.shape[1] // 128)]


def strains(stiffness, x):
    high, low = stiffness
    return columns(dot(jnp.concatenate([high, high], axis=1), x) + dot(low, x[:128]))


def faces_of(x):
    pick = picker()
    return columns(dot(jnp.concatenate([pick, pick], axis=1), x))


def take(x, index):
    return jnp.take_along_axis(x, index, axis=1, mode="promise_in_bounds")


def lift_of(jumps):
    high, low = halves(jnp.concatenate([jnp.concatenate(j, axis=0) for j in jumps], axis=1))
    lift = lifter()
    return columns(dot(lift, high) + dot(lift, low))


def own_jumps(place_ref, near_ref, own):
    jumps = [[] for _ in own]
    for face in range(FACES):
        p = partner_face[face]
        near = jnp.broadcast_to(near_ref[face : face + 1, :], (SHEET, 128))
        home = near // 128 == place_ref[0]
        slot = near % 128
        for k in range(len(own)):
            here = take(own[k][SHEET * p : SHEET * (p + 1)], slot)
            jumps[k].append(jnp.where(home, here, 0.0) - own[k][SHEET * face : SHEET * (face + 1)])
    return jumps


def rim_jumps(place_ref, near_ref, rims, n):
    mine, parts = place_ref[0], place_ref[1]
    follower = jnp.where(mine + 1 == parts, 0, mine + 1)
    jumps = [[] for _ in range(n)]
    for face in range(FACES):
        p = partner_face[face]
        near = jnp.broadcast_to(near_ref[face : face + 1, :], (SHEET, 128))
        target = near // 128
        away = target != mine
        index = near % RIM + jnp.where(target == follower, 64, 0)
        for k in range(n):
            across = take(rims[k // 2][SHEET * p : SHEET * (p + 1)], index + RIM * (k % 2))
            jumps[k].append(jnp.where(away, across, 0.0))
    return jumps


def merge(before, after):
    lane = iota(before.shape, 1)
    first = jnp.where(lane < 64, before, pltpu.roll(after, 64, 1))
    second = jnp.where(lane < 64, pltpu.roll(before, 64, 1), after)
    return first, second


def edges_of(smooth_ref):
    width = smooth_ref.shape[1]
    wide = jnp.concatenate([smooth_ref[...], jnp.zeros((4, 128 - width), F32)], axis=1)
    turned = jnp.concatenate([wide, jnp.zeros((124, 128), F32)], axis=0).T
    last, first = turned[width - 1 : width], turned[0:1]
    lane = iota((1, 128), 1)
    row = jnp.where(lane < 4, last, pltpu.roll(jnp.broadcast_to(first, (8, 128)), 4, 1)[0:1])
    return row, turned


def own_kernel(
    count_ref, place_ref, forward_ref, adjoint_ref, stiff_ref, near_ref, material_ref, smooth_ref,
    partial_ref, kernel_ref, edge_ref, turned_ref,
):
    live = live_mask(count_ref)
    material = jnp.broadcast_to(material_ref[...], (128, 128))
    fields = [padded(ref, c) * live for ref in (forward_ref, adjoint_ref) for c in range(3)]
    x = stacked(fields)
    strain = strains(split_stiffness(stiff_ref), x)
    lift = lift_of(own_jumps(place_ref, near_ref, faces_of(x)))
    for k in range(6):
        force = 0.5 * lift[k] - material * strain[k]
        partial_ref[k] = live * (fields[k] + 0.4 * force)
    kernel_ref[...] = sum(fields[c] * strain[3 + c] for c in range(3))
    row, turned = edges_of(smooth_ref)
    edge_ref[...] = jnp.broadcast_to(row, (8, 128))
    turned_ref[...] = turned[:8]


def step_kernel(
    scale, n_mesh,
    count_ref, place_ref, partial_ref, kernel_ref, before_ref, after_ref, near_ref, stiff_ref, project_ref,
    destination_ref, edge_ref,
    forward_ref, strain_ref, rim_ref, edge_out_ref, chunk_ref,
):
    live = live_mask(count_ref)
    first, second = merge(before_ref[:128], after_ref[:128])
    upper, lower = merge(before_ref[128:], after_ref[128:])
    rims = faces_of(stacked([first, second, jnp.concatenate([upper, lower], axis=0)]))
    lift = lift_of(rim_jumps(place_ref, near_ref, rims, 6))
    fields = [partial_ref[k] + live * (0.2 * lift[k]) for k in range(6)]
    rim = pack_rim(fields[:3])
    rim_ref[...] = jnp.where(iota((128, 128), 0) == NODES, jnp.broadcast_to(edge_ref[0:1, :], (128, 128)), rim)
    edge_out_ref[...] = edge_ref[...]
    strain = strains(split_stiffness(stiff_ref), stacked(fields))
    for c in range(3):
        forward_ref[c] = fields[c]
        strain_ref[c] = strain[c]
    kernel = kernel_ref[...] + sum(fields[c] * strain[3 + c] for c in range(3))
    k_high, k_low = halves(kernel)
    p_high, p_low = halves(jnp.concatenate([project_ref[...], jnp.zeros((64, 128 - NODES), F32)], axis=1))
    blocks = dot(jnp.concatenate([p_high, p_high], axis=1), jnp.concatenate([k_high, k_low], axis=0))
    blocks = (blocks + dot(p_low, k_high)) * scale
    turned = jnp.concatenate([blocks, pltpu.roll(blocks, 64, 1)], axis=0).T[:64]
    wanted = jnp.broadcast_to(destination_ref[...].astype(F32), (8, 128))
    for m in range(n_mesh):
        chunk_ref[m, :64] = turned
        chunk_ref[m, 64:] = wanted


def dense_kernel(n_event, n_mesh, tile_width, place_ref, parts_ref, before_ref, after_ref, wrap_ref, out_ref):
    rows = 4 * n_event
    row = iota((2 * rows, 128), 0)
    within = row % rows
    tile = (within // 4) * (n_mesh * tile_width) + within % 4 + 4 * (row // rows) - 2
    tile = tile.astype(F32) + (place_ref[0] * tile_width).astype(F32)
    lane = iota((64, 128), 1)
    left, right = [], []
    for m in range(n_mesh):
        x = parts_ref[m, :64]
        high = x.astype(BF16).astype(F32)
        low = x - high
        right.append(jnp.where(lane < 64, high, pltpu.roll(low, 64, 1)).astype(BF16))
        right.append(jnp.where(lane < 64, pltpu.roll(high, 64, 1), low).astype(BF16))
        wanted = jnp.broadcast_to(parts_ref[m, 64:65], (2 * rows, 128))
        left.append(jnp.where(wanted == tile, 1.0, 0.0).astype(BF16))
    both = dot(jnp.concatenate(left, axis=1), jnp.concatenate(right, axis=0))
    both = both + pltpu.roll(both, 64, 1)
    out_ref[...] = jnp.where(iota((rows, 128), 1) < 64, both[:rows], both[rows:])


def last_kernel(
    count_ref, place_ref, forward_ref, one_ref, strain_ref, before_ref, after_ref, near_ref, material_ref, turned_ref,
    wrap_ref,
    final_ref, coef_ref,
):
    live = live_mask(count_ref)
    material = jnp.broadcast_to(material_ref[...], (128, 128))
    fields = [one_ref[c] for c in range(3)]
    jumps = own_jumps(place_ref, near_ref, faces_of(stacked(fields)))
    row = iota((128, 128), 0)
    before = jnp.where(row < NODES, before_ref[...], 0.0)
    after = jnp.where(row < NODES, after_ref[...], 0.0)
    rims = faces_of(stacked(list(merge(before, after))))
    more = rim_jumps(place_ref, near_ref, rims, 3)
    lift = lift_of([[a + b for a, b in zip(*pair)] for pair in zip(jumps, more)])
    for c in range(3):
        force = 0.5 * lift[c] - material * strain_ref[c]
        out = live * (2.0 * fields[c] - padded(forward_ref, c) * live + 0.4 * force)
        final_ref[c] = out[:NODES]
    mine, parts = place_ref[0], place_ref[1]
    wrap = wrap_ref[0:1]
    first = jnp.where(jnp.full((1, 128), mine) == 0, wrap, before_ref[NODES : NODES + 1])
    last = jnp.where(jnp.full((1, 128), mine) == parts - 1, wrap, after_ref[NODES : NODES + 1])
    last = pltpu.roll(jnp.broadcast_to(last, (8, 128)), 124, 1)
    tile = iota((8, 128), 0)
    table = pltpu.roll(turned_ref[...], 2, 0)
    table = jnp.where((tile >= 2) & (tile < 6), table, 0.0)
    table = jnp.where(tile == 1, jnp.broadcast_to(first, (8, 128)), table)
    table = jnp.where(tile == 6, last, table)
    for d in range(4):
        coef_ref[d] = jnp.broadcast_to(table[:, d : d + 1], (8, 128))


def smooth_kernel(x_ref, coef_ref, o_ref):
    total = x_ref[0]
    for i in range(1, x_ref.shape[0]):
        total = total + x_ref[i]
    x = jnp.concatenate([total, pltpu.roll(total, 64, 1)], axis=0)
    node, tile = iota((8, 128), 1), iota((8, 128), 0)
    for _ in range(2):
        right = jnp.where(tile < 7, pltpu.roll(x, 7, 0), 0.0)
        left = jnp.where(tile > 0, pltpu.roll(x, 1, 0), 0.0)
        out = x + coef_ref[0] * (left + right - 2.0 * x)
        for d, stride in ((1, 16), (2, 4), (3, 1)):
            place = (node // stride) % 4
            up = jnp.where(place < 3, pltpu.roll(x, 128 - stride, 1), 0.0)
            down = jnp.where(place > 0, pltpu.roll(x, stride, 1), 0.0)
            out = out + coef_ref[d] * (up + down - 2.0 * x)
        x = out
    o_ref[...] = x[2:6, :64]


def call(kernel, out_shape, n_smem, n_vmem, n_any=0):
    many = isinstance(out_shape, tuple)
    return pl.pallas_call(
        kernel,
        out_shape=out_shape,
        in_specs=[SMEM] * n_smem + [VMEM] * n_vmem + [ANY] * n_any,
        out_specs=(VMEM,) * len(out_shape) if many else VMEM,
        compiler_params=PARAMS,
    )


def per_device(
    forward_start, adjoint_start, stiffness, projection, material, neighbours, destinations, counts, smoothing
):
    elements = forward_start.shape[-1]
    tile_width = smoothing.shape[1]
    n_mesh, n_event = lax.axis_size("mesh"), lax.axis_size("event")
    scale = math.sqrt(tile_width / elements) / STEPS
    forward, adjoint, near = forward_start[0], adjoint_start[0], neighbours[0]
    place = jnp.stack([lax.axis_index("mesh"), jnp.int32(n_mesh)]).astype(I32)
    up = [(i, (i + 1) % n_mesh) for i in range(n_mesh)]
    down = [(j, i) for i, j in up]
    ends = [((e + 1) * n_mesh - 1, (e + 1) * n_mesh) for e in range(n_event - 1)]
    ends = ends + [(j, i) for i, j in ends]

    rim = call(pack_kernel, shape(192, 128), 1, 2)(counts, forward, adjoint)
    before, after = lax.ppermute(rim, "mesh", up), lax.ppermute(rim, "mesh", down)
    partial, kernel, edge, turned = call(
        own_kernel, (shape(6, 128, 128), shape(128, 128), shape(8, 128), shape(8, 128)), 2, 6
    )(counts, place, forward, adjoint, stiffness, near, material, smoothing)

    def one_step(*refs):
        step_kernel(scale, n_mesh, *refs)

    one, strain, rim_one, edge, chunk = call(
        one_step,
        (shape(3, 128, 128), shape(3, 128, 128), shape(128, 128), shape(8, 128), shape(n_mesh, 72, 128)),
        2,
        9,
    )(counts, place, partial, kernel, before, after, near, stiffness, projection.T, destinations, edge)
    parts = lax.all_to_all(chunk, "mesh", 0, 0, tiled=True)
    before, after = lax.ppermute(rim_one, "mesh", up), lax.ppermute(rim_one, "mesh", down)
    wrap = lax.ppermute(edge, ("event", "mesh"), ends)

    def dense(*refs):
        dense_kernel(n_event, n_mesh, tile_width, *refs)

    partial = call(dense, shape(4 * n_event, 128), 1, 1, 3)(place, parts, before, after, wrap)
    pieces = lax.all_to_all(partial.reshape(n_event, 4, 128), "event", 0, 0, tiled=True)
    final, coefs = call(last_kernel, (shape(3, NODES, 128), shape(4, 8, 128)), 2, 9)(
        counts, place, forward, one, strain, before, after, near, material, turned, wrap
    )
    tiles = call(smooth_kernel, shape(tile_width, 64), 0, 2)(pieces, coefs)
    return final[None], tiles.T


def solution(mesh):
    in_specs = (
        P("event", None, None, "mesh"),
        P("event", None, None, "mesh"),
        P(),
        P(),
        P("event", "mesh"),
        P("event", None, "mesh"),
        P("event", "mesh"),
        P("event", "mesh"),
        P(None, ("event", "mesh")),
    )
    out_specs = (P("event", None, None, "mesh"), P(None, ("event", "mesh")))
    return jax.shard_map(per_device, mesh=mesh, in_specs=in_specs, out_specs=out_specs, check_vma=False)
```

time: 83.9 us -> 78.8 us (0.939)
  the two profiles are of different devices: /device:TPU:127 before, /device:TPU:1 now
where the time goes in v2:
time: 78.8 us; the launch traced here: 78.3 us
  starting transfers between devices  48.6 us (62%)
  waiting for transfers between devices  16.9 us (21%)
  Pallas kernels  8.12 us (10%)
  local copies, waits for them, and re-layouts  3.25 us (4%)
  between operations  1.41 us (2%)
    all_to_all x1, starting transfers between devices, per_device(): lax.all_to_all(partial.reshape(n_event, 4, 128), 'event', 0, 0, tiled=True)  17.3 us
    all_to_all x1, waiting for transfers between devices, per_device(): lax.all_to_all(partial.reshape(n_event, 4, 128), 'event', 0, 0, tiled=True)  10.9 us
    ppermute x1, starting transfers between devices, per_device(): wrap = lax.ppermute(edge, ('event', 'mesh'), ends)  9.69 us
    ppermute x1, starting transfers between devices, per_device(): lax.ppermute(rim, 'mesh', down)  7.67 us
    ppermute x1, starting transfers between devices, per_device(): lax.ppermute(rim_one, 'mesh', down)  6.56 us
    ppermute x1, waiting for transfers between devices, per_device(): lax.ppermute(rim, 'mesh', up)  4.66 us
    all_to_all x1, starting transfers between devices, per_device(): parts = lax.all_to_all(chunk, 'mesh', 0, 0, tiled=True)  3.58 us
    unnamed x15, local copies, waits for them, and re-layouts  3.25 us
  transfers between devices with their start and end apart: 7, of which 3 were waited for; matrix products, arithmetic and copies ran while one was open for 1% of the time, Pallas kernels for 3%

profile of v2, /device:TPU:1, one launch (start us, length us, event | category | flops | bytes accessed | tf_op | source)
XLA Modules:
  0.0 78.3 jit_solution(164535649496118219)
XLA Ops:
  1.3 1.0 %copy_bitcast_fusion = (f32[3,125,128]{2,1,0:T(8,128)S(1)}, f32[3,125,128]{2,1,0:T(8,128)S(1)}) fusion(f32[1,3,125,128]{3,0,2,1:T(1,128)} %param.10, f32[1,3,125,128]{3,0,2,1:T(1,128)} %param.9), kind=kLoop, calls=%fused_computation | loop fusion | bytes 768000
  2.3 0.0 copy-start
  2.3 0.2 shard_map.105
  2.5 0.0 copy-start.5
  2.5 7.7 %collective-permute-start.1 = (f32[192,128]{1,0:T(8,128)S(1)}, f32[192,128]{1,0:T(8,128)S(1)}, u32[]{:S(2)}, u32[]{:S(2)}) collective-permute-start(f32[192,128]{1,0:T(8,128)S(1)} %shard_map.105), channel_id=1, source_target_pairs={{1,0},{2,1},{3,2},{4,3},{5,4},{6,5},{7,6},{8,7},{9,8},{10,9},{11,1... | collective-permute-start | bytes 294920 | tf_op jit(solution)/shard_map/ppermute | solution.py:320
  10.2 1.9 %collective-permute-start = (f32[192,128]{1,0:T(8,128)S(1)}, f32[192,128]{1,0:T(8,128)S(1)}, u32[]{:S(2)}, u32[]{:S(2)}) collective-permute-start(f32[192,128]{1,0:T(8,128)S(1)} %shard_map.105), channel_id=1, source_target_pairs={{0,1},{1,2},{2,3},{3,4},{4,5},{5,6},{6,7},{7,8},{8,9},{9,10},{10,1... | collective-permute-start | bytes 294920 | tf_op jit(solution)/shard_map/ppermute | solution.py:320
  12.1 0.0 copy-done.5
  12.1 0.0 copy-start.2
  12.1 0.1 pad_add_fusion.place_ref.refs_1_.refs_0_
  12.2 0.0 copy-done
  12.2 0.6 copy-done.2
  12.8 0.1 copy-done.3
  12.9 1.3 %shard_map.104 = (f32[6,128,128]{2,1,0:T(8,128)S(1)}, f32[128,128]{1,0:T(8,128)S(1)}, f32[8,128]{1,0:T(8,128)S(1)}, f32[8,128]{1,0:T(8,128)S(1)}) custom-call(s32[1,1]{1,0:T(1,128)S(6)} %copy.19.count_ref.refs_0_, s32[2]{0:T(128)S(1)} %pad_add_fusion.place_ref.refs_1_.refs_0_, f32[3,125,128]{2,1,0:T(8,128)S(1)} %get-tuple-element.27.forward_ref, ...), custom_call_target="tpu_custom_call" | custom-call | tf_op jit(solution)/shard_map/pallas_call | solution.py:321
  14.2 0.0 collective-permute-done.1.refs_5_
  14.2 4.7 %collective-permute-done.refs_4_ = f32[192,128]{1,0:T(8,128)S(1)} collective-permute-done((f32[192,128]{1,0:T(8,128)S(1)}, f32[192,128]{1,0:T(8,128)S(1)}, u32[]{:S(2)}, u32[]{:S(2)}) %collective-permute-start) | collective-permute-done | bytes 98336 | tf_op jit(solution)/shard_map/ppermute | solution.py:320
  18.9 0.0 copy-done.1
  18.9 0.7 copy-done.4
  19.5 2.8 %shard_map.106 = (f32[3,128,128]{2,1,0:T(8,128)S(1)}, f32[3,128,128]{2,1,0:T(8,128)S(1)}, f32[128,128]{1,0:T(8,128)S(1)}, f32[8,128]{1,0:T(8,128)S(1)}, f32[16,72,128]{2,1,0:T(8,128)}) custom-call(s32[1,1]{1,0:T(1,128)S(6)} %copy.19.count_ref.refs_0_, s32[2]{0:T(128)S(1)} %pad_add_fusion.place_ref.refs_1_.refs_0_, ...), custom_call_target="tpu_custom_call" | custom-call | tf_op jit(solution)/shard_map/pallas_call | solution.py:328
  22.3 3.6 %all-to-all-start = ((f32[16,72,128]{2,1,0:T(8,128)}), f32[16,72,128]{2,1,0:T(8,128)S(1)}, u32[]{:S(2)}, u32[]{:S(2)}) async-start(f32[16,72,128]{2,1,0:T(8,128)} %get-tuple-element.22), calls=%async_computation | async-start | bytes 1179648 | tf_op jit(solution)/shard_map/all_to_all | solution.py:334
  25.9 6.6 %collective-permute-start.3 = (f32[128,128]{1,0:T(8,128)S(1)}, f32[128,128]{1,0:T(8,128)S(1)}, u32[]{:S(2)}, u32[]{:S(2)}) collective-permute-start(f32[128,128]{1,0:T(8,128)S(1)} %get-tuple-element.18), channel_id=1, source_target_pairs={{1,0},{2,1},{3,2},{4,3},{5,4},{6,5},{7,6},{8,7},{9,8},{10,9},{11,1... | collective-permute-start | bytes 196616 | tf_op jit(solution)/shard_map/ppermute | solution.py:335
  32.5 1.9 %collective-permute-start.2 = (f32[128,128]{1,0:T(8,128)S(1)}, f32[128,128]{1,0:T(8,128)S(1)}, u32[]{:S(2)}, u32[]{:S(2)}) collective-permute-start(f32[128,128]{1,0:T(8,128)S(1)} %get-tuple-element.18), channel_id=1, source_target_pairs={{0,1},{1,2},{2,3},{3,4},{4,5},{5,6},{6,7},{7,8},{8,9},{9,10},{10,1... | collective-permute-start | bytes 196616 | tf_op jit(solution)/shard_map/ppermute | solution.py:335
  34.4 9.7 %collective-permute-start.4 = (f32[8,128]{1,0:T(8,128)S(1)}, f32[8,128]{1,0:T(8,128)S(1)}, u32[]{:S(2)}, u32[]{:S(2)}) collective-permute-start(f32[8,128]{1,0:T(8,128)S(1)} %get-tuple-element.20), channel_id=1, source_target_pairs={{15,16},{31,32},{47,48},{63,64},{79,80},{95,96},{111,112},{127,128... | collective-permute-start | bytes 12296 | tf_op jit(solution)/shard_map/ppermute | solution.py:336
  44.1 1.3 %collective-permute-done.4.wrap_ref.refs_4_ = f32[8,128]{1,0:T(8,128)S(1)} collective-permute-done((f32[8,128]{1,0:T(8,128)S(1)}, f32[8,128]{1,0:T(8,128)S(1)}, u32[]{:S(2)}, u32[]{:S(2)}) %collective-permute-start.4) | collective-permute-done | bytes 4128 | tf_op jit(solution)/shard_map/ppermute | solution.py:336
  45.4 0.0 collective-permute-done.3.after_ref.refs_3_
  45.4 0.0 collective-permute-done.2.before_ref.refs_2_
  45.4 0.0 all-to-all-done.refs_1_
  45.4 1.8 %shard_map.108 = f32[128,128]{1,0:T(8,128)} custom-call(s32[2]{0:T(128)S(1)} %pad_add_fusion.place_ref.refs_1_.refs_0_, f32[16,72,128]{2,1,0:T(8,128)S(1)} %all-to-all-done.refs_1_, f32[128,128]{1,0:T(8,128)S(1)} %collective-permute-done.2.before_ref.refs_2_, f32[128,128]{1,0:T(8,128)S(1)} %collective-permute-done.3.after_ref.refs_3_, ...), custom_call_target="tpu_custom_call" | custom-call | tf_op jit(solution)/shard_map/pallas_call | solution.py:341
  47.1 17.3 %all-to-all-start.1 = ((f32[32,4,128]{2,1,0:T(4,128)}), f32[32,4,128]{2,1,0:T(4,128)S(1)}, u32[]{:S(2)}, u32[]{:S(2)}) async-start(f32[32,4,128]{2,1,0:T(4,128)} %bitcast.3), calls=%async_computation.1 | async-start | bytes 131072 | tf_op jit(solution)/shard_map/all_to_all | solution.py:342
  64.4 1.3 %shard_map.107 = (f32[3,125,128]{2,1,0:T(8,128)S(1)}, f32[4,8,128]{2,1,0:T(8,128)S(1)}) custom-call(s32[1,1]{1,0:T(1,128)S(6)} %copy.19.count_ref.refs_0_, s32[2]{0:T(128)S(1)} %pad_add_fusion.place_ref.refs_1_.refs_0_, f32[3,125,128]{2,1,0:T(8,128)S(1)} %get-tuple-element.27.forward_ref, f32[3,128,128]{2,1,0:T(8,128)S(1)} %get-tuple-element.16.one_ref, ...), custom_call_target="tpu_custom_call" | custom-call | tf_op jit(solution)/shard_map/pallas_call | solution.py:343
  65.7 0.9 %copy.11 = f32[1,3,125,128]{3,0,2,1:T(1,128)} copy(f32[1,3,125,128]{3,2,1,0:T(8,128)S(1)} %bitcast.12) | data formatting | bytes 384000
  66.6 10.9 %all-to-all-done.1.x_ref = f32[32,4,128]{2,1,0:T(4,128)S(1)} async-done(((f32[32,4,128]{2,1,0:T(4,128)}), f32[32,4,128]{2,1,0:T(4,128)S(1)}, u32[]{:S(2)}, u32[]{:S(2)}) %all-to-all-start.1) | async-done | bytes 65568 | tf_op jit(solution)/shard_map/all_to_all | solution.py:342
  77.5 0.8 %shard_map.109 = f32[4,64]{1,0:T(4,128)} custom-call(f32[32,4,128]{2,1,0:T(4,128)S(1)} %all-to-all-done.1.x_ref, f32[4,8,128]{2,1,0:T(8,128)S(1)} %get-tuple-element.23.coef_ref), custom_call_target="tpu_custom_call" | custom-call | tf_op jit(solution)/shard_map/pallas_call | solution.py:346
  (4 shorter events, 0.0 us)
Async XLA Ops:
  2.3 9.9 %copy-start = (f32[125,125]{1,0:T(8,128)S(1)}, f32[125,125]{1,0:T(8,128)}, u32[]{:S(2)}) copy-start(f32[125,125]{1,0:T(8,128)} %refs_7_.1) | copy-start | bytes 187504
  2.5 9.6 %copy-start.5 = (s32[1,6,128]{2,0,1:T(1,128)S(1)}, s32[1,6,128]{2,0,1:T(1,128)}, u32[]{:S(2)}) copy-start(s32[1,6,128]{2,0,1:T(1,128)} %param.14) | copy-start | bytes 9220
  2.5 11.7 %collective-permute-start.1 = (f32[192,128]{1,0:T(8,128)S(1)}, f32[192,128]{1,0:T(8,128)S(1)}, u32[]{:S(2)}, u32[]{:S(2)}) collective-permute-start(f32[192,128]{1,0:T(8,128)S(1)} %shard_map.105), channel_id=1, source_target_pairs={{1,0},{2,1},{3,2},{4,3},{5,4},{6,5},{7,6},{8,7},{9,8},{10,9},{11,1... | collective-permute-start | bytes 294920 | tf_op jit(solution)/shard_map/ppermute | solution.py:320
  10.2 8.7 %collective-permute-start = (f32[192,128]{1,0:T(8,128)S(1)}, f32[192,128]{1,0:T(8,128)S(1)}, u32[]{:S(2)}, u32[]{:S(2)}) collective-permute-start(f32[192,128]{1,0:T(8,128)S(1)} %shard_map.105), channel_id=1, source_target_pairs={{0,1},{1,2},{2,3},{3,4},{4,5},{5,6},{6,7},{7,8},{8,9},{9,10},{10,1... | collective-permute-start | bytes 294920 | tf_op jit(solution)/shard_map/ppermute | solution.py:320
  12.1 0.7 copy-start.2
  12.2 0.7 copy-start.3
  12.9 6.0 %copy-start.1 = (f32[125,64]{0,1:T(8,128)S(1)}, f32[125,64]{0,1:T(8,128)}, u32[]{:S(2)}) copy-start(f32[125,64]{0,1:T(8,128)} %param.12) | copy-start | bytes 96004
  18.9 0.7 copy-start.4
  22.3 23.1 %all-to-all-start = ((f32[16,72,128]{2,1,0:T(8,128)}), f32[16,72,128]{2,1,0:T(8,128)S(1)}, u32[]{:S(2)}, u32[]{:S(2)}) async-start(f32[16,72,128]{2,1,0:T(8,128)} %get-tuple-element.22), calls=%async_computation | async-start | bytes 1179648 | tf_op jit(solution)/shard_map/all_to_all | solution.py:334
  25.9 19.5 %collective-permute-start.3 = (f32[128,128]{1,0:T(8,128)S(1)}, f32[128,128]{1,0:T(8,128)S(1)}, u32[]{:S(2)}, u32[]{:S(2)}) collective-permute-start(f32[128,128]{1,0:T(8,128)S(1)} %get-tuple-element.18), channel_id=1, source_target_pairs={{1,0},{2,1},{3,2},{4,3},{5,4},{6,5},{7,6},{8,7},{9,8},{10,9},{11,1... | collective-permute-start | bytes 196616 | tf_op jit(solution)/shard_map/ppermute | solution.py:335
  32.5 12.9 %collective-permute-start.2 = (f32[128,128]{1,0:T(8,128)S(1)}, f32[128,128]{1,0:T(8,128)S(1)}, u32[]{:S(2)}, u32[]{:S(2)}) collective-permute-start(f32[128,128]{1,0:T(8,128)S(1)} %get-tuple-element.18), channel_id=1, source_target_pairs={{0,1},{1,2},{2,3},{3,4},{4,5},{5,6},{6,7},{7,8},{8,9},{9,10},{10,1... | collective-permute-start | bytes 196616 | tf_op jit(solution)/shard_map/ppermute | solution.py:335
  34.4 11.0 %collective-permute-start.4 = (f32[8,128]{1,0:T(8,128)S(1)}, f32[8,128]{1,0:T(8,128)S(1)}, u32[]{:S(2)}, u32[]{:S(2)}) collective-permute-start(f32[8,128]{1,0:T(8,128)S(1)} %get-tuple-element.20), channel_id=1, source_target_pairs={{15,16},{31,32},{47,48},{63,64},{79,80},{95,96},{111,112},{127,128... | collective-permute-start | bytes 12296 | tf_op jit(solution)/shard_map/ppermute | solution.py:336
  47.1 30.4 %all-to-all-start.1 = ((f32[32,4,128]{2,1,0:T(4,128)}), f32[32,4,128]{2,1,0:T(4,128)S(1)}, u32[]{:S(2)}, u32[]{:S(2)}) async-start(f32[32,4,128]{2,1,0:T(4,128)} %bitcast.3), calls=%async_computation.1 | async-start | bytes 131072 | tf_op jit(solution)/shard_map/all_to_all | solution.py:342

commit v3 on v2

--- a/solution.py
+++ b/solution.py
@@ -17,12 +17,12 @@
 
 VMEM = pl.BlockSpec(memory_space=pltpu.VMEM)
 SMEM = pl.BlockSpec(memory_space=pltpu.SMEM)
-ANY = pl.BlockSpec(memory_space=pl.ANY)
+HBM = pl.BlockSpec(memory_space=pltpu.HBM)
 PARAMS = pltpu.CompilerParams(vmem_limit_bytes=40 * 2**20)
 
 
-def shape(*dims):
-    return jax.ShapeDtypeStruct(dims, F32)
+def shape(*dims, dtype=F32):
+    return jax.ShapeDtypeStruct(dims, dtype)
 
 
 def iota(dims, axis):
@@ -61,8 +61,13 @@
     return jnp.where(face_nodes(dims, 1) == iota(dims, 0), 1.0, 0.0).astype(BF16)
 
 
-def padded(ref, index):
-    return jnp.concatenate([ref[index], jnp.zeros((128 - NODES, 128), F32)], axis=0)
+def rows_of(ref):
+    return ref.reshape(3 * NODES, 128)
+
+
+def padded(ref, c):
+    rows = rows_of(ref)[NODES * c : NODES * (c + 1)]
+    return jnp.concatenate([rows, jnp.zeros((128 - NODES, 128), F32)], axis=0)
 
 
 def stacked(fields):
@@ -86,11 +91,19 @@
     return (iota((128, 128), 1) < count_ref[0, 0]).astype(F32)
 
 
-def pack_kernel(count_ref, forward_ref, adjoint_ref, rim_ref):
+def pack_kernel(count_ref, forward_ref, adjoint_ref, rim_ref, field_ref, forward_in, adjoint_in, sems):
+    pairs = ((forward_ref, forward_in), (adjoint_ref, adjoint_in))
+    copies = [pltpu.make_async_copy(a, b, sems.at[i]) for i, (a, b) in enumerate(pairs)]
+    for copy in copies:
+        copy.start()
+    for copy in copies:
+        copy.wait()
     live = live_mask(count_ref)
-    fields = [padded(ref, c) * live for ref in (forward_ref, adjoint_ref) for c in range(3)]
+    fields = [padded(ref, c) * live for ref in (forward_in, adjoint_in) for c in range(3)]
     rim_ref[:128] = pack_rim(fields[:4])
     rim_ref[128:] = fold(pack_rim(fields[4:]))
+    for k in range(6):
+        field_ref[k] = fields[k]
 
 
 def split_stiffness(stiff_ref):
@@ -102,13 +115,11 @@
     return [x[:, 128 * k : 128 * (k + 1)] for k in range(x.shape[1] // 128)]
 
 
-def strains(stiffness, x):
-    high, low = stiffness
+def strains(high, low, x):
     return columns(dot(jnp.concatenate([high, high], axis=1), x) + dot(low, x[:128]))
 
 
-def faces_of(x):
-    pick = picker()
+def faces_of(pick, x):
     return columns(dot(jnp.concatenate([pick, pick], axis=1), x))
 
 
@@ -116,9 +127,8 @@
     return jnp.take_along_axis(x, index, axis=1, mode="promise_in_bounds")
 
 
-def lift_of(jumps):
+def lift_of(lift, jumps):
     high, low = halves(jnp.concatenate([jnp.concatenate(j, axis=0) for j in jumps], axis=1))
-    lift = lifter()
     return columns(dot(lift, high) + dot(lift, low))
 
 
@@ -126,7 +136,7 @@
     jumps = [[] for _ in own]
     for face in range(FACES):
         p = partner_face[face]
-        near = jnp.broadcast_to(near_ref[face : face + 1, :], (SHEET, 128))
+        near = jnp.broadcast_to(near_ref[face], (SHEET, 128))
         home = near // 128 == place_ref[0]
         slot = near % 128
         for k in range(len(own)):
@@ -141,7 +151,7 @@
     jumps = [[] for _ in range(n)]
     for face in range(FACES):
         p = partner_face[face]
-        near = jnp.broadcast_to(near_ref[face : face + 1, :], (SHEET, 128))
+        near = jnp.broadcast_to(near_ref[face], (SHEET, 128))
         target = near // 128
         away = target != mine
         index = near % RIM + jnp.where(target == follower, 64, 0)
@@ -169,56 +179,84 @@
 
 
 def own_kernel(
-    count_ref, place_ref, forward_ref, adjoint_ref, stiff_ref, near_ref, material_ref, smooth_ref,
-    partial_ref, kernel_ref, edge_ref, turned_ref,
+    count_ref, place_ref, field_ref, *refs
 ):
+    sources, refs = refs[:6], refs[6:]
+    partial_ref, kernel_ref, edge_ref, turned_ref, stiff_out_ref, pick_ref, lift_ref, project_out_ref = refs[:8]
+    wanted_ref, near_out_ref, material_out_ref = refs[8:11]
+    held, sems = refs[11:17], refs[17]
+    copies = [pltpu.make_async_copy(a, b, sems.at[i]) for i, (a, b) in enumerate(zip(sources, held))]
+    for copy in copies:
+        copy.start()
+    stiff_ref, near_ref, material_ref, smooth_ref, project_ref, destination_ref = held
     live = live_mask(count_ref)
+    fields = [field_ref[k] for k in range(6)]
+    pick, lift = picker(), lifter()
+    pick_ref[...] = pick
+    lift_ref[...] = lift
+    x = stacked(fields)
+    faces = faces_of(pick, x)
+    copies[1].wait()
+    near_out_ref[...] = near_ref[...]
+    lifted = lift_of(lift, own_jumps(place_ref, near_ref, faces))
+    copies[0].wait()
+    copies[2].wait()
+    high, low = split_stiffness(stiff_ref)
+    stiff_out_ref[0] = high
+    stiff_out_ref[1] = low
     material = jnp.broadcast_to(material_ref[...], (128, 128))
-    fields = [padded(ref, c) * live for ref in (forward_ref, adjoint_ref) for c in range(3)]
-    x = stacked(fields)
-    strain = strains(split_stiffness(stiff_ref), x)
-    lift = lift_of(own_jumps(place_ref, near_ref, faces_of(x)))
+    material_out_ref[...] = jnp.broadcast_to(material_ref[...], (8, 128))
+    strain = strains(high, low, x)
     for k in range(6):
-        force = 0.5 * lift[k] - material * strain[k]
+        force = 0.5 * lifted[k] - material * strain[k]
         partial_ref[k] = live * (fields[k] + 0.4 * force)
     kernel_ref[...] = sum(fields[c] * strain[3 + c] for c in range(3))
+    copies[3].wait()
     row, turned = edges_of(smooth_ref)
     edge_ref[...] = jnp.broadcast_to(row, (8, 128))
     turned_ref[...] = turned[:8]
+    copies[4].wait()
+    copies[5].wait()
+    high, low = halves(jnp.concatenate([project_ref[...], jnp.zeros((64, 128 - NODES), F32)], axis=1))
+    project_out_ref[0] = high
+    project_out_ref[1] = low
+    wanted_ref[...] = jnp.broadcast_to(destination_ref[...].astype(F32), (8, 128))
 
 
 def step_kernel(
     scale, n_mesh,
-    count_ref, place_ref, partial_ref, kernel_ref, before_ref, after_ref, near_ref, stiff_ref, project_ref,
-    destination_ref, edge_ref,
-    forward_ref, strain_ref, rim_ref, edge_out_ref, chunk_ref,
+    count_ref, place_ref, partial_ref, kernel_ref, before_ref, after_ref, near_ref, stiff_ref, pick_ref, lift_ref,
+    project_ref, wanted_ref, edge_ref,
+    forward_ref, strain_ref, rim_ref, chunk_ref,
 ):
     live = live_mask(count_ref)
     first, second = merge(before_ref[:128], after_ref[:128])
     upper, lower = merge(before_ref[128:], after_ref[128:])
-    rims = faces_of(stacked([first, second, jnp.concatenate([upper, lower], axis=0)]))
-    lift = lift_of(rim_jumps(place_ref, near_ref, rims, 6))
+    rims = faces_of(pick_ref[...], stacked([first, second, jnp.concatenate([upper, lower], axis=0)]))
+    lift = lift_of(lift_ref[...], rim_jumps(place_ref, near_ref, rims, 6))
     fields = [partial_ref[k] + live * (0.2 * lift[k]) for k in range(6)]
+    strain = strains(stiff_ref[0], stiff_ref[1], stacked(fields))
+    kernel = kernel_ref[...] + sum(fields[c] * strain[3 + c] for c in range(3))
+    k_high, k_low = halves(kernel)
+    p_high, p_low = project_ref[0], project_ref[1]
+    blocks = dot(jnp.concatenate([p_high, p_high], axis=1), jnp.concatenate([k_high, k_low], axis=0))
+    blocks = (blocks + dot(p_low, k_high)) * scale
+    turned = jnp.concatenate([blocks, pltpu.roll(blocks, 64, 1)], axis=0).T[:64]
+    for m in range(n_mesh):
+        chunk_ref[m, :64] = turned
+        chunk_ref[m, 64:] = wanted_ref[...]
     rim = pack_rim(fields[:3])
     rim_ref[...] = jnp.where(iota((128, 128), 0) == NODES, jnp.broadcast_to(edge_ref[0:1, :], (128, 128)), rim)
-    edge_out_ref[...] = edge_ref[...]
-    strain = strains(split_stiffness(stiff_ref), stacked(fields))
     for c in range(3):
         forward_ref[c] = fields[c]
         strain_ref[c] = strain[c]
-    kernel = kernel_ref[...] + sum(fields[c] * strain[3 + c] for c in range(3))
-    k_high, k_low = halves(kernel)
-    p_high, p_low = halves(jnp.concatenate([project_ref[...], jnp.zeros((64, 128 - NODES), F32)], axis=1))
-    blocks = dot(jnp.concatenate([p_high, p_high], axis=1), jnp.concatenate([k_high, k_low], axis=0))
-    blocks = (blocks + dot(p_low, k_high)) * scale
-    turned = jnp.concatenate([blocks, pltpu.roll(blocks, 64, 1)], axis=0).T[:64]
-    wanted = jnp.broadcast_to(destination_ref[...].astype(F32), (8, 128))
-    for m in range(n_mesh):
-        chunk_ref[m, :64] = turned
-        chunk_ref[m, 64:] = wanted
-
-
-def dense_kernel(n_event, n_mesh, tile_width, place_ref, parts_ref, before_ref, after_ref, wrap_ref, out_ref):
+
+
+def dense_kernel(
+    n_event, n_mesh, tile_width, place_ref, parts_ref, rim_ref, edge_ref, out_ref, rim_out_ref, edge_out_ref
+):
+    rim_out_ref[...] = rim_ref[...]
+    edge_out_ref[...] = edge_ref[...]
     rows = 4 * n_event
     row = iota((2 * rows, 128), 0)
     within = row % rows
@@ -240,24 +278,25 @@
 
 
 def last_kernel(
-    count_ref, place_ref, forward_ref, one_ref, strain_ref, before_ref, after_ref, near_ref, material_ref, turned_ref,
-    wrap_ref,
+    count_ref, place_ref, field_ref, one_ref, strain_ref, before_ref, after_ref, near_ref, material_ref, turned_ref,
+    wrap_ref, pick_ref, lift_ref,
     final_ref, coef_ref,
 ):
     live = live_mask(count_ref)
-    material = jnp.broadcast_to(material_ref[...], (128, 128))
+    material = jnp.broadcast_to(material_ref[0:1], (128, 128))
     fields = [one_ref[c] for c in range(3)]
-    jumps = own_jumps(place_ref, near_ref, faces_of(stacked(fields)))
+    jumps = own_jumps(place_ref, near_ref, faces_of(pick_ref[...], stacked(fields)))
     row = iota((128, 128), 0)
     before = jnp.where(row < NODES, before_ref[...], 0.0)
     after = jnp.where(row < NODES, after_ref[...], 0.0)
-    rims = faces_of(stacked(list(merge(before, after))))
+    rims = faces_of(pick_ref[...], stacked(list(merge(before, after))))
     more = rim_jumps(place_ref, near_ref, rims, 3)
-    lift = lift_of([[a + b for a, b in zip(*pair)] for pair in zip(jumps, more)])
+    lift = lift_of(lift_ref[...], [[a + b for a, b in zip(*pair)] for pair in zip(jumps, more)])
+    final = rows_of(final_ref)
     for c in range(3):
         force = 0.5 * lift[c] - material * strain_ref[c]
-        out = live * (2.0 * fields[c] - padded(forward_ref, c) * live + 0.4 * force)
-        final_ref[c] = out[:NODES]
+        out = live * (2.0 * fields[c] - field_ref[c] + 0.4 * force)
+        final[NODES * c : NODES * (c + 1)] = out[:NODES]
     mine, parts = place_ref[0], place_ref[1]
     wrap = wrap_ref[0:1]
     first = jnp.where(jnp.full((1, 128), mine) == 0, wrap, before_ref[NODES : NODES + 1])
@@ -291,13 +330,14 @@
     o_ref[...] = x[2:6, :64]
 
 
-def call(kernel, out_shape, n_smem, n_vmem, n_any=0):
+def call(kernel, out_shape, n_smem, n_vmem, n_hbm=0, scratch=()):
     many = isinstance(out_shape, tuple)
     return pl.pallas_call(
         kernel,
         out_shape=out_shape,
-        in_specs=[SMEM] * n_smem + [VMEM] * n_vmem + [ANY] * n_any,
+        in_specs=[SMEM] * n_smem + [VMEM] * n_vmem + [HBM] * n_hbm,
         out_specs=(VMEM,) * len(out_shape) if many else VMEM,
+        scratch_shapes=scratch,
         compiler_params=PARAMS,
     )
 
@@ -309,42 +349,62 @@
     tile_width = smoothing.shape[1]
     n_mesh, n_event = lax.axis_size("mesh"), lax.axis_size("event")
     scale = math.sqrt(tile_width / elements) / STEPS
-    forward, adjoint, near = forward_start[0], adjoint_start[0], neighbours[0]
+    forward, adjoint = (x.reshape(3, NODES, 1, 128) for x in (forward_start, adjoint_start))
     place = jnp.stack([lax.axis_index("mesh"), jnp.int32(n_mesh)]).astype(I32)
     up = [(i, (i + 1) % n_mesh) for i in range(n_mesh)]
     down = [(j, i) for i, j in up]
     ends = [((e + 1) * n_mesh - 1, (e + 1) * n_mesh) for e in range(n_event - 1)]
     ends = ends + [(j, i) for i, j in ends]
 
-    rim = call(pack_kernel, shape(192, 128), 1, 2)(counts, forward, adjoint)
+    held = [pltpu.VMEM(x.shape, F32) for x in (forward, adjoint)] + [pltpu.SemaphoreType.DMA((2,))]
+    forward, adjoint = (pltpu.with_memory_space_constraint(x, pltpu.HBM) for x in (forward, adjoint))
+    rim, fields = call(pack_kernel, (shape(192, 128), shape(6, 128, 128)), 1, 0, 2, held)(counts, forward, adjoint)
     before, after = lax.ppermute(rim, "mesh", up), lax.ppermute(rim, "mesh", down)
-    partial, kernel, edge, turned = call(
-        own_kernel, (shape(6, 128, 128), shape(128, 128), shape(8, 128), shape(8, 128)), 2, 6
-    )(counts, place, forward, adjoint, stiffness, near, material, smoothing)
+    small = (stiffness, neighbours.reshape(FACES, 1, 128), material, smoothing, projection.T, destinations)
+    small = tuple(pltpu.with_memory_space_constraint(x, pltpu.HBM) for x in small)
+    partial, kernel, edge, turned, stiff, pick, lift, project, wanted, near, material = call(
+        own_kernel,
+        (
+            shape(6, 128, 128),
+            shape(128, 128),
+            shape(8, 128),
+            shape(8, 128),
+            shape(2, 128, 128, dtype=BF16),
+            shape(FACES * SHEET, 128, dtype=BF16),
+            shape(128, FACES * SHEET, dtype=BF16),
+            shape(2, 64, 128, dtype=BF16),
+            shape(8, 128),
+            shape(FACES, 1, 128, dtype=I32),
+            shape(8, 128),
+        ),
+        2,
+        1,
+        6,
+        [pltpu.VMEM(x.shape, x.dtype) for x in small] + [pltpu.SemaphoreType.DMA((6,))],
+    )(counts, place, fields, *small)
 
     def one_step(*refs):
         step_kernel(scale, n_mesh, *refs)
 
-    one, strain, rim_one, edge, chunk = call(
-        one_step,
-        (shape(3, 128, 128), shape(3, 128, 128), shape(128, 128), shape(8, 128), shape(n_mesh, 72, 128)),
-        2,
-        9,
-    )(counts, place, partial, kernel, before, after, near, stiffness, projection.T, destinations, edge)
+    one, strain, rim_one, chunk = call(
+        one_step, (shape(3, 128, 128), shape(3, 128, 128), shape(128, 128), shape(n_mesh, 72, 128)), 2, 11
+    )(counts, place, partial, kernel, before, after, near, stiff, pick, lift, project, wanted, edge)
     parts = lax.all_to_all(chunk, "mesh", 0, 0, tiled=True)
+
+    def dense(*refs):
+        dense_kernel(n_event, n_mesh, tile_width, *refs)
+
+    partial, rim_one, edge = call(dense, (shape(4 * n_event, 128), shape(128, 128), shape(8, 128)), 1, 3)(
+        place, parts, rim_one, edge
+    )
+    pieces = lax.all_to_all(partial.reshape(n_event, 4, 128), "event", 0, 0, tiled=True)
     before, after = lax.ppermute(rim_one, "mesh", up), lax.ppermute(rim_one, "mesh", down)
     wrap = lax.ppermute(edge, ("event", "mesh"), ends)
-
-    def dense(*refs):
-        dense_kernel(n_event, n_mesh, tile_width, *refs)
-
-    partial = call(dense, shape(4 * n_event, 128), 1, 1, 3)(place, parts, before, after, wrap)
-    pieces = lax.all_to_all(partial.reshape(n_event, 4, 128), "event", 0, 0, tiled=True)
-    final, coefs = call(last_kernel, (shape(3, NODES, 128), shape(4, 8, 128)), 2, 9)(
-        counts, place, forward, one, strain, before, after, near, material, turned, wrap
+    final, coefs = call(last_kernel, (shape(3, NODES, 1, 128), shape(4, 8, 128)), 2, 11)(
+        counts, place, fields, one, strain, before, after, near, material, turned, wrap, pick, lift
     )
     tiles = call(smooth_kernel, shape(tile_width, 64), 0, 2)(pieces, coefs)
-    return final[None], tiles.T
+    return final.reshape(1, 3, NODES, 128), tiles.T
 
 
 def solution(mesh):

time: 78.8 us -> 70.9 us (0.90)
  blocking collectives: 0 us -> 12.2 us
  waiting for transfers between devices: 16.9 us -> 5.85 us
  starting transfers between devices: 48.6 us -> 41 us
  local copies, waits for them, and re-layouts: 3.25 us -> 0 us
  Pallas kernels: 8.12 us -> 10.1 us
    all_to_all x0 -> x1, blocking collectives: none -> 12.2 us  [per_device(): parts = lax.all_to_all(chunk, 'mesh', 0, 0, tiled=True)]
    all_to_all x1, waiting for transfers between devices: 10.9 us -> 0.01 us  [per_device(): lax.all_to_all(partial.reshape(n_event, 4, 128), 'event', 0, 0, tiled=True)]
    all_to_all x1 -> x0, starting transfers between devices: 3.58 us -> none  [per_device(): parts = lax.all_to_all(chunk, 'mesh', 0, 0, tiled=True)]
    unnamed x15 -> x0, local copies, waits for them, and re-layouts: 3.25 us -> none
    ppermute x1, starting transfers between devices: 6.56 us -> 3.37 us  [per_device(): lax.ppermute(rim_one, 'mesh', down)]
    ppermute x1, starting transfers between devices: 9.69 us -> 7.36 us  [per_device(): wrap = lax.ppermute(edge, ('event', 'mesh'), ends)]
    pallas_call x3, Pallas kernels: 3.21 us -> 4.92 us  [the longest x1 1.96 us: per_device(): call(last_kernel, (shape(3, NODES, 1, 128), shape(4, 8, 128)), 2, 11)]
    all_to_all x1, starting transfers between devices: 17.3 us -> 18.8 us  [per_device(): lax.all_to_all(partial.reshape(n_event, 4, 128), 'event', 0, 0, tiled=True)]
  transfers between devices with their start and end apart: 7 -> 6, of which waited for: 3 -> 2; matrix products, arithmetic and copies ran while one was open for 1% -> 0% of each run, Pallas kernels for 3% -> 6%
where the time goes in v3:
time: 70.9 us; the launch traced here: 70.6 us
  starting transfers between devices  41 us (58%)
  blocking collectives  12.2 us (17%)
  Pallas kernels  10.1 us (14%)
  waiting for transfers between devices  5.85 us (8%)
  between operations  1.36 us (2%)
    all_to_all x1, starting transfers between devices, per_device(): lax.all_to_all(partial.reshape(n_event, 4, 128), 'event', 0, 0, tiled=True)  18.8 us
    all_to_all x1, blocking collectives, per_device(): parts = lax.all_to_all(chunk, 'mesh', 0, 0, tiled=True)  12.2 us
    ppermute x1, starting transfers between devices, per_device(): lax.ppermute(rim, 'mesh', down)  7.67 us
    ppermute x1, starting transfers between devices, per_device(): wrap = lax.ppermute(edge, ('event', 'mesh'), ends)  7.36 us
    ppermute x1, waiting for transfers between devices, per_device(): lax.ppermute(rim, 'mesh', up)  4.27 us
    ppermute x1, starting transfers between devices, per_device(): lax.ppermute(rim_one, 'mesh', down)  3.37 us
    pallas_call x1, Pallas kernels, per_device(): call(own_kernel, (shape(6, 128, 128), shape(128, 128), shape(8, 128), sha...  2.38 us
    pallas_call x1, Pallas kernels, per_device(): call(last_kernel, (shape(3, NODES, 1, 128), shape(4, 8, 128)), 2, 11)  1.96 us
  transfers between devices with their start and end apart: 6, of which 2 were waited for; matrix products, arithmetic and copies ran while one was open for 0% of the time, Pallas kernels for 6%

profile of v3, /device:TPU:1, one launch (start us, length us, event | category | flops | bytes accessed | tf_op | source)
XLA Modules:
  0.0 70.6 jit_solution(14167932450528383455)
XLA Ops:
  1.3 1.2 %shard_map.104 = (f32[192,128]{1,0:T(8,128)S(1)}, f32[6,128,128]{2,1,0:T(8,128)S(1)}) custom-call(s32[1,1]{1,0:T(1,128)S(6)} %copy.11.count_ref.refs_0_, f32[3,125,1,128]{3,2,1,0:T(1,128)} %bitcast.8, f32[3,125,1,128]{3,2,1,0:T(1,128)} %bitcast.9), custom_call_target="tpu_custom_call" | custom-call | tf_op jit(solution)/shard_map/pallas_call | solution.py:361
  2.5 7.7 %collective-permute-start.1 = (f32[192,128]{1,0:T(8,128)S(1)}, f32[192,128]{1,0:T(8,128)S(1)}, u32[]{:S(2)}, u32[]{:S(2)}) collective-permute-start(f32[192,128]{1,0:T(8,128)S(1)} %get-tuple-element.27), channel_id=1, source_target_pairs={{1,0},{2,1},{3,2},{4,3},{5,4},{6,5},{7,6},{8,7},{9,8},{10,9},{11,1... | collective-permute-start | bytes 294920 | tf_op jit(solution)/shard_map/ppermute | solution.py:362
  10.1 1.9 %collective-permute-start = (f32[192,128]{1,0:T(8,128)S(1)}, f32[192,128]{1,0:T(8,128)S(1)}, u32[]{:S(2)}, u32[]{:S(2)}) collective-permute-start(f32[192,128]{1,0:T(8,128)S(1)} %get-tuple-element.27), channel_id=1, source_target_pairs={{0,1},{1,2},{2,3},{3,4},{4,5},{5,6},{6,7},{7,8},{8,9},{9,10},{10,1... | collective-permute-start | bytes 294920 | tf_op jit(solution)/shard_map/ppermute | solution.py:362
  12.1 0.1 pad_add_fusion.place_ref.refs_1_.refs_0_
  12.2 2.4 %shard_map.105 = (f32[6,128,128]{2,1,0:T(8,128)S(1)}, f32[128,128]{1,0:T(8,128)S(1)}, f32[8,128]{1,0:T(8,128)S(1)}, f32[8,128]{1,0:T(8,128)S(1)}, bf16[2,128,128...) custom-call(s32[1,1]{1,0:T(1,128)S(6)} %copy.11.count_ref.refs_0_, ...), custom_call_target="tpu_custom_call" | custom-call | tf_op jit(solution)/shard_map/pallas_call | solution.py:365
  14.5 0.0 collective-permute-done.1.refs_5_
  14.6 4.3 %collective-permute-done.refs_4_ = f32[192,128]{1,0:T(8,128)S(1)} collective-permute-done((f32[192,128]{1,0:T(8,128)S(1)}, f32[192,128]{1,0:T(8,128)S(1)}, u32[]{:S(2)}, u32[]{:S(2)}) %collective-permute-start) | collective-permute-done | bytes 98336 | tf_op jit(solution)/shard_map/ppermute | solution.py:362
  18.8 1.9 %shard_map.106 = (f32[3,128,128]{2,1,0:T(8,128)S(1)}, f32[3,128,128]{2,1,0:T(8,128)S(1)}, f32[128,128]{1,0:T(8,128)S(1)}, f32[16,72,128]{2,1,0:T(8,128)S(1)}) custom-call(s32[1,1]{1,0:T(1,128)S(6)} %copy.11.count_ref.refs_0_, s32[2]{0:T(128)S(1)} %pad_add_fusion.place_ref.refs_1_.refs_0_, f32[6,128,128]{2,1,0:T(8,128)S(1)} %get-tuple-element.25.refs_2_, ...), custom_call_target="tpu_custom_call" | custom-call | tf_op jit(solution)/shard_map/pallas_call | solution.py:389
  20.8 12.2 %all_to_all.10.refs_1_ = f32[16,72,128]{2,1,0:T(8,128)S(1)} all-to-all(f32[16,72,128]{2,1,0:T(8,128)S(1)} %get-tuple-element.37), channel_id=1, replica_groups=mesh['event'=32,'mesh'=16] {'mesh'}, dimensions={0} | all-to-all | bytes 1179648 | tf_op jit(solution)/shard_map/all_to_all | solution.py:392
  32.9 1.8 %shard_map.107 = (f32[128,128]{1,0:T(8,128)}, f32[128,128]{1,0:T(8,128)S(1)}, f32[8,128]{1,0:T(8,128)S(1)}) custom-call(s32[2]{0:T(128)S(1)} %pad_add_fusion.place_ref.refs_1_.refs_0_, f32[16,72,128]{2,1,0:T(8,128)S(1)} %all_to_all.10.refs_1_, f32[128,128]{1,0:T(8,128)S(1)} %get-tuple-element.38.refs_2_, f32[8,128]{1,0:T(8,128)S(1)} %get-tuple-element.34.refs_12_.refs_3_), custom_call_target="tpu_custom_call" | custom-call | tf_op jit(solution)/shard_map/pallas_call | solution.py:397
  34.7 18.8 %all-to-all-start.1 = ((f32[32,4,128]{2,1,0:T(4,128)}), f32[32,4,128]{2,1,0:T(4,128)S(1)}, u32[]{:S(2)}, u32[]{:S(2)}) async-start(f32[32,4,128]{2,1,0:T(4,128)} %bitcast.6), calls=%async_computation.1 | async-start | bytes 131072 | tf_op jit(solution)/shard_map/all_to_all | solution.py:400
  53.5 3.4 %collective-permute-start.3 = (f32[128,128]{1,0:T(8,128)S(1)}, f32[128,128]{1,0:T(8,128)S(1)}, u32[]{:S(2)}, u32[]{:S(2)}) collective-permute-start(f32[128,128]{1,0:T(8,128)S(1)} %get-tuple-element.39), channel_id=1, source_target_pairs={{1,0},{2,1},{3,2},{4,3},{5,4},{6,5},{7,6},{8,7},{9,8},{10,9},{11,1... | collective-permute-start | bytes 196616 | tf_op jit(solution)/shard_map/ppermute | solution.py:401
  56.9 1.9 %collective-permute-start.2 = (f32[128,128]{1,0:T(8,128)S(1)}, f32[128,128]{1,0:T(8,128)S(1)}, u32[]{:S(2)}, u32[]{:S(2)}) collective-permute-start(f32[128,128]{1,0:T(8,128)S(1)} %get-tuple-element.39), channel_id=1, source_target_pairs={{0,1},{1,2},{2,3},{3,4},{4,5},{5,6},{6,7},{7,8},{8,9},{9,10},{10,1... | collective-permute-start | bytes 196616 | tf_op jit(solution)/shard_map/ppermute | solution.py:401
  58.8 7.4 %collective-permute-start.4 = (f32[8,128]{1,0:T(8,128)S(1)}, f32[8,128]{1,0:T(8,128)S(1)}, u32[]{:S(2)}, u32[]{:S(2)}) collective-permute-start(f32[8,128]{1,0:T(8,128)S(1)} %get-tuple-element.42), channel_id=1, source_target_pairs={{15,16},{31,32},{47,48},{63,64},{79,80},{95,96},{111,112},{127,128... | collective-permute-start | bytes 12296 | tf_op jit(solution)/shard_map/ppermute | solution.py:402
  66.2 1.6 %collective-permute-done.4.wrap_ref = f32[8,128]{1,0:T(8,128)S(1)} collective-permute-done((f32[8,128]{1,0:T(8,128)S(1)}, f32[8,128]{1,0:T(8,128)S(1)}, u32[]{:S(2)}, u32[]{:S(2)}) %collective-permute-start.4) | collective-permute-done | bytes 4128 | tf_op jit(solution)/shard_map/ppermute | solution.py:402
  67.8 0.0 collective-permute-done.3.after_ref
  67.8 0.0 collective-permute-done.2.before_ref
  67.8 2.0 %shard_map.108 = (f32[3,125,1,128]{3,2,1,0:T(1,128)}, f32[4,8,128]{2,1,0:T(8,128)S(1)}) custom-call(s32[1,1]{1,0:T(1,128)S(6)} %copy.11.count_ref.refs_0_, s32[2]{0:T(128)S(1)} %pad_add_fusion.place_ref.refs_1_.refs_0_, f32[6,128,128]{2,1,0:T(8,128)S(1)} %get-tuple-element.24.field_ref, f32[3,128,128]{2,1,0:T(8,128)S(1)} %get-tuple-element.35.one_ref, ...), custom_call_target="tpu_custom_call" | custom-call | tf_op jit(solution)/shard_map/pallas_call | solution.py:403
  69.7 0.0 all-to-all-done.1.x_ref
  69.7 0.8 %shard_map.109 = f32[4,64]{1,0:T(4,128)} custom-call(f32[32,4,128]{2,1,0:T(4,128)S(1)} %all-to-all-done.1.x_ref, f32[4,8,128]{2,1,0:T(8,128)S(1)} %get-tuple-element.45.coef_ref), custom_call_target="tpu_custom_call" | custom-call | tf_op jit(solution)/shard_map/pallas_call | solution.py:406
Async XLA Ops:
  2.5 12.1 %collective-permute-start.1 = (f32[192,128]{1,0:T(8,128)S(1)}, f32[192,128]{1,0:T(8,128)S(1)}, u32[]{:S(2)}, u32[]{:S(2)}) collective-permute-start(f32[192,128]{1,0:T(8,128)S(1)} %get-tuple-element.27), channel_id=1, source_target_pairs={{1,0},{2,1},{3,2},{4,3},{5,4},{6,5},{7,6},{8,7},{9,8},{10,9},{11,1... | collective-permute-start | bytes 294920 | tf_op jit(solution)/shard_map/ppermute | solution.py:362
  10.1 8.7 %collective-permute-start = (f32[192,128]{1,0:T(8,128)S(1)}, f32[192,128]{1,0:T(8,128)S(1)}, u32[]{:S(2)}, u32[]{:S(2)}) collective-permute-start(f32[192,128]{1,0:T(8,128)S(1)} %get-tuple-element.27), channel_id=1, source_target_pairs={{0,1},{1,2},{2,3},{3,4},{4,5},{5,6},{6,7},{7,8},{8,9},{9,10},{10,1... | collective-permute-start | bytes 294920 | tf_op jit(solution)/shard_map/ppermute | solution.py:362
  34.7 35.0 %all-to-all-start.1 = ((f32[32,4,128]{2,1,0:T(4,128)}), f32[32,4,128]{2,1,0:T(4,128)S(1)}, u32[]{:S(2)}, u32[]{:S(2)}) async-start(f32[32,4,128]{2,1,0:T(4,128)} %bitcast.6), calls=%async_computation.1 | async-start | bytes 131072 | tf_op jit(solution)/shard_map/all_to_all | solution.py:400
  53.5 14.2 %collective-permute-start.3 = (f32[128,128]{1,0:T(8,128)S(1)}, f32[128,128]{1,0:T(8,128)S(1)}, u32[]{:S(2)}, u32[]{:S(2)}) collective-permute-start(f32[128,128]{1,0:T(8,128)S(1)} %get-tuple-element.39), channel_id=1, source_target_pairs={{1,0},{2,1},{3,2},{4,3},{5,4},{6,5},{7,6},{8,7},{9,8},{10,9},{11,1... | collective-permute-start | bytes 196616 | tf_op jit(solution)/shard_map/ppermute | solution.py:401
  56.9 10.9 %collective-permute-start.2 = (f32[128,128]{1,0:T(8,128)S(1)}, f32[128,128]{1,0:T(8,128)S(1)}, u32[]{:S(2)}, u32[]{:S(2)}) collective-permute-start(f32[128,128]{1,0:T(8,128)S(1)} %get-tuple-element.39), channel_id=1, source_target_pairs={{0,1},{1,2},{2,3},{3,4},{4,5},{5,6},{6,7},{7,8},{8,9},{9,10},{10,1... | collective-permute-start | bytes 196616 | tf_op jit(solution)/shard_map/ppermute | solution.py:401
  58.8 8.9 %collective-permute-start.4 = (f32[8,128]{1,0:T(8,128)S(1)}, f32[8,128]{1,0:T(8,128)S(1)}, u32[]{:S(2)}, u32[]{:S(2)}) collective-permute-start(f32[8,128]{1,0:T(8,128)S(1)} %get-tuple-element.42), channel_id=1, source_target_pairs={{15,16},{31,32},{47,48},{63,64},{79,80},{95,96},{111,112},{127,128... | collective-permute-start | bytes 12296 | tf_op jit(solution)/shard_map/ppermute | solution.py:402

commit v4 on v3

v4 whole, which is shorter than its diff:
```python
import math

import jax
import jax.numpy as jnp
from jax import lax
from jax.experimental import pallas as pl
from jax.experimental.pallas import tpu as pltpu
from jax.sharding import PartitionSpec as P

STEPS = 2
NODES = 125
RIM = 32
SHEET = 32
FACES = 6
F32, BF16, I32 = jnp.float32, jnp.bfloat16, jnp.int32
partner_face = (1, 0, 3, 2, 5, 4)

VMEM = pl.BlockSpec(memory_space=pltpu.VMEM)
SMEM = pl.BlockSpec(memory_space=pltpu.SMEM)
HBM = pl.BlockSpec(memory_space=pltpu.HBM)
PARAMS = pltpu.CompilerParams(vmem_limit_bytes=40 * 2**20)


def shape(*dims, dtype=F32):
    return jax.ShapeDtypeStruct(dims, dtype)


def iota(dims, axis):
    return lax.broadcasted_iota(I32, dims, axis)


def halves(x):
    high = x.astype(BF16)
    return high, (x - high.astype(F32)).astype(BF16)


def dot(a, b):
    return lax.dot_general(a, b, (((1,), (0,)), ((), ())), preferred_element_type=F32)


def face_nodes(dims, axis):
    row = iota(dims, axis)
    face, q = row // SHEET, row % SHEET
    a = sum((q >= 5 * i).astype(I32) for i in range(1, 5))
    b = q - 5 * a
    node = jnp.where(face == 0, q, q + 100)
    node = jnp.where(face == 2, 25 * a + b, node)
    node = jnp.where(face == 3, 25 * a + 20 + b, node)
    node = jnp.where(face == 4, 5 * q, node)
    node = jnp.where(face == 5, 5 * q + 4, node)
    return jnp.where(q < 25, node, -1)


def picker():
    dims = (FACES * SHEET, 128)
    return jnp.where(face_nodes(dims, 0) == iota(dims, 1), 1.0, 0.0).astype(BF16)


def lifter():
    dims = (128, FACES * SHEET)
    return jnp.where(face_nodes(dims, 1) == iota(dims, 0), 1.0, 0.0).astype(BF16)


def rows_of(ref):
    return ref.reshape(3 * NODES, 128)


def flat_of(ref):
    return ref.reshape(ref.shape[0], 128)


def padded(ref, c):
    rows = rows_of(ref)[NODES * c : NODES * (c + 1)]
    return jnp.concatenate([rows, jnp.zeros((128 - NODES, 128), F32)], axis=0)


def stacked(fields):
    high, low = halves(jnp.concatenate(fields, axis=1))
    return jnp.concatenate([high, low], axis=0)


def pack_rim(fields):
    lane = iota((128, 128), 1)
    out = fields[0]
    for k in range(1, len(fields)):
        out = jnp.where(lane < RIM * k, out, pltpu.roll(fields[k], RIM * k, 1))
    return jnp.where(lane < RIM * len(fields), out, 0.0)


def fold(x):
    return jnp.where(iota((64, 128), 1) < 64, x[:64], pltpu.roll(x[64:], 64, 1))


def live_mask(count_ref):
    return (iota((128, 128), 1) < count_ref[0, 0]).astype(F32)


def edge_row(smooth_ref):
    width = smooth_ref.shape[1]
    last = jnp.broadcast_to(smooth_ref[:, width - 1 : width], (4, 128))
    first = jnp.broadcast_to(smooth_ref[:, 0:1], (4, 128))
    lane, row = iota((4, 128), 1), iota((4, 128), 0)
    spread = jnp.where(lane == row, last, 0.0) + jnp.where(lane == row + 4, first, 0.0)
    return jnp.sum(spread, axis=0, keepdims=True)


def pack_kernel(count_ref, *refs):
    sources, rim_ref, field_ref, targets, sems = refs[:8], refs[8], refs[9], refs[10:18], refs[18]
    copies = [pltpu.make_async_copy(a, b, sems.at[i]) for i, (a, b) in enumerate(zip(sources, targets))]
    for copy in copies[6:] + copies[:6]:
        copy.start()
    for copy in copies[6:]:
        copy.wait()
    live = live_mask(count_ref)
    fields = [padded(ref, c) * live for ref in targets[6:] for c in range(3)]
    rim_ref[:128] = pack_rim(fields[:4])
    rim_ref[128:192] = fold(pack_rim(fields[4:]))
    for k in range(6):
        field_ref[k] = fields[k]
    for copy in copies[:6]:
        copy.wait()
    rim_ref[192:] = jnp.broadcast_to(edge_row(targets[3]), (8, 128))


def split_stiffness(stiff_ref):
    wide = jnp.concatenate([stiff_ref[...], jnp.zeros((NODES, 128 - NODES), F32)], axis=1)
    return halves(jnp.concatenate([wide, jnp.zeros((128 - NODES, 128), F32)], axis=0))


def columns(x):
    return [x[:, 128 * k : 128 * (k + 1)] for k in range(x.shape[1] // 128)]


def strains(high, low, x):
    return columns(dot(jnp.concatenate([high, high], axis=1), x) + dot(low, x[:128]))


def faces_of(pick, x):
    return columns(dot(jnp.concatenate([pick, pick], axis=1), x))


def take(x, index):
    return jnp.take_along_axis(x, index, axis=1, mode="promise_in_bounds")


def lift_of(lift, jumps):
    high, low = halves(jnp.concatenate([jnp.concatenate(j, axis=0) for j in jumps], axis=1))
    return columns(dot(lift, high) + dot(lift, low))


def own_jumps(place_ref, near_ref, own):
    jumps = [[] for _ in own]
    for face in range(FACES):
        p = partner_face[face]
        near = jnp.broadcast_to(near_ref[face], (SHEET, 128))
        home = near // 128 == place_ref[0]
        slot = near % 128
        for k in range(len(own)):
            here = take(own[k][SHEET * p : SHEET * (p + 1)], slot)
            jumps[k].append(jnp.where(home, here, 0.0) - own[k][SHEET * face : SHEET * (face + 1)])
    return jumps


def rim_jumps(place_ref, near_ref, rims, n):
    mine, parts = place_ref[0], place_ref[1]
    follower = jnp.where(mine + 1 == parts, 0, mine + 1)
    jumps = [[] for _ in range(n)]
    for face in range(FACES):
        p = partner_face[face]
        near = jnp.broadcast_to(near_ref[face], (SHEET, 128))
        target = near // 128
        away = target != mine
        index = near % RIM + jnp.where(target == follower, 64, 0)
        for k in range(n):
            across = take(rims[k // 2][SHEET * p : SHEET * (p + 1)], index + RIM * (k % 2))
            jumps[k].append(jnp.where(away, across, 0.0))
    return jumps


def merge(before, after):
    lane = iota(before.shape, 1)
    first = jnp.where(lane < 64, before, pltpu.roll(after, 64, 1))
    second = jnp.where(lane < 64, pltpu.roll(before, 64, 1), after)
    return first, second


def own_kernel(
    count_ref, place_ref, field_ref, stiff_ref, near_ref, material_ref, smooth_ref, project_ref, destination_ref,
    partial_ref, kernel_ref, turned_ref, stiff_out_ref, pick_ref, lift_ref, project_out_ref, wanted_ref,
):
    live = live_mask(count_ref)
    material = jnp.broadcast_to(material_ref[...], (128, 128))
    fields = [field_ref[k] for k in range(6)]
    pick, lift = picker(), lifter()
    pick_ref[...] = pick
    lift_ref[...] = lift
    x = stacked(fields)
    lifted = lift_of(lift, own_jumps(place_ref, near_ref, faces_of(pick, x)))
    high, low = split_stiffness(stiff_ref)
    stiff_out_ref[0] = high
    stiff_out_ref[1] = low
    strain = strains(high, low, x)
    for k in range(6):
        force = 0.5 * lifted[k] - material * strain[k]
        partial_ref[k] = live * (fields[k] + 0.4 * force)
    kernel_ref[...] = sum(fields[c] * strain[3 + c] for c in range(3))
    high, low = halves(jnp.concatenate([project_ref[...], jnp.zeros((64, 128 - NODES), F32)], axis=1))
    project_out_ref[0] = high
    project_out_ref[1] = low
    wanted_ref[...] = jnp.broadcast_to(destination_ref[...].astype(F32), (8, 128))
    width = smooth_ref.shape[1]
    wide = jnp.concatenate([smooth_ref[...], jnp.zeros((4, 128 - width), F32)], axis=1)
    turned_ref[...] = jnp.concatenate([wide, jnp.zeros((124, 128), F32)], axis=0).T[:8]


def step_kernel(
    scale, n_mesh,
    count_ref, place_ref, partial_ref, kernel_ref, before_ref, after_ref, near_ref, stiff_ref, pick_ref, lift_ref,
    project_ref, wanted_ref,
    forward_ref, strain_ref, rim_ref, edge_ref, chunk_ref,
):
    live = live_mask(count_ref)
    first, second = merge(before_ref[:128], after_ref[:128])
    upper, lower = merge(before_ref[128:192], after_ref[128:192])
    rims = faces_of(pick_ref[...], stacked([first, second, jnp.concatenate([upper, lower], axis=0)]))
    lift = lift_of(lift_ref[...], rim_jumps(place_ref, near_ref, rims, 6))
    fields = [partial_ref[k] + live * (0.2 * lift[k]) for k in range(6)]
    strain = strains(stiff_ref[0], stiff_ref[1], stacked(fields))
    kernel = kernel_ref[...] + sum(fields[c] * strain[3 + c] for c in range(3))
    k_high, k_low = halves(kernel)
    p_high, p_low = project_ref[0], project_ref[1]
    blocks = dot(jnp.concatenate([p_high, p_high], axis=1), jnp.concatenate([k_high, k_low], axis=0))
    blocks = (blocks + dot(p_low, k_high)) * scale
    turned = jnp.concatenate([blocks, pltpu.roll(blocks, 64, 1)], axis=0).T[:64]
    for m in range(n_mesh):
        chunk_ref[m, :64] = turned
        chunk_ref[m, 64:] = wanted_ref[...]
    rim_ref[...] = pack_rim(fields[:3])
    edge_ref[...] = jnp.where(iota((8, 128), 1) < 4, before_ref[192:], after_ref[192:])
    for c in range(3):
        forward_ref[c] = fields[c]
        strain_ref[c] = strain[c]


def dense_kernel(n_event, n_mesh, tile_width, first, place_ref, parts_ref, edge_ref, before_ref, after_ref, out_ref):
    rows = 4 * n_event
    row = iota((2 * rows, 128), 0)
    within = row % rows
    event = (within // 4 + first) % n_event
    tile = event * (n_mesh * tile_width) + within % 4 + 4 * (row // rows) - 2
    tile = tile.astype(F32) + (place_ref[0] * tile_width).astype(F32)
    lane = iota((64, 128), 1)
    left, right = [], []
    for m in range(n_mesh):
        x = parts_ref[m, :64]
        high = x.astype(BF16).astype(F32)
        low = x - high
        right.append(jnp.where(lane < 64, high, pltpu.roll(low, 64, 1)).astype(BF16))
        right.append(jnp.where(lane < 64, pltpu.roll(high, 64, 1), low).astype(BF16))
        wanted = jnp.broadcast_to(parts_ref[m, 64:65], (2 * rows, 128))
        left.append(jnp.where(wanted == tile, 1.0, 0.0).astype(BF16))
    both = dot(jnp.concatenate(left, axis=1), jnp.concatenate(right, axis=0))
    both = both + pltpu.roll(both, 64, 1)
    both = jnp.where(iota((rows, 128), 1) < 64, both[:rows], both[rows:])
    out = flat_of(out_ref)
    for p in range(n_event):
        out[5 * p : 5 * p + 4] = both[4 * p : 4 * p + 4]
        out[5 * p + 4 : 5 * p + 5] = edge_ref[0:1]


def last_kernel(
    count_ref, place_ref, field_ref, one_ref, strain_ref, before_ref, after_ref, near_ref, material_ref, turned_ref,
    edge_ref, pick_ref, lift_ref,
    final_ref, table_ref,
):
    live = live_mask(count_ref)
    material = jnp.broadcast_to(material_ref[...], (128, 128))
    fields = [one_ref[c] for c in range(3)]
    jumps = own_jumps(place_ref, near_ref, faces_of(pick_ref[...], stacked(fields)))
    rims = faces_of(pick_ref[...], stacked(list(merge(before_ref[...], after_ref[...]))))
    more = rim_jumps(place_ref, near_ref, rims, 3)
    lift = lift_of(lift_ref[...], [[a + b for a, b in zip(*pair)] for pair in zip(jumps, more)])
    final = rows_of(final_ref)
    for c in range(3):
        force = 0.5 * lift[c] - material * strain_ref[c]
        out = live * (2.0 * fields[c] - field_ref[c] + 0.4 * force)
        final[NODES * c : NODES * (c + 1)] = out[:NODES]
    tile = iota((8, 128), 0)
    table = jnp.where((tile >= 2) & (tile < 6), pltpu.roll(turned_ref[...], 2, 0), 0.0)
    table = jnp.where(tile == 1, edge_ref[...], table)
    table_ref[...] = jnp.where(tile == 6, pltpu.roll(edge_ref[...], 124, 1), table)


def total_of(parts):
    while len(parts) > 1:
        parts = [sum(parts[i : i + 2][1:], parts[i]) for i in range(0, len(parts), 2)]
    return parts[0]


def smooth_kernel(n_event, first, place_ref, x_ref, table_ref, o_ref):
    rows = flat_of(x_ref)
    mine, parts, event = place_ref[0], place_ref[1], place_ref[2]
    node, tile = iota((8, 128), 1), iota((8, 128), 0)
    table = table_ref[...]
    for row, end, there, by in ((1, mine == 0, event - 1, 0), (6, mine == parts - 1, event + 1, 124)):
        inside = (there >= 0) & (there < n_event)
        index = lax.rem(there - first + 2 * n_event, n_event)
        edge = jnp.broadcast_to(x_ref[5 * index + 4], (8, 128))
        edge = jnp.where(inside, pltpu.roll(edge, by, 1) if by else edge, 0.0)
        table = jnp.where((tile == row) & end, edge, table)
    coef = [jnp.broadcast_to(table[:, d : d + 1], (8, 128)) for d in range(4)]
    total = total_of([rows[5 * p : 5 * p + 4] for p in range(n_event)])
    x = jnp.concatenate([total, pltpu.roll(total, 64, 1)], axis=0)
    for _ in range(2):
        right = jnp.where(tile < 7, pltpu.roll(x, 7, 0), 0.0)
        left = jnp.where(tile > 0, pltpu.roll(x, 1, 0), 0.0)
        out = x + coef[0] * (left + right - 2.0 * x)
        for d, shift in ((1, 4), (2, 2), (3, 0)):
            place, stride = (node >> shift) & 3, 1 << shift
            up = jnp.where(place < 3, pltpu.roll(x, 128 - stride, 1), 0.0)
            down = jnp.where(place > 0, pltpu.roll(x, stride, 1), 0.0)
            out = out + coef[d] * (up + down - 2.0 * x)
        x = out
    o_ref[...] = x[2:6, :64]


def call(kernel, out_shape, n_smem, n_vmem, n_hbm=0, scratch=()):
    many = isinstance(out_shape, tuple)
    return pl.pallas_call(
        kernel,
        out_shape=out_shape,
        in_specs=[SMEM] * n_smem + [VMEM] * n_vmem + [HBM] * n_hbm,
        out_specs=(VMEM,) * len(out_shape) if many else VMEM,
        scratch_shapes=scratch,
        compiler_params=PARAMS,
    )


def per_device(
    forward_start, adjoint_start, stiffness, projection, material, neighbours, destinations, counts, smoothing
):
    elements = forward_start.shape[-1]
    tile_width = smoothing.shape[1]
    n_mesh, n_event = lax.axis_size("mesh"), lax.axis_size("event")
    scale = math.sqrt(tile_width / elements) / STEPS
    forward, adjoint = (x.reshape(3, NODES, 1, 128) for x in (forward_start, adjoint_start))
    place = jnp.stack([lax.axis_index("mesh"), jnp.int32(n_mesh), lax.axis_index("event")]).astype(I32)
    up = [(i, (i + 1) % n_mesh) for i in range(n_mesh)]
    down = [(j, i) for i, j in up]
    first_mesh, first_event = 5 * n_mesh // 8, n_event // 2
    mesh_group = [(i + first_mesh) % n_mesh for i in range(n_mesh)]
    event_group = [(i + first_event) % n_event for i in range(n_event)]

    inputs = (
        stiffness, neighbours.reshape(FACES, 1, 128), material, smoothing, projection.T, destinations, forward, adjoint
    )
    held = tuple(shape(*x.shape, dtype=x.dtype) for x in inputs)
    inputs = tuple(pltpu.with_memory_space_constraint(x, pltpu.HBM) for x in inputs)
    rim, fields, *small = call(
        pack_kernel, (shape(200, 128), shape(6, 128, 128)) + held, 1, 0, 8, [pltpu.SemaphoreType.DMA((8,))]
    )(counts, *inputs)
    small = small[:6]
    near, material = small[1], small[2]
    before, after = lax.ppermute(rim, "mesh", up), lax.ppermute(rim, "mesh", down)
    partial, kernel, turned, stiff, pick, lift, project, wanted = call(
        own_kernel,
        (
            shape(6, 128, 128),
            shape(128, 128),
            shape(8, 128),
            shape(2, 128, 128, dtype=BF16),
            shape(FACES * SHEET, 128, dtype=BF16),
            shape(128, FACES * SHEET, dtype=BF16),
            shape(2, 64, 128, dtype=BF16),
            shape(8, 128),
        ),
        2,
        7,
    )(counts, place, fields, *small)

    def one_step(*refs):
        step_kernel(scale, n_mesh, *refs)

    one, strain, rim_one, edge, chunk = call(
        one_step,
        (shape(3, 128, 128), shape(3, 128, 128), shape(128, 128), shape(8, 128), shape(n_mesh, 72, 128)),
        2,
        10,
    )(counts, place, partial, kernel, before, after, near, stiff, pick, lift, project, wanted)
    parts = lax.all_to_all(chunk, "mesh", 0, 0, tiled=True, axis_index_groups=[mesh_group])
    before, after = lax.ppermute(rim_one, "mesh", up), lax.ppermute(rim_one, "mesh", down)

    def dense(*refs):
        dense_kernel(n_event, n_mesh, tile_width, first_event, *refs)

    partial = call(dense, shape(5 * n_event, 1, 128), 1, 4)(place, parts, edge, before, after)
    pieces = lax.all_to_all(partial, "event", 0, 0, tiled=True, axis_index_groups=[event_group])
    final, table = call(last_kernel, (shape(3, NODES, 1, 128), shape(8, 128)), 2, 11)(
        counts, place, fields, one, strain, before, after, near, material, turned, edge, pick, lift
    )

    def smooth(*refs):
        smooth_kernel(n_event, first_event, *refs)

    tiles = call(smooth, shape(tile_width, 64), 1, 2)(place, pieces, table)
    return final.reshape(1, 3, NODES, 128), tiles.T


def solution(mesh):
    in_specs = (
        P("event", None, None, "mesh"),
        P("event", None, None, "mesh"),
        P(),
        P(),
        P("event", "mesh"),
        P("event", None, "mesh"),
        P("event", "mesh"),
        P("event", "mesh"),
        P(None, ("event", "mesh")),
    )
    out_specs = (P("event", None, None, "mesh"), P(None, ("event", "mesh")))
    return jax.shard_map(per_device, mesh=mesh, in_specs=in_specs, out_specs=out_specs, check_vma=False)
```

time: 70.9 us -> 70.9 us (level)
  blocking collectives: 12.2 us -> 0 us
  waiting for transfers between devices: 5.85 us -> 13.7 us
  starting transfers between devices: 41 us -> 44.3 us
  Pallas kernels: 10.1 us -> 11.2 us
    all_to_all x1 -> x0, blocking collectives: 12.2 us -> none  [per_device(): parts = lax.all_to_all(chunk, 'mesh', 0, 0, tiled=True)]
    all_to_all x1 -> x2, starting transfers between devices: 18.8 us -> 29.4 us  [the longest x1 22.7 us: per_device(): lax.all_to_all(partial, 'event', 0, 0, tiled=True, axis_index_groups=[eve...]
    ppermute x1 -> x0, starting transfers between devices: 7.36 us -> none  [per_device(): wrap = lax.ppermute(edge, ('event', 'mesh'), ends)]
    ppermute x1, waiting for transfers between devices: 0.01 us -> 3.37 us  [per_device(): lax.ppermute(rim_one, 'mesh', down)]
    all_to_all x1 -> x2, waiting for transfers between devices: 0.01 us -> 3.07 us  [the longest x1 3.06 us: per_device(): lax.all_to_all(partial, 'event', 0, 0, tiled=True, axis_index_groups=[eve...]
    ppermute x1, waiting for transfers between devices: 0.01 us -> 1.86 us  [per_device(): lax.ppermute(rim_one, 'mesh', up)]
    ppermute x1 -> x0, waiting for transfers between devices: 1.57 us -> none  [per_device(): wrap = lax.ppermute(edge, ('event', 'mesh'), ends)]
    pallas_call x4, Pallas kernels: 5.75 us -> 7.13 us  [the longest x1 2 us: per_device(): call(pack_kernel, (shape(200, 128), shape(6, 128, 128)) + held, 1, 0, 8,...]
  transfers between devices with their start and end apart: 6 -> 6, of which waited for: 2 -> 4; matrix products, arithmetic and copies ran while one was open for 0% -> 0% of each run, Pallas kernels for 6% -> 5%
where the time goes in v4:
time: 70.9 us; the launch traced here: 70.5 us
  starting transfers between devices  44.3 us (62%)
  waiting for transfers between devices  13.7 us (19%)
  Pallas kernels  11.2 us (16%)
  between operations  1.35 us (2%)
    all_to_all x1, starting transfers between devices, per_device(): lax.all_to_all(partial, 'event', 0, 0, tiled=True, axis_index_groups=[eve...  22.7 us
    ppermute x1, starting transfers between devices, per_device(): lax.ppermute(rim, 'mesh', down)  7.67 us
    all_to_all x1, starting transfers between devices, per_device(): lax.all_to_all(chunk, 'mesh', 0, 0, tiled=True, axis_index_groups=[mesh_g...  6.66 us
    ppermute x1, waiting for transfers between devices, per_device(): lax.ppermute(rim, 'mesh', up)  5.38 us
    ppermute x1, waiting for transfers between devices, per_device(): lax.ppermute(rim_one, 'mesh', down)  3.37 us
    ppermute x1, starting transfers between devices, per_device(): lax.ppermute(rim_one, 'mesh', up)  3.09 us
    all_to_all x1, waiting for transfers between devices, per_device(): lax.all_to_all(partial, 'event', 0, 0, tiled=True, axis_index_groups=[eve...  3.06 us
    pallas_call x1, Pallas kernels, per_device(): call(one_step, (shape(3, 128, 128), shape(3, 128, 128), shape(128, 128),...  2.73 us
  transfers between devices with their start and end apart: 6, of which 4 were waited for; matrix products, arithmetic and copies ran while one was open for 0% of the time, Pallas kernels for 5%

profile of v4, /device:TPU:1, one launch (start us, length us, event | category | flops | bytes accessed | tf_op | source)
XLA Modules:
  0.0 70.5 jit_solution(10759558730346085781)
XLA Ops:
  1.3 2.0 %shard_map.104 = (f32[200,128]{1,0:T(8,128)S(1)}, f32[6,128,128]{2,1,0:T(8,128)S(1)}, f32[125,125]{1,0:T(8,128)S(1)}, s32[6,1,128]{2,1,0:T(1,128)S(1)}, f32[1,12...) custom-call(s32[1,1]{1,0:T(1,128)S(6)} %copy.11.count_ref.refs_0_, ...), custom_call_target="tpu_custom_call" | custom-call | tf_op jit(solution)/shard_map/pallas_call | solution.py:359
  3.3 7.7 %collective-permute-start.1 = (f32[200,128]{1,0:T(8,128)S(1)}, f32[200,128]{1,0:T(8,128)S(1)}, u32[]{:S(2)}, u32[]{:S(2)}) collective-permute-start(f32[200,128]{1,0:T(8,128)S(1)} %get-tuple-element.34), channel_id=1, source_target_pairs={{1,0},{2,1},{3,2},{4,3},{5,4},{6,5},{7,6},{8,7},{9,8},{10,9},{11,1... | collective-permute-start | bytes 307208 | tf_op jit(solution)/shard_map/ppermute | solution.py:364
  11.0 1.9 %collective-permute-start = (f32[200,128]{1,0:T(8,128)S(1)}, f32[200,128]{1,0:T(8,128)S(1)}, u32[]{:S(2)}, u32[]{:S(2)}) collective-permute-start(f32[200,128]{1,0:T(8,128)S(1)} %get-tuple-element.34), channel_id=1, source_target_pairs={{0,1},{1,2},{2,3},{3,4},{4,5},{5,6},{6,7},{7,8},{8,9},{9,10},{10,1... | collective-permute-start | bytes 307208 | tf_op jit(solution)/shard_map/ppermute | solution.py:364
  12.9 0.1 pad_add_fusion.place_ref.refs_1_.refs_0_
  13.0 1.3 %shard_map.105 = (f32[6,128,128]{2,1,0:T(8,128)S(1)}, f32[128,128]{1,0:T(8,128)S(1)}, f32[8,128]{1,0:T(8,128)S(1)}, bf16[2,128,128]{2,1,0:T(8,128)(2,1)S(1)}, bf...) custom-call(s32[1,1]{1,0:T(1,128)S(6)} %copy.11.count_ref.refs_0_, ...), custom_call_target="tpu_custom_call" | custom-call | tf_op jit(solution)/shard_map/pallas_call | solution.py:365
  14.3 0.0 collective-permute-done.1.refs_5_
  14.3 5.4 %collective-permute-done.refs_4_ = f32[200,128]{1,0:T(8,128)S(1)} collective-permute-done((f32[200,128]{1,0:T(8,128)S(1)}, f32[200,128]{1,0:T(8,128)S(1)}, u32[]{:S(2)}, u32[]{:S(2)}) %collective-permute-start) | collective-permute-done | bytes 102432 | tf_op jit(solution)/shard_map/ppermute | solution.py:364
  19.7 2.7 %shard_map.106 = (f32[3,128,128]{2,1,0:T(8,128)S(1)}, f32[3,128,128]{2,1,0:T(8,128)S(1)}, f32[128,128]{1,0:T(8,128)S(1)}, f32[8,128]{1,0:T(8,128)S(1)}, f32[16,72,128]{2,1,0:T(8,128)}) custom-call(s32[1,1]{1,0:T(1,128)S(6)} %copy.11.count_ref.refs_0_, s32[3]{0:T(128)S(1)} %pad_add_fusion.place_ref.refs_1_.refs_0_, ...), custom_call_target="tpu_custom_call" | custom-call | tf_op jit(solution)/shard_map/pallas_call | solution.py:384
  22.4 6.7 %all-to-all-start = ((f32[16,72,128]{2,1,0:T(8,128)}), f32[16,72,128]{2,1,0:T(8,128)S(1)}, u32[]{:S(2)}, u32[]{:S(2)}) async-start(f32[16,72,128]{2,1,0:T(8,128)} %get-tuple-element.46), calls=%async_computation | async-start | bytes 1179648 | tf_op jit(solution)/shard_map/all_to_all | solution.py:390
  29.1 2.2 %collective-permute-start.3 = (f32[128,128]{1,0:T(8,128)S(1)}, f32[128,128]{1,0:T(8,128)S(1)}, u32[]{:S(2)}, u32[]{:S(2)}) collective-permute-start(f32[128,128]{1,0:T(8,128)S(1)} %get-tuple-element.42), channel_id=1, source_target_pairs={{1,0},{2,1},{3,2},{4,3},{5,4},{6,5},{7,6},{8,7},{9,8},{10,9},{11,1... | collective-permute-start | bytes 196616 | tf_op jit(solution)/shard_map/ppermute | solution.py:391
  31.3 3.1 %collective-permute-start.2 = (f32[128,128]{1,0:T(8,128)S(1)}, f32[128,128]{1,0:T(8,128)S(1)}, u32[]{:S(2)}, u32[]{:S(2)}) collective-permute-start(f32[128,128]{1,0:T(8,128)S(1)} %get-tuple-element.42), channel_id=1, source_target_pairs={{0,1},{1,2},{2,3},{3,4},{4,5},{5,6},{6,7},{7,8},{8,9},{9,10},{10,1... | collective-permute-start | bytes 196616 | tf_op jit(solution)/shard_map/ppermute | solution.py:391
  34.4 3.4 %collective-permute-done.3.after_ref.refs_4_ = f32[128,128]{1,0:T(8,128)S(1)} collective-permute-done((f32[128,128]{1,0:T(8,128)S(1)}, f32[128,128]{1,0:T(8,128)S(1)}, u32[]{:S(2)}, u32[]{:S(2)}) %collective-permute-start.3) | collective-permute-done | bytes 65568 | tf_op jit(solution)/shard_map/ppermute | solution.py:391
  37.7 1.9 %collective-permute-done.2.before_ref.refs_3_ = f32[128,128]{1,0:T(8,128)S(1)} collective-permute-done((f32[128,128]{1,0:T(8,128)S(1)}, f32[128,128]{1,0:T(8,128)S(1)}, u32[]{:S(2)}, u32[]{:S(2)}) %collective-permute-start.2) | collective-permute-done | bytes 65568 | tf_op jit(solution)/shard_map/ppermute | solution.py:391
  39.6 0.0 all-to-all-done.refs_1_
  39.6 1.8 %shard_map.108 = f32[160,1,128]{2,1,0:T(1,128)} custom-call(s32[3]{0:T(128)S(1)} %pad_add_fusion.place_ref.refs_1_.refs_0_, f32[16,72,128]{2,1,0:T(8,128)S(1)} %all-to-all-done.refs_1_, f32[8,128]{1,0:T(8,128)S(1)} %get-tuple-element.44.edge_ref.refs_2_, f32[128,128]{1,0:T(8,128)S(1)} %collective-permute-done.2.before_ref.refs_3_, ...), custom_call_target="tpu_custom_call" | custom-call | tf_op jit(solution)/shard_map/pallas_call | solution.py:396
  41.4 22.7 %all-to-all-start.1 = ((f32[160,1,128]{2,1,0:T(1,128)}), f32[160,1,128]{2,1,0:T(1,128)S(1)}, u32[]{:S(2)}, u32[]{:S(2)}) async-start(f32[160,1,128]{2,1,0:T(1,128)} %shard_map.108), calls=%async_computation.1 | async-start | bytes 163840 | tf_op jit(solution)/shard_map/all_to_all | solution.py:397
  64.2 2.0 %shard_map.107 = (f32[3,125,1,128]{3,2,1,0:T(1,128)}, f32[8,128]{1,0:T(8,128)S(1)}) custom-call(s32[1,1]{1,0:T(1,128)S(6)} %copy.11.count_ref.refs_0_, s32[3]{0:T(128)S(1)} %pad_add_fusion.place_ref.refs_1_.refs_0_, f32[6,128,128]{2,1,0:T(8,128)S(1)} %get-tuple-element.25.field_ref, f32[3,128,128]{2,1,0:T(8,128)S(1)} %get-tuple-element.40.one_ref, ...), custom_call_target="tpu_custom_call" | custom-call | tf_op jit(solution)/shard_map/pallas_call | solution.py:398
  66.1 3.1 %all-to-all-done.1.refs_1_ = f32[160,1,128]{2,1,0:T(1,128)S(1)} async-done(((f32[160,1,128]{2,1,0:T(1,128)}), f32[160,1,128]{2,1,0:T(1,128)S(1)}, u32[]{:S(2)}, u32[]{:S(2)}) %all-to-all-start.1) | async-done | bytes 81952 | tf_op jit(solution)/shard_map/all_to_all | solution.py:397
  69.2 1.4 %shard_map.109 = f32[4,64]{1,0:T(4,128)} custom-call(s32[3]{0:T(128)S(1)} %pad_add_fusion.place_ref.refs_1_.refs_0_, f32[160,1,128]{2,1,0:T(1,128)S(1)} %all-to-all-done.1.refs_1_, f32[8,128]{1,0:T(8,128)S(1)} %get-tuple-element.47.refs_2_), custom_call_target="tpu_custom_call" | custom-call | tf_op jit(solution)/shard_map/pallas_call | solution.py:405
Async XLA Ops:
  3.3 11.0 %collective-permute-start.1 = (f32[200,128]{1,0:T(8,128)S(1)}, f32[200,128]{1,0:T(8,128)S(1)}, u32[]{:S(2)}, u32[]{:S(2)}) collective-permute-start(f32[200,128]{1,0:T(8,128)S(1)} %get-tuple-element.34), channel_id=1, source_target_pairs={{1,0},{2,1},{3,2},{4,3},{5,4},{6,5},{7,6},{8,7},{9,8},{10,9},{11,1... | collective-permute-start | bytes 307208 | tf_op jit(solution)/shard_map/ppermute | solution.py:364
  11.0 8.7 %collective-permute-start = (f32[200,128]{1,0:T(8,128)S(1)}, f32[200,128]{1,0:T(8,128)S(1)}, u32[]{:S(2)}, u32[]{:S(2)}) collective-permute-start(f32[200,128]{1,0:T(8,128)S(1)} %get-tuple-element.34), channel_id=1, source_target_pairs={{0,1},{1,2},{2,3},{3,4},{4,5},{5,6},{6,7},{7,8},{8,9},{9,10},{10,1... | collective-permute-start | bytes 307208 | tf_op jit(solution)/shard_map/ppermute | solution.py:364
  22.4 17.2 %all-to-all-start = ((f32[16,72,128]{2,1,0:T(8,128)}), f32[16,72,128]{2,1,0:T(8,128)S(1)}, u32[]{:S(2)}, u32[]{:S(2)}) async-start(f32[16,72,128]{2,1,0:T(8,128)} %get-tuple-element.46), calls=%async_computation | async-start | bytes 1179648 | tf_op jit(solution)/shard_map/all_to_all | solution.py:390
  29.1 8.7 %collective-permute-start.3 = (f32[128,128]{1,0:T(8,128)S(1)}, f32[128,128]{1,0:T(8,128)S(1)}, u32[]{:S(2)}, u32[]{:S(2)}) collective-permute-start(f32[128,128]{1,0:T(8,128)S(1)} %get-tuple-element.42), channel_id=1, source_target_pairs={{1,0},{2,1},{3,2},{4,3},{5,4},{6,5},{7,6},{8,7},{9,8},{10,9},{11,1... | collective-permute-start | bytes 196616 | tf_op jit(solution)/shard_map/ppermute | solution.py:391
  31.3 8.3 %collective-permute-start.2 = (f32[128,128]{1,0:T(8,128)S(1)}, f32[128,128]{1,0:T(8,128)S(1)}, u32[]{:S(2)}, u32[]{:S(2)}) collective-permute-start(f32[128,128]{1,0:T(8,128)S(1)} %get-tuple-element.42), channel_id=1, source_target_pairs={{0,1},{1,2},{2,3},{3,4},{4,5},{5,6},{6,7},{7,8},{8,9},{9,10},{10,1... | collective-permute-start | bytes 196616 | tf_op jit(solution)/shard_map/ppermute | solution.py:391
  41.4 27.8 %all-to-all-start.1 = ((f32[160,1,128]{2,1,0:T(1,128)}), f32[160,1,128]{2,1,0:T(1,128)S(1)}, u32[]{:S(2)}, u32[]{:S(2)}) async-start(f32[160,1,128]{2,1,0:T(1,128)} %shard_map.108), calls=%async_computation.1 | async-start | bytes 163840 | tf_op jit(solution)/shard_map/all_to_all | solution.py:397

commit v5 on v4

--- a/solution.py
+++ b/solution.py
@@ -104,22 +104,26 @@
     return jnp.sum(spread, axis=0, keepdims=True)
 
 
-def pack_kernel(count_ref, *refs):
-    sources, rim_ref, field_ref, targets, sems = refs[:8], refs[8], refs[9], refs[10:18], refs[18]
+def copies_of(sources, targets, sems):
     copies = [pltpu.make_async_copy(a, b, sems.at[i]) for i, (a, b) in enumerate(zip(sources, targets))]
-    for copy in copies[6:] + copies[:6]:
+    for copy in copies:
         copy.start()
-    for copy in copies[6:]:
+    return copies
+
+
+def pack_kernel(count_ref, forward_ref, adjoint_ref, smooth_ref, rim_ref, field_ref, smooth_out_ref, *held):
+    copies = copies_of((forward_ref, adjoint_ref, smooth_ref), (*held[:2], smooth_out_ref), held[2])
+    live = live_mask(count_ref)
+    fields = []
+    for ref, copy in zip(held[:2], copies):
         copy.wait()
-    live = live_mask(count_ref)
-    fields = [padded(ref, c) * live for ref in targets[6:] for c in range(3)]
+        fields += [padded(ref, c) * live for c in range(3)]
     rim_ref[:128] = pack_rim(fields[:4])
     rim_ref[128:192] = fold(pack_rim(fields[4:]))
     for k in range(6):
         field_ref[k] = fields[k]
-    for copy in copies[:6]:
-        copy.wait()
-    rim_ref[192:] = jnp.broadcast_to(edge_row(targets[3]), (8, 128))
+    copies[2].wait()
+    rim_ref[192:] = jnp.broadcast_to(edge_row(smooth_out_ref), (8, 128))
 
 
 def split_stiffness(stiff_ref):
@@ -185,17 +189,27 @@
 
 
 def own_kernel(
-    count_ref, place_ref, field_ref, stiff_ref, near_ref, material_ref, smooth_ref, project_ref, destination_ref,
-    partial_ref, kernel_ref, turned_ref, stiff_out_ref, pick_ref, lift_ref, project_out_ref, wanted_ref,
+    count_ref, place_ref, field_ref, smooth_ref, near_in, stiff_in, material_in, project_in, destination_in,
+    partial_ref, kernel_ref, turned_ref, stiff_out_ref, pick_ref, lift_ref, project_out_ref, wanted_ref, near_ref,
+    material_ref, stiff_ref, project_ref, destination_ref, sems,
 ):
+    copies = copies_of(
+        (near_in, stiff_in, material_in, project_in, destination_in),
+        (near_ref, stiff_ref, material_ref, project_ref, destination_ref),
+        sems,
+    )
     live = live_mask(count_ref)
-    material = jnp.broadcast_to(material_ref[...], (128, 128))
     fields = [field_ref[k] for k in range(6)]
     pick, lift = picker(), lifter()
     pick_ref[...] = pick
     lift_ref[...] = lift
     x = stacked(fields)
-    lifted = lift_of(lift, own_jumps(place_ref, near_ref, faces_of(pick, x)))
+    faces = faces_of(pick, x)
+    copies[0].wait()
+    lifted = lift_of(lift, own_jumps(place_ref, near_ref, faces))
+    for copy in copies[1:]:
+        copy.wait()
+    material = jnp.broadcast_to(material_ref[...], (128, 128))
     high, low = split_stiffness(stiff_ref)
     stiff_out_ref[0] = high
     stiff_out_ref[1] = low
@@ -242,7 +256,7 @@
         strain_ref[c] = strain[c]
 
 
-def dense_kernel(n_event, n_mesh, tile_width, first, place_ref, parts_ref, edge_ref, before_ref, after_ref, out_ref):
+def dense_kernel(n_event, n_mesh, tile_width, first, place_ref, parts_ref, edge_ref, final_ref, out_ref):
     rows = 4 * n_event
     row = iota((2 * rows, 128), 0)
     within = row % rows
@@ -263,15 +277,18 @@
     both = both + pltpu.roll(both, 64, 1)
     both = jnp.where(iota((rows, 128), 1) < 64, both[:rows], both[rows:])
     out = flat_of(out_ref)
+    lane, apart = iota((n_event, 128), 1), (iota((n_event, 128), 0) + first) % n_event - place_ref[2]
+    used = ((apart == 1) & (lane < 4)) | ((apart == -1) & (lane >= 4) & (lane < 8))
+    edges = jnp.where(used, jnp.broadcast_to(edge_ref[0:1], (n_event, 128)), 0.0)
     for p in range(n_event):
         out[5 * p : 5 * p + 4] = both[4 * p : 4 * p + 4]
-        out[5 * p + 4 : 5 * p + 5] = edge_ref[0:1]
+        out[5 * p + 4 : 5 * p + 5] = edges[p : p + 1]
 
 
 def last_kernel(
-    count_ref, place_ref, field_ref, one_ref, strain_ref, before_ref, after_ref, near_ref, material_ref, turned_ref,
-    edge_ref, pick_ref, lift_ref,
-    final_ref, table_ref,
+    count_ref, place_ref, field_ref, one_ref, strain_ref, before_ref, after_ref, near_ref, material_ref,
+    pick_ref, lift_ref,
+    final_ref,
 ):
     live = live_mask(count_ref)
     material = jnp.broadcast_to(material_ref[...], (128, 128))
@@ -285,10 +302,6 @@
         force = 0.5 * lift[c] - material * strain_ref[c]
         out = live * (2.0 * fields[c] - field_ref[c] + 0.4 * force)
         final[NODES * c : NODES * (c + 1)] = out[:NODES]
-    tile = iota((8, 128), 0)
-    table = jnp.where((tile >= 2) & (tile < 6), pltpu.roll(turned_ref[...], 2, 0), 0.0)
-    table = jnp.where(tile == 1, edge_ref[...], table)
-    table_ref[...] = jnp.where(tile == 6, pltpu.roll(edge_ref[...], 124, 1), table)
 
 
 def total_of(parts):
@@ -297,19 +310,19 @@
     return parts[0]
 
 
-def smooth_kernel(n_event, first, place_ref, x_ref, table_ref, o_ref):
+def smooth_kernel(n_event, place_ref, x_ref, turned_ref, edge_ref, o_ref):
     rows = flat_of(x_ref)
-    mine, parts, event = place_ref[0], place_ref[1], place_ref[2]
+    mine, parts = place_ref[0], place_ref[1]
     node, tile = iota((8, 128), 1), iota((8, 128), 0)
-    table = table_ref[...]
-    for row, end, there, by in ((1, mine == 0, event - 1, 0), (6, mine == parts - 1, event + 1, 124)):
-        inside = (there >= 0) & (there < n_event)
-        index = lax.rem(there - first + 2 * n_event, n_event)
-        edge = jnp.broadcast_to(x_ref[5 * index + 4], (8, 128))
-        edge = jnp.where(inside, pltpu.roll(edge, by, 1) if by else edge, 0.0)
-        table = jnp.where((tile == row) & end, edge, table)
+    total = total_of([rows[5 * p : 5 * p + 5] for p in range(n_event)])
+    lane = iota((1, 128), 1)
+    beside = ((lane < 4) & (mine > 0)) | ((lane >= 4) & (mine < parts - 1))
+    edge = jnp.broadcast_to(jnp.where(beside, edge_ref[0:1], total[4:5]), (8, 128))
+    table = jnp.where((tile >= 2) & (tile < 6), pltpu.roll(turned_ref[...], 2, 0), 0.0)
+    table = jnp.where(tile == 1, edge, table)
+    table = jnp.where(tile == 6, pltpu.roll(edge, 124, 1), table)
     coef = [jnp.broadcast_to(table[:, d : d + 1], (8, 128)) for d in range(4)]
-    total = total_of([rows[5 * p : 5 * p + 4] for p in range(n_event)])
+    total = total[:4]
     x = jnp.concatenate([total, pltpu.roll(total, 64, 1)], axis=0)
     for _ in range(2):
         right = jnp.where(tile < 7, pltpu.roll(x, 7, 0), 0.0)
@@ -351,18 +364,23 @@
     mesh_group = [(i + first_mesh) % n_mesh for i in range(n_mesh)]
     event_group = [(i + first_event) % n_event for i in range(n_event)]
 
-    inputs = (
-        stiffness, neighbours.reshape(FACES, 1, 128), material, smoothing, projection.T, destinations, forward, adjoint
-    )
-    held = tuple(shape(*x.shape, dtype=x.dtype) for x in inputs)
-    inputs = tuple(pltpu.with_memory_space_constraint(x, pltpu.HBM) for x in inputs)
-    rim, fields, *small = call(
-        pack_kernel, (shape(200, 128), shape(6, 128, 128)) + held, 1, 0, 8, [pltpu.SemaphoreType.DMA((8,))]
-    )(counts, *inputs)
-    small = small[:6]
-    near, material = small[1], small[2]
+    near, project = neighbours.reshape(FACES, 1, 128), projection.T
+    inputs = (forward, adjoint, smoothing, near, stiffness, material, project, destinations)
+    inputs = [pltpu.with_memory_space_constraint(x, pltpu.HBM) for x in inputs]
+    rim, fields, smooth_in = call(
+        pack_kernel,
+        (shape(200, 128), shape(6, 128, 128), shape(4, tile_width)),
+        1,
+        0,
+        3,
+        [pltpu.VMEM(x.shape, F32) for x in (forward, adjoint)] + [pltpu.SemaphoreType.DMA((3,))],
+    )(counts, *inputs[:3])
+    cores = min(n_event, 2)
+    planes, event = n_event // cores, lax.axis_index("event")
+    is_near = (event < cores * (planes // 4 + 1)) | (event >= cores * (planes - planes // 4))
+    is_near, rim = lax.optimization_barrier((is_near, rim))
     before, after = lax.ppermute(rim, "mesh", up), lax.ppermute(rim, "mesh", down)
-    partial, kernel, turned, stiff, pick, lift, project, wanted = call(
+    partial, kernel, turned, stiff, pick, lift, project, wanted, near, material = call(
         own_kernel,
         (
             shape(6, 128, 128),
@@ -373,10 +391,14 @@
             shape(128, FACES * SHEET, dtype=BF16),
             shape(2, 64, 128, dtype=BF16),
             shape(8, 128),
+            shape(FACES, 1, 128, dtype=I32),
+            shape(1, 128),
         ),
         2,
-        7,
-    )(counts, place, fields, *small)
+        2,
+        5,
+        [pltpu.VMEM(x.shape, x.dtype) for x in (stiffness, project, destinations)] + [pltpu.SemaphoreType.DMA((5,))],
+    )(counts, place, fields, smooth_in, *inputs[3:])
 
     def one_step(*refs):
         step_kernel(scale, n_mesh, *refs)
@@ -388,21 +410,28 @@
         10,
     )(counts, place, partial, kernel, before, after, near, stiff, pick, lift, project, wanted)
     parts = lax.all_to_all(chunk, "mesh", 0, 0, tiled=True, axis_index_groups=[mesh_group])
-    before, after = lax.ppermute(rim_one, "mesh", up), lax.ppermute(rim_one, "mesh", down)
+
+    def last(rim_one, *rest):
+        before, after = lax.ppermute(rim_one, "mesh", up), lax.ppermute(rim_one, "mesh", down)
+        return call(last_kernel, shape(3, NODES, 1, 128), 2, 9)(
+            counts, place, fields, one, strain, before, after, near, material, pick, lift
+        )
+
+    rim_one, parts, is_near = lax.optimization_barrier((rim_one, parts, is_near))
+    final = lax.cond(is_near, last, lambda rim_one: jnp.zeros((3, NODES, 1, 128), F32), rim_one)
 
     def dense(*refs):
         dense_kernel(n_event, n_mesh, tile_width, first_event, *refs)
 
-    partial = call(dense, shape(5 * n_event, 1, 128), 1, 4)(place, parts, edge, before, after)
+    partial = call(dense, shape(5 * n_event, 1, 128), 1, 3)(place, parts, edge, final)
     pieces = lax.all_to_all(partial, "event", 0, 0, tiled=True, axis_index_groups=[event_group])
-    final, table = call(last_kernel, (shape(3, NODES, 1, 128), shape(8, 128)), 2, 11)(
-        counts, place, fields, one, strain, before, after, near, material, turned, edge, pick, lift
-    )
+    rim_one, final, _ = lax.optimization_barrier((rim_one, final, partial))
+    final = lax.cond(is_near, lambda rim_one, final: final, last, rim_one, final)
 
     def smooth(*refs):
-        smooth_kernel(n_event, first_event, *refs)
-
-    tiles = call(smooth, shape(tile_width, 64), 1, 2)(place, pieces, table)
+        smooth_kernel(n_event, *refs)
+
+    tiles = call(smooth, shape(tile_width, 64), 1, 3)(place, pieces, turned, edge)
     return final.reshape(1, 3, NODES, 128), tiles.T
 
 

time: 70.9 us -> 81.6 us (1.15)
  waiting for transfers between devices: 13.7 us -> 21.1 us
  starting transfers between devices: 44.3 us -> 47.4 us
    all_to_all x1, waiting for transfers between devices: 0.01 us -> 5.09 us  [per_device(): lax.all_to_all(chunk, 'mesh', 0, 0, tiled=True, axis_index_groups=[mesh_g...]
    ppermute x2, starting transfers between devices: 5.27 us -> 7.59 us  [the longest x1 5.67 us: last(): lax.ppermute(rim_one, 'mesh', down)]
    all_to_all x1, waiting for transfers between devices: 3.06 us -> 4.99 us  [per_device(): lax.all_to_all(partial, 'event', 0, 0, tiled=True, axis_index_groups=[eve...]
    ppermute x2, waiting for transfers between devices: 5.23 us -> 6.39 us  [the longest x1 6.39 us: last(): lax.ppermute(rim_one, 'mesh', up)]
  transfers between devices with their start and end apart: 6 -> 6, of which waited for: 4 -> 4; matrix products, arithmetic and copies ran while one was open for 0% -> 0% of each run, Pallas kernels for 5% -> 3%
where the time goes in v5:
time: 81.6 us; the launch traced here: 81.2 us
  starting transfers between devices  47.4 us (58%)
  waiting for transfers between devices  21.1 us (26%)
  Pallas kernels  11.2 us (14%)
  between operations  1.36 us (2%)
    all_to_all x1, starting transfers between devices, per_device(): lax.all_to_all(partial, 'event', 0, 0, tiled=True, axis_index_groups=[eve...  23.6 us
    ppermute x1, starting transfers between devices, per_device(): lax.ppermute(rim, 'mesh', down)  7.67 us
    all_to_all x1, starting transfers between devices, per_device(): lax.all_to_all(chunk, 'mesh', 0, 0, tiled=True, axis_index_groups=[mesh_g...  6.66 us
    ppermute x1, waiting for transfers between devices, last(): lax.ppermute(rim_one, 'mesh', up)  6.39 us
    ppermute x1, starting transfers between devices, last(): lax.ppermute(rim_one, 'mesh', down)  5.67 us
    all_to_all x1, waiting for transfers between devices, per_device(): lax.all_to_all(chunk, 'mesh', 0, 0, tiled=True, axis_index_groups=[mesh_g...  5.09 us
    all_to_all x1, waiting for transfers between devices, per_device(): lax.all_to_all(partial, 'event', 0, 0, tiled=True, axis_index_groups=[eve...  4.99 us
    ppermute x1, waiting for transfers between devices, per_device(): lax.ppermute(rim, 'mesh', up)  4.65 us
  transfers between devices with their start and end apart: 6, of which 4 were waited for; matrix products, arithmetic and copies ran while one was open for 0% of the time, Pallas kernels for 3%

profile of v5, /device:TPU:1, one launch (start us, length us, event | category | flops | bytes accessed | tf_op | source)
XLA Modules:
  0.0 81.2 jit_solution(13950117050912276966)
XLA Ops:
  1.3 1.3 %shard_map.104 = (f32[200,128]{1,0:T(8,128)S(1)}, f32[6,128,128]{2,1,0:T(8,128)S(1)}, f32[4,4]{1,0:T(4,128)S(1)}) custom-call(s32[1,1]{1,0:T(1,128)S(6)} %copy.16.count_ref.refs_0_, f32[3,125,1,128]{3,2,1,0:T(1,128)} %bitcast.11, f32[3,125,1,128]{3,2,1,0:T(1,128)} %bitcast.12, f32[4,4]{1,0:T(4,128)} %smooth_ref.1), custom_call_target="tpu_custom_call" | custom-call | tf_op jit(solution)/shard_map/pallas_call | solution.py:370
  2.6 7.7 %collective-permute-start.5 = (f32[200,128]{1,0:T(8,128)S(1)}, f32[200,128]{1,0:T(8,128)S(1)}, u32[]{:S(2)}, u32[]{:S(2)}) collective-permute-start(f32[200,128]{1,0:T(8,128)S(1)} %get-tuple-element.101), channel_id=1, source_target_pairs={{1,0},{2,1},{3,2},{4,3},{5,4},{6,5},{7,6},{8,7},{9,8},{10,9},{11,1... | collective-permute-start | bytes 307208 | tf_op jit(solution)/shard_map/ppermute | solution.py:382
  10.2 1.9 %collective-permute-start.4 = (f32[200,128]{1,0:T(8,128)S(1)}, f32[200,128]{1,0:T(8,128)S(1)}, u32[]{:S(2)}, u32[]{:S(2)}) collective-permute-start(f32[200,128]{1,0:T(8,128)S(1)} %get-tuple-element.101), channel_id=1, source_target_pairs={{0,1},{1,2},{2,3},{3,4},{4,5},{5,6},{6,7},{7,8},{8,9},{9,10},{10,1... | collective-permute-start | bytes 307208 | tf_op jit(solution)/shard_map/ppermute | solution.py:382
  12.2 0.1 pad_add_fusion.place_ref.refs_1_.refs_0_
  12.3 2.0 %shard_map.105 = (f32[6,128,128]{2,1,0:T(8,128)S(1)}, f32[128,128]{1,0:T(8,128)S(1)}, f32[8,128]{1,0:T(8,128)S(1)}, bf16[2,128,128]{2,1,0:T(8,128)(2,1)S(1)}, bf...) custom-call(s32[1,1]{1,0:T(1,128)S(6)} %copy.16.count_ref.refs_0_, ...), custom_call_target="tpu_custom_call" | custom-call | tf_op jit(solution)/shard_map/pallas_call | solution.py:383
  14.3 0.0 collective-permute-done.5.refs_5_
  14.3 4.6 %collective-permute-done.4.refs_4_ = f32[200,128]{1,0:T(8,128)S(1)} collective-permute-done((f32[200,128]{1,0:T(8,128)S(1)}, f32[200,128]{1,0:T(8,128)S(1)}, u32[]{:S(2)}, u32[]{:S(2)}) %collective-permute-start.4) | collective-permute-done | bytes 102432 | tf_op jit(solution)/shard_map/ppermute | solution.py:382
  19.0 2.8 %shard_map.106 = (f32[3,128,128]{2,1,0:T(8,128)S(1)}, f32[3,128,128]{2,1,0:T(8,128)S(1)}, f32[128,128]{1,0:T(8,128)S(1)}, f32[8,128]{1,0:T(8,128)S(1)}, f32[16,72,128]{2,1,0:T(8,128)}) custom-call(s32[1,1]{1,0:T(1,128)S(6)} %copy.16.count_ref.refs_0_, s32[3]{0:T(128)S(1)} %pad_add_fusion.place_ref.refs_1_.refs_0_, ...), custom_call_target="tpu_custom_call" | custom-call | tf_op jit(solution)/shard_map/pallas_call | solution.py:406
  21.7 6.7 %all-to-all-start = ((f32[16,72,128]{2,1,0:T(8,128)}), f32[16,72,128]{2,1,0:T(8,128)S(1)}, u32[]{:S(2)}, u32[]{:S(2)}) async-start(f32[16,72,128]{2,1,0:T(8,128)} %get-tuple-element.109), calls=%async_computation | async-start | bytes 1179648 | tf_op jit(solution)/shard_map/all_to_all | solution.py:412
  28.4 5.1 %all-to-all-done.refs_1_ = f32[16,72,128]{2,1,0:T(8,128)S(1)} async-done(((f32[16,72,128]{2,1,0:T(8,128)}), f32[16,72,128]{2,1,0:T(8,128)S(1)}, u32[]{:S(2)}, u32[]{:S(2)}) %all-to-all-start) | async-done | bytes 589856 | tf_op jit(solution)/shard_map/all_to_all | solution.py:412
  33.5 15.9 %conditional.2 = (f32[3,125,1,128]{3,2,1,0:T(1,128)S(1)}) conditional(s32[]{:T(128)} %convert_element_type.4, () %tuple.27, (f32[128,128]{1,0:T(8,128)S(1)}, s32[1,1]{1,0:T(1,128)}, s32[3]{0:T(128)S(1)}, f32[6,128,128]{2,1,0:T(8,128)S(1)}, f32[3,128,128]{2,1,0:T(8,128)S(1)}, /*index=5*/f32[3,128,128]{2,1,0:T(8,128)S(1)}, s32[6,1,128]{2,1,0:T(1,128)S(1)}, ...), branch_computations={%region_0.0_spmd, %region_1.0_spmd} | conditional | bytes 524376 | solution.py:421
  33.5 5.7 %collective-permute-start.1 = (f32[128,128]{1,0:T(8,128)S(1)}, f32[128,128]{1,0:T(8,128)S(1)}, u32[]{:S(2)}, u32[]{:S(2)}) collective-permute-start(f32[128,128]{1,0:T(8,128)S(1)} %get-tuple-element.54), channel_id=1, source_target_pairs={{1,0},{2,1},{3,2},{4,3},{5,4},{6,5},{7,6},{8,7},{9,8},{10,9},{11,1... | collective-permute-start | bytes 196616 | tf_op jit(solution)/shard_map/cond/branch_1_fun/ppermute | solution.py:415
  39.2 1.9 %collective-permute-start = (f32[128,128]{1,0:T(8,128)S(1)}, f32[128,128]{1,0:T(8,128)S(1)}, u32[]{:S(2)}, u32[]{:S(2)}) collective-permute-start(f32[128,128]{1,0:T(8,128)S(1)} %get-tuple-element.54), channel_id=1, source_target_pairs={{0,1},{1,2},{2,3},{3,4},{4,5},{5,6},{6,7},{7,8},{8,9},{9,10},{10,1... | collective-permute-start | bytes 196616 | tf_op jit(solution)/shard_map/cond/branch_1_fun/ppermute | solution.py:415
  41.1 0.0 collective-permute-done.1.after_ref
  41.1 6.4 %collective-permute-done.before_ref = f32[128,128]{1,0:T(8,128)S(1)} collective-permute-done((f32[128,128]{1,0:T(8,128)S(1)}, f32[128,128]{1,0:T(8,128)S(1)}, u32[]{:S(2)}, u32[]{:S(2)}) %collective-permute-start) | collective-permute-done | bytes 65568 | tf_op jit(solution)/shard_map/cond/branch_1_fun/ppermute | solution.py:415
  47.5 1.9 %branch_1_fun.1 = f32[3,125,1,128]{3,2,1,0:T(1,128)S(1)} custom-call(s32[1,1]{1,0:T(1,128)} %get-tuple-element.49.count_ref, s32[3]{0:T(128)S(1)} %get-tuple-element.50.place_ref, f32[6,128,128]{2,1,0:T(8,128)S(1)} %get-tuple-element.51.field_ref, f32[3,128,128]{2,1,0:T(8,128)S(1)} %get-tuple-element.52.one_ref, ...), custom_call_target="tpu_custom_call" | custom-call | tf_op jit(solution)/shard_map/cond/branch_1_fun/pallas_call | solution.py:416
  49.4 1.8 %shard_map.107 = f32[160,1,128]{2,1,0:T(1,128)} custom-call(s32[3]{0:T(128)S(1)} %pad_add_fusion.place_ref.refs_1_.refs_0_, f32[16,72,128]{2,1,0:T(8,128)S(1)} %all-to-all-done.refs_1_, f32[8,128]{1,0:T(8,128)S(1)} %get-tuple-element.117.refs_2_.refs_3_, f32[3,125,1,128]{3,2,1,0:T(1,128)S(1)} %get-tuple-element.121.refs_3_), custom_call_target="tpu_custom_call" | custom-call | tf_op jit(solution)/shard_map/pallas_call | solution.py:426
  51.2 23.6 %all-to-all-start.1 = ((f32[160,1,128]{2,1,0:T(1,128)}), f32[160,1,128]{2,1,0:T(1,128)S(1)}, u32[]{:S(2)}, u32[]{:S(2)}) async-start(f32[160,1,128]{2,1,0:T(1,128)} %shard_map.107), calls=%async_computation.1 | async-start | bytes 163840 | tf_op jit(solution)/shard_map/all_to_all | solution.py:427
  74.8 0.0 copy-start
  74.8 5.0 %all-to-all-done.1.refs_1_ = f32[160,1,128]{2,1,0:T(1,128)S(1)} async-done(((f32[160,1,128]{2,1,0:T(1,128)}), f32[160,1,128]{2,1,0:T(1,128)S(1)}, u32[]{:S(2)}, u32[]{:S(2)}) %all-to-all-start.1) | async-done | bytes 81952 | tf_op jit(solution)/shard_map/all_to_all | solution.py:427
  79.8 1.4 %shard_map.108 = f32[4,64]{1,0:T(4,128)} custom-call(s32[3]{0:T(128)S(1)} %pad_add_fusion.place_ref.refs_1_.refs_0_, f32[160,1,128]{2,1,0:T(1,128)S(1)} %all-to-all-done.1.refs_1_, f32[8,128]{1,0:T(8,128)S(1)} %get-tuple-element.120.refs_2_, f32[8,128]{1,0:T(8,128)S(1)} %get-tuple-element.117.refs_2_.refs_3_), custom_call_target="tpu_custom_call" | custom-call | tf_op jit(solution)/shard_map/pallas_call | solution.py:434
  81.2 0.0 copy-done
  (1 shorter events, 0.0 us)
Async XLA Ops:
  2.6 11.7 %collective-permute-start.5 = (f32[200,128]{1,0:T(8,128)S(1)}, f32[200,128]{1,0:T(8,128)S(1)}, u32[]{:S(2)}, u32[]{:S(2)}) collective-permute-start(f32[200,128]{1,0:T(8,128)S(1)} %get-tuple-element.101), channel_id=1, source_target_pairs={{1,0},{2,1},{3,2},{4,3},{5,4},{6,5},{7,6},{8,7},{9,8},{10,9},{11,1... | collective-permute-start | bytes 307208 | tf_op jit(solution)/shard_map/ppermute | solution.py:382
  10.2 8.7 %collective-permute-start.4 = (f32[200,128]{1,0:T(8,128)S(1)}, f32[200,128]{1,0:T(8,128)S(1)}, u32[]{:S(2)}, u32[]{:S(2)}) collective-permute-start(f32[200,128]{1,0:T(8,128)S(1)} %get-tuple-element.101), channel_id=1, source_target_pairs={{0,1},{1,2},{2,3},{3,4},{4,5},{5,6},{6,7},{7,8},{8,9},{9,10},{10,1... | collective-permute-start | bytes 307208 | tf_op jit(solution)/shard_map/ppermute | solution.py:382
  21.7 11.8 %all-to-all-start = ((f32[16,72,128]{2,1,0:T(8,128)}), f32[16,72,128]{2,1,0:T(8,128)S(1)}, u32[]{:S(2)}, u32[]{:S(2)}) async-start(f32[16,72,128]{2,1,0:T(8,128)} %get-tuple-element.109), calls=%async_computation | async-start | bytes 1179648 | tf_op jit(solution)/shard_map/all_to_all | solution.py:412
  33.5 7.6 %collective-permute-start.1 = (f32[128,128]{1,0:T(8,128)S(1)}, f32[128,128]{1,0:T(8,128)S(1)}, u32[]{:S(2)}, u32[]{:S(2)}) collective-permute-start(f32[128,128]{1,0:T(8,128)S(1)} %get-tuple-element.54), channel_id=1, source_target_pairs={{1,0},{2,1},{3,2},{4,3},{5,4},{6,5},{7,6},{8,7},{9,8},{10,9},{11,1... | collective-permute-start | bytes 196616 | tf_op jit(solution)/shard_map/cond/branch_1_fun/ppermute | solution.py:415
  39.2 8.3 %collective-permute-start = (f32[128,128]{1,0:T(8,128)S(1)}, f32[128,128]{1,0:T(8,128)S(1)}, u32[]{:S(2)}, u32[]{:S(2)}) collective-permute-start(f32[128,128]{1,0:T(8,128)S(1)} %get-tuple-element.54), channel_id=1, source_target_pairs={{0,1},{1,2},{2,3},{3,4},{4,5},{5,6},{6,7},{7,8},{8,9},{9,10},{10,1... | collective-permute-start | bytes 196616 | tf_op jit(solution)/shard_map/cond/branch_1_fun/ppermute | solution.py:415
  51.2 28.6 %all-to-all-start.1 = ((f32[160,1,128]{2,1,0:T(1,128)}), f32[160,1,128]{2,1,0:T(1,128)S(1)}, u32[]{:S(2)}, u32[]{:S(2)}) async-start(f32[160,1,128]{2,1,0:T(1,128)} %shard_map.107), calls=%async_computation.1 | async-start | bytes 163840 | tf_op jit(solution)/shard_map/all_to_all | solution.py:427
  74.8 6.4 %copy-start = (f32[1,3,125,128]{3,0,2,1:T(1,128)}, f32[1,3,125,128]{3,0,2,1:T(1,128)S(1)}, u32[]{:S(2)}) copy-start(f32[1,3,125,128]{3,0,2,1:T(1,128)S(1)} %get-tuple-element.122) | copy-start | bytes 576004

commit v6 on v5

--- a/solution.py
+++ b/solution.py
@@ -256,7 +256,7 @@
         strain_ref[c] = strain[c]
 
 
-def dense_kernel(n_event, n_mesh, tile_width, first, place_ref, parts_ref, edge_ref, final_ref, out_ref):
+def dense_kernel(n_event, n_mesh, tile_width, first, place_ref, parts_ref, edge_ref, out_ref):
     rows = 4 * n_event
     row = iota((2 * rows, 128), 0)
     within = row % rows
@@ -314,7 +314,9 @@
     rows = flat_of(x_ref)
     mine, parts = place_ref[0], place_ref[1]
     node, tile = iota((8, 128), 1), iota((8, 128), 0)
-    total = total_of([rows[5 * p : 5 * p + 5] for p in range(n_event)])
+    span = 40 if n_event % 8 == 0 else 5 * n_event
+    total = total_of([rows[i : i + span] for i in range(0, 5 * n_event, span)])
+    total = total_of([total[i : i + 5] for i in range(0, span, 5)])
     lane = iota((1, 128), 1)
     beside = ((lane < 4) & (mine > 0)) | ((lane >= 4) & (mine < parts - 1))
     edge = jnp.broadcast_to(jnp.where(beside, edge_ref[0:1], total[4:5]), (8, 128))
@@ -376,8 +378,8 @@
         [pltpu.VMEM(x.shape, F32) for x in (forward, adjoint)] + [pltpu.SemaphoreType.DMA((3,))],
     )(counts, *inputs[:3])
     cores = min(n_event, 2)
-    planes, event = n_event // cores, lax.axis_index("event")
-    is_near = (event < cores * (planes // 4 + 1)) | (event >= cores * (planes - planes // 4))
+    event = lax.axis_index("event")
+    is_near = event < cores
     is_near, rim = lax.optimization_barrier((is_near, rim))
     before, after = lax.ppermute(rim, "mesh", up), lax.ppermute(rim, "mesh", down)
     partial, kernel, turned, stiff, pick, lift, project, wanted, near, material = call(
@@ -409,24 +411,24 @@
         2,
         10,
     )(counts, place, partial, kernel, before, after, near, stiff, pick, lift, project, wanted)
+    def halo(rim_one, *_):
+        return lax.ppermute(rim_one, "mesh", up), lax.ppermute(rim_one, "mesh", down)
+
+    none = jnp.zeros((128, 128), F32)
+    sides = lax.cond(is_near, halo, lambda rim_one: (none, none), rim_one)
+    chunk, sides = lax.optimization_barrier((chunk, sides))
     parts = lax.all_to_all(chunk, "mesh", 0, 0, tiled=True, axis_index_groups=[mesh_group])
-
-    def last(rim_one, *rest):
-        before, after = lax.ppermute(rim_one, "mesh", up), lax.ppermute(rim_one, "mesh", down)
-        return call(last_kernel, shape(3, NODES, 1, 128), 2, 9)(
-            counts, place, fields, one, strain, before, after, near, material, pick, lift
-        )
-
-    rim_one, parts, is_near = lax.optimization_barrier((rim_one, parts, is_near))
-    final = lax.cond(is_near, last, lambda rim_one: jnp.zeros((3, NODES, 1, 128), F32), rim_one)
 
     def dense(*refs):
         dense_kernel(n_event, n_mesh, tile_width, first_event, *refs)
 
-    partial = call(dense, shape(5 * n_event, 1, 128), 1, 3)(place, parts, edge, final)
+    partial = call(dense, shape(5 * n_event, 1, 128), 1, 2)(place, parts, edge)
     pieces = lax.all_to_all(partial, "event", 0, 0, tiled=True, axis_index_groups=[event_group])
-    rim_one, final, _ = lax.optimization_barrier((rim_one, final, partial))
-    final = lax.cond(is_near, lambda rim_one, final: final, last, rim_one, final)
+    rim_one, is_near, _ = lax.optimization_barrier((rim_one, is_near, partial))
+    before, after = lax.cond(is_near, lambda rim_one, sides: sides, halo, rim_one, sides)
+    final = call(last_kernel, shape(3, NODES, 1, 128), 2, 9)(
+        counts, place, fields, one, strain, before, after, near, material, pick, lift
+    )
 
     def smooth(*refs):
         smooth_kernel(n_event, *refs)

time: 81.6 us -> 76.3 us (0.935)
  the two profiles are of different devices: /device:TPU:1 before, /device:TPU:62 now
where the time goes in v6:
time: 76.3 us; the launch traced here: 75.8 us
  starting transfers between devices  38.4 us (50%)
  blocking collectives  13.5 us (18%)
  waiting for transfers between devices  10.7 us (14%)
  Pallas kernels  10.4 us (14%)
  between operations  1.35 us (2%)
  local copies, waits for them, and re-layouts  1.26 us (2%)
    all_to_all x1, starting transfers between devices, per_device(): lax.all_to_all(partial, 'event', 0, 0, tiled=True, axis_index_groups=[eve...  26.7 us
    all_to_all x1, blocking collectives, per_device(): lax.all_to_all(chunk, 'mesh', 0, 0, tiled=True, axis_index_groups=[mesh_g...  13.5 us
    ppermute x1, waiting for transfers between devices, halo(): lax.ppermute(rim_one, 'mesh', down)  6.5 us
    ppermute x1, waiting for transfers between devices, per_device(): lax.ppermute(rim, 'mesh', down)  3.92 us
    ppermute x1, starting transfers between devices, per_device(): lax.ppermute(rim, 'mesh', down)  3.8 us
    ppermute x1, starting transfers between devices, halo(): lax.ppermute(rim_one, 'mesh', up)  3.17 us
    ppermute x1, starting transfers between devices, halo(): lax.ppermute(rim_one, 'mesh', down)  2.67 us
    pallas_call x1, Pallas kernels, per_device(): call(own_kernel, (shape(6, 128, 128), shape(128, 128), shape(8, 128), sha...  2.05 us
  transfers between devices with their start and end apart: 5, of which 3 were waited for; matrix products, arithmetic and copies ran while one was open for 0% of the time, Pallas kernels for 5%

profile of v6, /device:TPU:62, one launch (start us, length us, event | category | flops | bytes accessed | tf_op | source)
XLA Modules:
  0.0 75.8 jit_solution(13615060162779131778)
XLA Ops:
  1.3 1.3 %shard_map.104 = (f32[200,128]{1,0:T(8,128)S(1)}, f32[6,128,128]{2,1,0:T(8,128)S(1)}, f32[4,4]{1,0:T(4,128)S(1)}) custom-call(s32[1,1]{1,0:T(1,128)S(6)} %copy.19.count_ref.refs_0_, f32[3,125,1,128]{3,2,1,0:T(1,128)} %bitcast.9, f32[3,125,1,128]{3,2,1,0:T(1,128)} %bitcast.10, f32[4,4]{1,0:T(4,128)} %smooth_ref.1), custom_call_target="tpu_custom_call" | custom-call | tf_op jit(solution)/shard_map/pallas_call | solution.py:372
  2.6 2.0 %collective-permute-start.4 = (f32[200,128]{1,0:T(8,128)S(1)}, f32[200,128]{1,0:T(8,128)S(1)}, u32[]{:S(2)}, u32[]{:S(2)}) collective-permute-start(f32[200,128]{1,0:T(8,128)S(1)} %get-tuple-element.42), channel_id=1, source_target_pairs={{0,1},{1,2},{2,3},{3,4},{4,5},{5,6},{6,7},{7,8},{8,9},{9,10},{10,1... | collective-permute-start | bytes 307208 | tf_op jit(solution)/shard_map/ppermute | solution.py:384
  4.6 3.8 %collective-permute-start.5 = (f32[200,128]{1,0:T(8,128)S(1)}, f32[200,128]{1,0:T(8,128)S(1)}, u32[]{:S(2)}, u32[]{:S(2)}) collective-permute-start(f32[200,128]{1,0:T(8,128)S(1)} %get-tuple-element.42), channel_id=1, source_target_pairs={{1,0},{2,1},{3,2},{4,3},{5,4},{6,5},{7,6},{8,7},{9,8},{10,9},{11,1... | collective-permute-start | bytes 307208 | tf_op jit(solution)/shard_map/ppermute | solution.py:384
  8.4 0.1 pad_add_fusion.place_ref.refs_1_.refs_0_
  8.5 2.0 %shard_map.105 = (f32[6,128,128]{2,1,0:T(8,128)S(1)}, f32[128,128]{1,0:T(8,128)S(1)}, f32[8,128]{1,0:T(8,128)S(1)}, bf16[2,128,128]{2,1,0:T(8,128)(2,1)S(1)}, bf...) custom-call(s32[1,1]{1,0:T(1,128)S(6)} %copy.19.count_ref.refs_0_, ...), custom_call_target="tpu_custom_call" | custom-call | tf_op jit(solution)/shard_map/pallas_call | solution.py:385
  10.6 0.0 collective-permute-done.4.refs_4_
  10.6 3.9 %collective-permute-done.5.refs_5_ = f32[200,128]{1,0:T(8,128)S(1)} collective-permute-done((f32[200,128]{1,0:T(8,128)S(1)}, f32[200,128]{1,0:T(8,128)S(1)}, u32[]{:S(2)}, u32[]{:S(2)}) %collective-permute-start.5) | collective-permute-done | bytes 102432 | tf_op jit(solution)/shard_map/ppermute | solution.py:384
  14.5 1.9 %shard_map.106 = (f32[3,128,128]{2,1,0:T(8,128)S(1)}, f32[3,128,128]{2,1,0:T(8,128)S(1)}, f32[128,128]{1,0:T(8,128)S(1)}, f32[8,128]{1,0:T(8,128)S(1)}, f32[16,72,128]{2,1,0:T(8,128)S(1)}) custom-call(s32[1,1]{1,0:T(1,128)S(6)} %copy.19.count_ref.refs_0_, s32[3]{0:T(128)S(1)} %pad_add_fusion.place_ref.refs_1_.refs_0_, ...), custom_call_target="tpu_custom_call" | custom-call | tf_op jit(solution)/shard_map/pallas_call | solution.py:408
  16.4 1.3 %conditional.2 = (f32[128,128]{1,0:T(8,128)}, f32[128,128]{1,0:T(8,128)}) conditional(s32[]{:T(128)} %convert_element_type.6, () %tuple.27, f32[128,128]{1,0:T(8,128)S(1)} %get-tuple-element.59), branch_computations={%region_0.0_spmd, %region_1.0_spmd} | conditional | bytes 524384 | solution.py:418
  16.4 0.6 broadcast_in_dim.2
  17.1 0.6 broadcast_in_dim.2.clone
  17.7 13.5 %all_to_all.10.refs_1_ = f32[16,72,128]{2,1,0:T(8,128)S(1)} all-to-all(f32[16,72,128]{2,1,0:T(8,128)S(1)} %get-tuple-element.56), channel_id=1, replica_groups={{10,11,12,13,14,15,0,1,2,3,4,5,6,7,8,9},{26,27,28,29,30,31,16,17,18,19,..., dimensions={0} | all-to-all | bytes 1179648 | tf_op jit(solution)/shard_map/all_to_all | solution.py:420
  31.3 1.8 %shard_map.107 = f32[160,1,128]{2,1,0:T(1,128)} custom-call(s32[3]{0:T(128)S(1)} %pad_add_fusion.place_ref.refs_1_.refs_0_, f32[16,72,128]{2,1,0:T(8,128)S(1)} %all_to_all.10.refs_1_, f32[8,128]{1,0:T(8,128)S(1)} %get-tuple-element.57.refs_2_.refs_3_), custom_call_target="tpu_custom_call" | custom-call | tf_op jit(solution)/shard_map/pallas_call | solution.py:425
  33.1 26.7 %all-to-all-start.1 = ((f32[160,1,128]{2,1,0:T(1,128)}), f32[160,1,128]{2,1,0:T(1,128)S(1)}, u32[]{:S(2)}, u32[]{:S(2)}) async-start(f32[160,1,128]{2,1,0:T(1,128)} %shard_map.107), calls=%async_computation.1 | async-start | bytes 163840 | tf_op jit(solution)/shard_map/all_to_all | solution.py:426
  59.8 12.7 %conditional.3 = (f32[128,128]{1,0:T(8,128)S(1)}, f32[128,128]{1,0:T(8,128)S(1)}) conditional(s32[]{:T(128)} %convert_element_type.7, f32[128,128]{1,0:T(8,128)S(1)} %get-tuple-element.59, (f32[128,128]{1,0:T(8,128)}, f32[128,128]{1,0:T(8,128)}) %conditional.2), branch_computations={%region_2.0_spmd, %region_3.0_spmd} | conditional | bytes 524384 | solution.py:428
  59.8 3.2 %collective-permute-start.2 = (f32[128,128]{1,0:T(8,128)S(1)}, f32[128,128]{1,0:T(8,128)S(1)}, u32[]{:S(2)}, u32[]{:S(2)}) collective-permute-start(f32[128,128]{1,0:T(8,128)S(1)} %param.2), channel_id=1, source_target_pairs={{0,1},{1,2},{2,3},{3,4},{4,5},{5,6},{6,7},{7,8},{8,9},{9,10},{10,1... | collective-permute-start | bytes 196616 | tf_op jit(solution)/shard_map/cond/branch_0_fun/ppermute | solution.py:415
  63.0 2.7 %collective-permute-start.3 = (f32[128,128]{1,0:T(8,128)S(1)}, f32[128,128]{1,0:T(8,128)S(1)}, u32[]{:S(2)}, u32[]{:S(2)}) collective-permute-start(f32[128,128]{1,0:T(8,128)S(1)} %param.2), channel_id=1, source_target_pairs={{1,0},{2,1},{3,2},{4,3},{5,4},{6,5},{7,6},{8,7},{9,8},{10,9},{11,1... | collective-permute-start | bytes 196616 | tf_op jit(solution)/shard_map/cond/branch_0_fun/ppermute | solution.py:415
  65.7 0.3 collective-permute-done.2
  66.0 6.5 %collective-permute-done.3 = f32[128,128]{1,0:T(8,128)S(1)} collective-permute-done((f32[128,128]{1,0:T(8,128)S(1)}, f32[128,128]{1,0:T(8,128)S(1)}, u32[]{:S(2)}, u32[]{:S(2)}) %collective-permute-start.3) | collective-permute-done | bytes 65568 | tf_op jit(solution)/shard_map/cond/branch_0_fun/ppermute | solution.py:415
  72.5 2.0 %shard_map.108 = f32[3,125,1,128]{3,2,1,0:T(1,128)} custom-call(s32[1,1]{1,0:T(1,128)S(6)} %copy.19.count_ref.refs_0_, s32[3]{0:T(128)S(1)} %pad_add_fusion.place_ref.refs_1_.refs_0_, f32[6,128,128]{2,1,0:T(8,128)S(1)} %get-tuple-element.37.field_ref, f32[3,128,128]{2,1,0:T(8,128)S(1)} %get-tuple-element.49.one_ref, ...), custom_call_target="tpu_custom_call" | custom-call | tf_op jit(solution)/shard_map/pallas_call | solution.py:429
  74.4 0.0 all-to-all-done.1.refs_1_
  74.4 1.4 %shard_map.109 = f32[4,64]{1,0:T(4,128)} custom-call(s32[3]{0:T(128)S(1)} %pad_add_fusion.place_ref.refs_1_.refs_0_, f32[160,1,128]{2,1,0:T(1,128)S(1)} %all-to-all-done.1.refs_1_, f32[8,128]{1,0:T(8,128)S(1)} %get-tuple-element.65.refs_2_, f32[8,128]{1,0:T(8,128)S(1)} %get-tuple-element.57.refs_2_.refs_3_), custom_call_target="tpu_custom_call" | custom-call | tf_op jit(solution)/shard_map/pallas_call | solution.py:436
Async XLA Ops:
  2.6 8.0 %collective-permute-start.4 = (f32[200,128]{1,0:T(8,128)S(1)}, f32[200,128]{1,0:T(8,128)S(1)}, u32[]{:S(2)}, u32[]{:S(2)}) collective-permute-start(f32[200,128]{1,0:T(8,128)S(1)} %get-tuple-element.42), channel_id=1, source_target_pairs={{0,1},{1,2},{2,3},{3,4},{4,5},{5,6},{6,7},{7,8},{8,9},{9,10},{10,1... | collective-permute-start | bytes 307208 | tf_op jit(solution)/shard_map/ppermute | solution.py:384
  4.6 9.9 %collective-permute-start.5 = (f32[200,128]{1,0:T(8,128)S(1)}, f32[200,128]{1,0:T(8,128)S(1)}, u32[]{:S(2)}, u32[]{:S(2)}) collective-permute-start(f32[200,128]{1,0:T(8,128)S(1)} %get-tuple-element.42), channel_id=1, source_target_pairs={{1,0},{2,1},{3,2},{4,3},{5,4},{6,5},{7,6},{8,7},{9,8},{10,9},{11,1... | collective-permute-start | bytes 307208 | tf_op jit(solution)/shard_map/ppermute | solution.py:384
  33.1 41.4 %all-to-all-start.1 = ((f32[160,1,128]{2,1,0:T(1,128)}), f32[160,1,128]{2,1,0:T(1,128)S(1)}, u32[]{:S(2)}, u32[]{:S(2)}) async-start(f32[160,1,128]{2,1,0:T(1,128)} %shard_map.107), calls=%async_computation.1 | async-start | bytes 163840 | tf_op jit(solution)/shard_map/all_to_all | solution.py:426
  59.8 6.2 %collective-permute-start.2 = (f32[128,128]{1,0:T(8,128)S(1)}, f32[128,128]{1,0:T(8,128)S(1)}, u32[]{:S(2)}, u32[]{:S(2)}) collective-permute-start(f32[128,128]{1,0:T(8,128)S(1)} %param.2), channel_id=1, source_target_pairs={{0,1},{1,2},{2,3},{3,4},{4,5},{5,6},{6,7},{7,8},{8,9},{9,10},{10,1... | collective-permute-start | bytes 196616 | tf_op jit(solution)/shard_map/cond/branch_0_fun/ppermute | solution.py:415
  63.0 9.5 %collective-permute-start.3 = (f32[128,128]{1,0:T(8,128)S(1)}, f32[128,128]{1,0:T(8,128)S(1)}, u32[]{:S(2)}, u32[]{:S(2)}) collective-permute-start(f32[128,128]{1,0:T(8,128)S(1)} %param.2), channel_id=1, source_target_pairs={{1,0},{2,1},{3,2},{4,3},{5,4},{6,5},{7,6},{8,7},{9,8},{10,9},{11,1... | collective-permute-start | bytes 196616 | tf_op jit(solution)/shard_map/cond/branch_0_fun/ppermute | solution.py:415

commit v7 on v6

--- a/solution.py
+++ b/solution.py
@@ -63,10 +63,6 @@
 
 def rows_of(ref):
     return ref.reshape(3 * NODES, 128)
-
-
-def flat_of(ref):
-    return ref.reshape(ref.shape[0], 128)
 
 
 def padded(ref, c):
@@ -276,31 +272,33 @@
     both = dot(jnp.concatenate(left, axis=1), jnp.concatenate(right, axis=0))
     both = both + pltpu.roll(both, 64, 1)
     both = jnp.where(iota((rows, 128), 1) < 64, both[:rows], both[rows:])
-    out = flat_of(out_ref)
     lane, apart = iota((n_event, 128), 1), (iota((n_event, 128), 0) + first) % n_event - place_ref[2]
     used = ((apart == 1) & (lane < 4)) | ((apart == -1) & (lane >= 4) & (lane < 8))
     edges = jnp.where(used, jnp.broadcast_to(edge_ref[0:1], (n_event, 128)), 0.0)
     for p in range(n_event):
-        out[5 * p : 5 * p + 4] = both[4 * p : 4 * p + 4]
-        out[5 * p + 4 : 5 * p + 5] = edges[p : p + 1]
-
-
-def last_kernel(
-    count_ref, place_ref, field_ref, one_ref, strain_ref, before_ref, after_ref, near_ref, material_ref,
-    pick_ref, lift_ref,
-    final_ref,
+        out_ref[5 * p : 5 * p + 4] = both[4 * p : 4 * p + 4]
+        out_ref[5 * p + 4 : 5 * p + 5] = edges[p : p + 1]
+
+
+def last_own_kernel(
+    count_ref, place_ref, field_ref, one_ref, strain_ref, near_ref, material_ref, pick_ref, lift_ref, partial_ref
 ):
     live = live_mask(count_ref)
     material = jnp.broadcast_to(material_ref[...], (128, 128))
     fields = [one_ref[c] for c in range(3)]
-    jumps = own_jumps(place_ref, near_ref, faces_of(pick_ref[...], stacked(fields)))
+    lift = lift_of(lift_ref[...], own_jumps(place_ref, near_ref, faces_of(pick_ref[...], stacked(fields))))
+    for c in range(3):
+        force = 0.5 * lift[c] - material * strain_ref[c]
+        partial_ref[c] = live * (2.0 * fields[c] - field_ref[c] + 0.4 * force)
+
+
+def last_kernel(count_ref, place_ref, partial_ref, before_ref, after_ref, near_ref, pick_ref, lift_ref, final_ref):
+    live = live_mask(count_ref)
     rims = faces_of(pick_ref[...], stacked(list(merge(before_ref[...], after_ref[...]))))
-    more = rim_jumps(place_ref, near_ref, rims, 3)
-    lift = lift_of(lift_ref[...], [[a + b for a, b in zip(*pair)] for pair in zip(jumps, more)])
+    lift = lift_of(lift_ref[...], rim_jumps(place_ref, near_ref, rims, 3))
     final = rows_of(final_ref)
     for c in range(3):
-        force = 0.5 * lift[c] - material * strain_ref[c]
-        out = live * (2.0 * fields[c] - field_ref[c] + 0.4 * force)
+        out = partial_ref[c] + live * (0.2 * lift[c])
         final[NODES * c : NODES * (c + 1)] = out[:NODES]
 
 
@@ -311,11 +309,10 @@
 
 
 def smooth_kernel(n_event, place_ref, x_ref, turned_ref, edge_ref, o_ref):
-    rows = flat_of(x_ref)
     mine, parts = place_ref[0], place_ref[1]
     node, tile = iota((8, 128), 1), iota((8, 128), 0)
     span = 40 if n_event % 8 == 0 else 5 * n_event
-    total = total_of([rows[i : i + span] for i in range(0, 5 * n_event, span)])
+    total = total_of([x_ref[i : i + span] for i in range(0, 5 * n_event, span)])
     total = total_of([total[i : i + 5] for i in range(0, span, 5)])
     lane = iota((1, 128), 1)
     beside = ((lane < 4) & (mine > 0)) | ((lane >= 4) & (mine < parts - 1))
@@ -362,7 +359,7 @@
     place = jnp.stack([lax.axis_index("mesh"), jnp.int32(n_mesh), lax.axis_index("event")]).astype(I32)
     up = [(i, (i + 1) % n_mesh) for i in range(n_mesh)]
     down = [(j, i) for i, j in up]
-    first_mesh, first_event = 5 * n_mesh // 8, n_event // 2
+    first_mesh, first_event = 5 * n_mesh // 8, 3 * n_event // 4
     mesh_group = [(i + first_mesh) % n_mesh for i in range(n_mesh)]
     event_group = [(i + first_event) % n_event for i in range(n_event)]
 
@@ -377,10 +374,6 @@
         3,
         [pltpu.VMEM(x.shape, F32) for x in (forward, adjoint)] + [pltpu.SemaphoreType.DMA((3,))],
     )(counts, *inputs[:3])
-    cores = min(n_event, 2)
-    event = lax.axis_index("event")
-    is_near = event < cores
-    is_near, rim = lax.optimization_barrier((is_near, rim))
     before, after = lax.ppermute(rim, "mesh", up), lax.ppermute(rim, "mesh", down)
     partial, kernel, turned, stiff, pick, lift, project, wanted, near, material = call(
         own_kernel,
@@ -411,23 +404,21 @@
         2,
         10,
     )(counts, place, partial, kernel, before, after, near, stiff, pick, lift, project, wanted)
-    def halo(rim_one, *_):
-        return lax.ppermute(rim_one, "mesh", up), lax.ppermute(rim_one, "mesh", down)
-
-    none = jnp.zeros((128, 128), F32)
-    sides = lax.cond(is_near, halo, lambda rim_one: (none, none), rim_one)
-    chunk, sides = lax.optimization_barrier((chunk, sides))
     parts = lax.all_to_all(chunk, "mesh", 0, 0, tiled=True, axis_index_groups=[mesh_group])
 
     def dense(*refs):
         dense_kernel(n_event, n_mesh, tile_width, first_event, *refs)
 
-    partial = call(dense, shape(5 * n_event, 1, 128), 1, 2)(place, parts, edge)
-    pieces = lax.all_to_all(partial, "event", 0, 0, tiled=True, axis_index_groups=[event_group])
-    rim_one, is_near, _ = lax.optimization_barrier((rim_one, is_near, partial))
-    before, after = lax.cond(is_near, lambda rim_one, sides: sides, halo, rim_one, sides)
-    final = call(last_kernel, shape(3, NODES, 1, 128), 2, 9)(
-        counts, place, fields, one, strain, before, after, near, material, pick, lift
+    partial = call(dense, shape(5 * n_event, 128), 1, 2)(place, parts, edge)
+    pieces = lax.all_to_all(partial.reshape(-1, 1, 128), "event", 0, 0, tiled=True, axis_index_groups=[event_group])
+    pieces = pieces.reshape(-1, 128)
+    rim_one, one, _ = lax.optimization_barrier((rim_one, one, partial))
+    before, after = lax.ppermute(rim_one, "mesh", up), lax.ppermute(rim_one, "mesh", down)
+    partial = call(last_own_kernel, shape(3, 128, 128), 2, 7)(
+        counts, place, fields, one, strain, near, material, pick, lift
+    )
+    final = call(last_kernel, shape(3, NODES, 1, 128), 2, 6)(
+        counts, place, partial, before, after, near, pick, lift
     )
 
     def smooth(*refs):

time: 76.3 us -> 70.8 us (0.928)
  the two profiles are of different devices: /device:TPU:62 before, /device:TPU:1 now
where the time goes in v7:
time: 70.8 us; the launch traced here: 70.5 us
  starting transfers between devices  36.3 us (51%)
  Pallas kernels  11.4 us (16%)
  blocking collectives  11.4 us (16%)
  waiting for transfers between devices  9.97 us (14%)
  between operations  1.37 us (2%)
    all_to_all x1, starting transfers between devices, per_device(): lax.all_to_all(partial.reshape(-1, 1, 128), 'event', 0, 0, tiled=True, ax...  19.3 us
    all_to_all x1, blocking collectives, per_device(): lax.all_to_all(chunk, 'mesh', 0, 0, tiled=True, axis_index_groups=[mesh_g...  11.4 us
    ppermute x1, starting transfers between devices, per_device(): lax.ppermute(rim, 'mesh', down)  7.67 us
    ppermute x1, starting transfers between devices, per_device(): lax.ppermute(rim_one, 'mesh', down)  5.55 us
    ppermute x1, waiting for transfers between devices, per_device(): lax.ppermute(rim_one, 'mesh', up)  5.31 us
    ppermute x1, waiting for transfers between devices, per_device(): lax.ppermute(rim, 'mesh', up)  4.65 us
    pallas_call x1, Pallas kernels, per_device(): call(own_kernel, (shape(6, 128, 128), shape(128, 128), shape(8, 128), sha...  2.05 us
    pallas_call x1, Pallas kernels, per_device(): call(one_step, (shape(3, 128, 128), shape(3, 128, 128), shape(128, 128),...  1.92 us
  transfers between devices with their start and end apart: 5, of which 2 were waited for; matrix products, arithmetic and copies ran while one was open for 0% of the time, Pallas kernels for 7%

profile of v7, /device:TPU:1, one launch (start us, length us, event | category | flops | bytes accessed | tf_op | source)
XLA Modules:
  0.0 70.5 jit_solution(1500409649716724026)
XLA Ops:
  1.3 1.3 %shard_map.104 = (f32[200,128]{1,0:T(8,128)S(1)}, f32[6,128,128]{2,1,0:T(8,128)S(1)}, f32[4,4]{1,0:T(4,128)S(1)}) custom-call(s32[1,1]{1,0:T(1,128)S(6)} %copy.12.count_ref.refs_0_, f32[3,125,1,128]{3,2,1,0:T(1,128)} %bitcast.13, f32[3,125,1,128]{3,2,1,0:T(1,128)} %bitcast.14, f32[4,4]{1,0:T(4,128)} %smooth_ref.1), custom_call_target="tpu_custom_call" | custom-call | tf_op jit(solution)/shard_map/pallas_call | solution.py:369
  2.6 7.7 %collective-permute-start.1 = (f32[200,128]{1,0:T(8,128)S(1)}, f32[200,128]{1,0:T(8,128)S(1)}, u32[]{:S(2)}, u32[]{:S(2)}) collective-permute-start(f32[200,128]{1,0:T(8,128)S(1)} %get-tuple-element.26), channel_id=1, source_target_pairs={{1,0},{2,1},{3,2},{4,3},{5,4},{6,5},{7,6},{8,7},{9,8},{10,9},{11,1... | collective-permute-start | bytes 307208 | tf_op jit(solution)/shard_map/ppermute | solution.py:377
  10.2 1.9 %collective-permute-start = (f32[200,128]{1,0:T(8,128)S(1)}, f32[200,128]{1,0:T(8,128)S(1)}, u32[]{:S(2)}, u32[]{:S(2)}) collective-permute-start(f32[200,128]{1,0:T(8,128)S(1)} %get-tuple-element.26), channel_id=1, source_target_pairs={{0,1},{1,2},{2,3},{3,4},{4,5},{5,6},{6,7},{7,8},{8,9},{9,10},{10,1... | collective-permute-start | bytes 307208 | tf_op jit(solution)/shard_map/ppermute | solution.py:377
  12.2 0.1 pad_add_fusion.place_ref.refs_1_.refs_0_
  12.2 2.0 %shard_map.105 = (f32[6,128,128]{2,1,0:T(8,128)S(1)}, f32[128,128]{1,0:T(8,128)S(1)}, f32[8,128]{1,0:T(8,128)S(1)}, bf16[2,128,128]{2,1,0:T(8,128)(2,1)S(1)}, bf...) custom-call(s32[1,1]{1,0:T(1,128)S(6)} %copy.12.count_ref.refs_0_, ...), custom_call_target="tpu_custom_call" | custom-call | tf_op jit(solution)/shard_map/pallas_call | solution.py:378
  14.3 0.0 collective-permute-done.1.refs_5_
  14.3 4.6 %collective-permute-done.refs_4_ = f32[200,128]{1,0:T(8,128)S(1)} collective-permute-done((f32[200,128]{1,0:T(8,128)S(1)}, f32[200,128]{1,0:T(8,128)S(1)}, u32[]{:S(2)}, u32[]{:S(2)}) %collective-permute-start) | collective-permute-done | bytes 102432 | tf_op jit(solution)/shard_map/ppermute | solution.py:377
  19.0 1.9 %shard_map.106 = (f32[3,128,128]{2,1,0:T(8,128)S(1)}, f32[3,128,128]{2,1,0:T(8,128)S(1)}, f32[128,128]{1,0:T(8,128)S(1)}, f32[8,128]{1,0:T(8,128)S(1)}, f32[16,72,128]{2,1,0:T(8,128)S(1)}) custom-call(s32[1,1]{1,0:T(1,128)S(6)} %copy.12.count_ref.refs_0_, s32[3]{0:T(128)S(1)} %pad_add_fusion.place_ref.refs_1_.refs_0_, ...), custom_call_target="tpu_custom_call" | custom-call | tf_op jit(solution)/shard_map/pallas_call | solution.py:401
  20.9 11.4 %all_to_all.10.refs_1_ = f32[16,72,128]{2,1,0:T(8,128)S(1)} all-to-all(f32[16,72,128]{2,1,0:T(8,128)S(1)} %get-tuple-element.35), channel_id=1, replica_groups={{10,11,12,13,14,15,0,1,2,3,4,5,6,7,8,9},{26,27,28,29,30,31,16,17,18,19,..., dimensions={0} | all-to-all | bytes 1179648 | tf_op jit(solution)/shard_map/all_to_all | solution.py:407
  32.2 1.8 %shard_map.107 = f32[160,128]{1,0:T(8,128)} custom-call(s32[3]{0:T(128)S(1)} %pad_add_fusion.place_ref.refs_1_.refs_0_, f32[16,72,128]{2,1,0:T(8,128)S(1)} %all_to_all.10.refs_1_, f32[8,128]{1,0:T(8,128)S(1)} %get-tuple-element.36.refs_2_.refs_3_), custom_call_target="tpu_custom_call" | custom-call | tf_op jit(solution)/shard_map/pallas_call | solution.py:412
  34.1 19.3 %all-to-all-start.1 = ((f32[160,1,128]{2,1,0:T(1,128)}), f32[160,1,128]{2,1,0:T(1,128)S(1)}, u32[]{:S(2)}, u32[]{:S(2)}) async-start(f32[160,1,128]{2,1,0:T(1,128)} %bitcast.8), calls=%async_computation.1 | async-start | bytes 163840 | tf_op jit(solution)/shard_map/all_to_all | solution.py:413
  53.3 5.5 %collective-permute-start.3 = (f32[128,128]{1,0:T(8,128)S(1)}, f32[128,128]{1,0:T(8,128)S(1)}, u32[]{:S(2)}, u32[]{:S(2)}) collective-permute-start(f32[128,128]{1,0:T(8,128)S(1)} %get-tuple-element.40), channel_id=1, source_target_pairs={{1,0},{2,1},{3,2},{4,3},{5,4},{6,5},{7,6},{8,7},{9,8},{10,9},{11,1... | collective-permute-start | bytes 196616 | tf_op jit(solution)/shard_map/ppermute | solution.py:416
  58.9 1.9 %collective-permute-start.2 = (f32[128,128]{1,0:T(8,128)S(1)}, f32[128,128]{1,0:T(8,128)S(1)}, u32[]{:S(2)}, u32[]{:S(2)}) collective-permute-start(f32[128,128]{1,0:T(8,128)S(1)} %get-tuple-element.40), channel_id=1, source_target_pairs={{0,1},{1,2},{2,3},{3,4},{4,5},{5,6},{6,7},{7,8},{8,9},{9,10},{10,1... | collective-permute-start | bytes 196616 | tf_op jit(solution)/shard_map/ppermute | solution.py:416
  60.8 1.1 %shard_map.108.partial_ref = f32[3,128,128]{2,1,0:T(8,128)S(1)} custom-call(s32[1,1]{1,0:T(1,128)S(6)} %copy.12.count_ref.refs_0_, s32[3]{0:T(128)S(1)} %pad_add_fusion.place_ref.refs_1_.refs_0_, f32[6,128,128]{2,1,0:T(8,128)S(1)} %get-tuple-element.22.field_ref, f32[3,128,128]{2,1,0:T(8,128)S(1)} %get-tuple-element.37.one_ref, ...), custom_call_target="tpu_custom_call" | custom-call | tf_op jit(solution)/shard_map/pallas_call | solution.py:417
  61.9 0.0 collective-permute-done.3.after_ref
  61.9 5.3 %collective-permute-done.2.before_ref = f32[128,128]{1,0:T(8,128)S(1)} collective-permute-done((f32[128,128]{1,0:T(8,128)S(1)}, f32[128,128]{1,0:T(8,128)S(1)}, u32[]{:S(2)}, u32[]{:S(2)}) %collective-permute-start.2) | collective-permute-done | bytes 65568 | tf_op jit(solution)/shard_map/ppermute | solution.py:416
  67.2 1.9 %shard_map.109 = f32[3,125,1,128]{3,2,1,0:T(1,128)} custom-call(s32[1,1]{1,0:T(1,128)S(6)} %copy.12.count_ref.refs_0_, s32[3]{0:T(128)S(1)} %pad_add_fusion.place_ref.refs_1_.refs_0_, f32[3,128,128]{2,1,0:T(8,128)S(1)} %shard_map.108.partial_ref, f32[128,128]{1,0:T(8,128)S(1)} %collective-permute-done.2.before_ref, ...), custom_call_target="tpu_custom_call" | custom-call | tf_op jit(solution)/shard_map/pallas_call | solution.py:420
  69.1 0.0 all-to-all-done.1
  69.1 1.4 %shard_map.110 = f32[4,64]{1,0:T(4,128)} custom-call(s32[3]{0:T(128)S(1)} %pad_add_fusion.place_ref.refs_1_.refs_0_, f32[160,128]{1,0:T(8,128)S(1)} %bitcast.12, f32[8,128]{1,0:T(8,128)S(1)} %get-tuple-element.41.refs_2_, f32[8,128]{1,0:T(8,128)S(1)} %get-tuple-element.36.refs_2_.refs_3_), custom_call_target="tpu_custom_call" | custom-call | tf_op jit(solution)/shard_map/pallas_call | solution.py:427
Async XLA Ops:
  2.6 11.7 %collective-permute-start.1 = (f32[200,128]{1,0:T(8,128)S(1)}, f32[200,128]{1,0:T(8,128)S(1)}, u32[]{:S(2)}, u32[]{:S(2)}) collective-permute-start(f32[200,128]{1,0:T(8,128)S(1)} %get-tuple-element.26), channel_id=1, source_target_pairs={{1,0},{2,1},{3,2},{4,3},{5,4},{6,5},{7,6},{8,7},{9,8},{10,9},{11,1... | collective-permute-start | bytes 307208 | tf_op jit(solution)/shard_map/ppermute | solution.py:377
  10.2 8.7 %collective-permute-start = (f32[200,128]{1,0:T(8,128)S(1)}, f32[200,128]{1,0:T(8,128)S(1)}, u32[]{:S(2)}, u32[]{:S(2)}) collective-permute-start(f32[200,128]{1,0:T(8,128)S(1)} %get-tuple-element.26), channel_id=1, source_target_pairs={{0,1},{1,2},{2,3},{3,4},{4,5},{5,6},{6,7},{7,8},{8,9},{9,10},{10,1... | collective-permute-start | bytes 307208 | tf_op jit(solution)/shard_map/ppermute | solution.py:377
  34.1 35.0 %all-to-all-start.1 = ((f32[160,1,128]{2,1,0:T(1,128)}), f32[160,1,128]{2,1,0:T(1,128)S(1)}, u32[]{:S(2)}, u32[]{:S(2)}) async-start(f32[160,1,128]{2,1,0:T(1,128)} %bitcast.8), calls=%async_computation.1 | async-start | bytes 163840 | tf_op jit(solution)/shard_map/all_to_all | solution.py:413
  53.3 8.6 %collective-permute-start.3 = (f32[128,128]{1,0:T(8,128)S(1)}, f32[128,128]{1,0:T(8,128)S(1)}, u32[]{:S(2)}, u32[]{:S(2)}) collective-permute-start(f32[128,128]{1,0:T(8,128)S(1)} %get-tuple-element.40), channel_id=1, source_target_pairs={{1,0},{2,1},{3,2},{4,3},{5,4},{6,5},{7,6},{8,7},{9,8},{10,9},{11,1... | collective-permute-start | bytes 196616 | tf_op jit(solution)/shard_map/ppermute | solution.py:416
  58.9 8.3 %collective-permute-start.2 = (f32[128,128]{1,0:T(8,128)S(1)}, f32[128,128]{1,0:T(8,128)S(1)}, u32[]{:S(2)}, u32[]{:S(2)}) collective-permute-start(f32[128,128]{1,0:T(8,128)S(1)} %get-tuple-element.40), channel_id=1, source_target_pairs={{0,1},{1,2},{2,3},{3,4},{4,5},{5,6},{6,7},{7,8},{8,9},{9,10},{10,1... | collective-permute-start | bytes 196616 | tf_op jit(solution)/shard_map/ppermute | solution.py:416

commit v8 on v7

--- a/solution.py
+++ b/solution.py
@@ -148,12 +148,12 @@
     return columns(dot(lift, high) + dot(lift, low))
 
 
-def own_jumps(place_ref, near_ref, own):
+def own_jumps(near_ref, own):
     jumps = [[] for _ in own]
     for face in range(FACES):
         p = partner_face[face]
         near = jnp.broadcast_to(near_ref[face], (SHEET, 128))
-        home = near // 128 == place_ref[0]
+        home = near // 128 == lax.axis_index("mesh")
         slot = near % 128
         for k in range(len(own)):
             here = take(own[k][SHEET * p : SHEET * (p + 1)], slot)
@@ -161,8 +161,8 @@
     return jumps
 
 
-def rim_jumps(place_ref, near_ref, rims, n):
-    mine, parts = place_ref[0], place_ref[1]
+def rim_jumps(near_ref, rims, n):
+    mine, parts = lax.axis_index("mesh"), lax.axis_size("mesh")
     follower = jnp.where(mine + 1 == parts, 0, mine + 1)
     jumps = [[] for _ in range(n)]
     for face in range(FACES):
@@ -185,7 +185,7 @@
 
 
 def own_kernel(
-    count_ref, place_ref, field_ref, smooth_ref, near_in, stiff_in, material_in, project_in, destination_in,
+    count_ref, field_ref, smooth_ref, near_in, stiff_in, material_in, project_in, destination_in,
     partial_ref, kernel_ref, turned_ref, stiff_out_ref, pick_ref, lift_ref, project_out_ref, wanted_ref, near_ref,
     material_ref, stiff_ref, project_ref, destination_ref, sems,
 ):
@@ -202,7 +202,7 @@
     x = stacked(fields)
     faces = faces_of(pick, x)
     copies[0].wait()
-    lifted = lift_of(lift, own_jumps(place_ref, near_ref, faces))
+    lifted = lift_of(lift, own_jumps(near_ref, faces))
     for copy in copies[1:]:
         copy.wait()
     material = jnp.broadcast_to(material_ref[...], (128, 128))
@@ -225,7 +225,7 @@
 
 def step_kernel(
     scale, n_mesh,
-    count_ref, place_ref, partial_ref, kernel_ref, before_ref, after_ref, near_ref, stiff_ref, pick_ref, lift_ref,
+    count_ref, partial_ref, kernel_ref, before_ref, after_ref, near_ref, stiff_ref, pick_ref, lift_ref,
     project_ref, wanted_ref,
     forward_ref, strain_ref, rim_ref, edge_ref, chunk_ref,
 ):
@@ -233,7 +233,7 @@
     first, second = merge(before_ref[:128], after_ref[:128])
     upper, lower = merge(before_ref[128:192], after_ref[128:192])
     rims = faces_of(pick_ref[...], stacked([first, second, jnp.concatenate([upper, lower], axis=0)]))
-    lift = lift_of(lift_ref[...], rim_jumps(place_ref, near_ref, rims, 6))
+    lift = lift_of(lift_ref[...], rim_jumps(near_ref, rims, 6))
     fields = [partial_ref[k] + live * (0.2 * lift[k]) for k in range(6)]
     strain = strains(stiff_ref[0], stiff_ref[1], stacked(fields))
     kernel = kernel_ref[...] + sum(fields[c] * strain[3 + c] for c in range(3))
@@ -241,9 +241,8 @@
     p_high, p_low = project_ref[0], project_ref[1]
     blocks = dot(jnp.concatenate([p_high, p_high], axis=1), jnp.concatenate([k_high, k_low], axis=0))
     blocks = (blocks + dot(p_low, k_high)) * scale
-    turned = jnp.concatenate([blocks, pltpu.roll(blocks, 64, 1)], axis=0).T[:64]
     for m in range(n_mesh):
-        chunk_ref[m, :64] = turned
+        chunk_ref[m, :64] = blocks
         chunk_ref[m, 64:] = wanted_ref[...]
     rim_ref[...] = pack_rim(fields[:3])
     edge_ref[...] = jnp.where(iota((8, 128), 1) < 4, before_ref[192:], after_ref[192:])
@@ -252,54 +251,54 @@
         strain_ref[c] = strain[c]
 
 
-def dense_kernel(n_event, n_mesh, tile_width, first, place_ref, parts_ref, edge_ref, out_ref):
-    rows = 4 * n_event
-    row = iota((2 * rows, 128), 0)
-    within = row % rows
-    event = (within // 4 + first) % n_event
-    tile = event * (n_mesh * tile_width) + within % 4 + 4 * (row // rows) - 2
-    tile = tile.astype(F32) + (place_ref[0] * tile_width).astype(F32)
-    lane = iota((64, 128), 1)
+def dense_kernel(n_event, n_mesh, tile_width, first, parts_ref, edge_ref, before_ref, after_ref, out_ref):
+    rows = 8 * n_event
+    row = iota((rows, 128), 0)
+    tile = (row % n_event + first) % n_event * (n_mesh * tile_width) + row // n_event - 2
+    tile = tile.astype(F32) + (lax.axis_index("mesh") * tile_width).astype(F32)
     left, right = [], []
     for m in range(n_mesh):
-        x = parts_ref[m, :64]
-        high = x.astype(BF16).astype(F32)
-        low = x - high
-        right.append(jnp.where(lane < 64, high, pltpu.roll(low, 64, 1)).astype(BF16))
-        right.append(jnp.where(lane < 64, pltpu.roll(high, 64, 1), low).astype(BF16))
-        wanted = jnp.broadcast_to(parts_ref[m, 64:65], (2 * rows, 128))
-        left.append(jnp.where(wanted == tile, 1.0, 0.0).astype(BF16))
-    both = dot(jnp.concatenate(left, axis=1), jnp.concatenate(right, axis=0))
-    both = both + pltpu.roll(both, 64, 1)
-    both = jnp.where(iota((rows, 128), 1) < 64, both[:rows], both[rows:])
-    lane, apart = iota((n_event, 128), 1), (iota((n_event, 128), 0) + first) % n_event - place_ref[2]
+        left.append(jnp.concatenate(halves(parts_ref[m, :64]), axis=0))
+        wanted = jnp.broadcast_to(parts_ref[m, 64:65], (rows, 128))
+        right.append(jnp.where(wanted == tile, 1.0, 0.0).astype(BF16))
+    left, right = jnp.concatenate(left, axis=1), jnp.concatenate(right, axis=1)
+    both = lax.dot_general(left, right, (((1,), (1,)), ((), ())), preferred_element_type=F32)
+    both = both[:64] + both[64:]
+    half = 4 * n_event
+    both = jnp.concatenate([both[:, :half], both[:, half:]], axis=0).T
+    for j in range(4):
+        out_ref[pl.ds(j, n_event, stride=5)] = both[n_event * j : n_event * (j + 1)]
+    lane, event = iota((n_event, 128), 1), (iota((n_event, 128), 0) + first) % n_event
+    apart = event - lax.axis_index("event")
     used = ((apart == 1) & (lane < 4)) | ((apart == -1) & (lane >= 4) & (lane < 8))
     edges = jnp.where(used, jnp.broadcast_to(edge_ref[0:1], (n_event, 128)), 0.0)
-    for p in range(n_event):
-        out_ref[5 * p : 5 * p + 4] = both[4 * p : 4 * p + 4]
-        out_ref[5 * p + 4 : 5 * p + 5] = edges[p : p + 1]
-
-
-def last_own_kernel(
-    count_ref, place_ref, field_ref, one_ref, strain_ref, near_ref, material_ref, pick_ref, lift_ref, partial_ref
+    out_ref[pl.ds(4, n_event, stride=5)] = edges
+
+
+def last_kernel(
+    count_ref, field_ref, one_ref, strain_ref, before_ref, after_ref, near_ref, material_ref, pick_ref, lift_ref,
+    turned_ref, edge_ref,
+    final_ref, table_ref, open_ref,
 ):
     live = live_mask(count_ref)
     material = jnp.broadcast_to(material_ref[...], (128, 128))
     fields = [one_ref[c] for c in range(3)]
-    lift = lift_of(lift_ref[...], own_jumps(place_ref, near_ref, faces_of(pick_ref[...], stacked(fields))))
+    jumps = own_jumps(near_ref, faces_of(pick_ref[...], stacked(fields)))
+    rims = faces_of(pick_ref[...], stacked(list(merge(before_ref[...], after_ref[...]))))
+    more = rim_jumps(near_ref, rims, 3)
+    lift = lift_of(lift_ref[...], [[a + b for a, b in zip(*pair)] for pair in zip(jumps, more)])
+    final = rows_of(final_ref)
     for c in range(3):
         force = 0.5 * lift[c] - material * strain_ref[c]
-        partial_ref[c] = live * (2.0 * fields[c] - field_ref[c] + 0.4 * force)
-
-
-def last_kernel(count_ref, place_ref, partial_ref, before_ref, after_ref, near_ref, pick_ref, lift_ref, final_ref):
-    live = live_mask(count_ref)
-    rims = faces_of(pick_ref[...], stacked(list(merge(before_ref[...], after_ref[...]))))
-    lift = lift_of(lift_ref[...], rim_jumps(place_ref, near_ref, rims, 3))
-    final = rows_of(final_ref)
-    for c in range(3):
-        out = partial_ref[c] + live * (0.2 * lift[c])
+        out = live * (2.0 * fields[c] - field_ref[c] + 0.4 * force)
         final[NODES * c : NODES * (c + 1)] = out[:NODES]
+    mine, parts = lax.axis_index("mesh"), lax.axis_size("mesh")
+    tile = iota((8, 128), 0)
+    is_open = ((tile == 1) & (mine == 0)) | ((tile == 6) & (mine == parts - 1))
+    edge = jnp.where(tile == 6, pltpu.roll(edge_ref[...], 124, 1), edge_ref[...])
+    edge = jnp.where(((tile == 1) | (tile == 6)) & ~is_open, edge, 0.0)
+    table_ref[...] = jnp.where((tile >= 2) & (tile < 6), pltpu.roll(turned_ref[...], 2, 0), edge)
+    open_ref[...] = is_open.astype(F32)
 
 
 def total_of(parts):
@@ -308,18 +307,14 @@
     return parts[0]
 
 
-def smooth_kernel(n_event, place_ref, x_ref, turned_ref, edge_ref, o_ref):
-    mine, parts = place_ref[0], place_ref[1]
+def smooth_kernel(n_event, x_ref, table_ref, open_ref, o_ref):
     node, tile = iota((8, 128), 1), iota((8, 128), 0)
     span = 40 if n_event % 8 == 0 else 5 * n_event
     total = total_of([x_ref[i : i + span] for i in range(0, 5 * n_event, span)])
     total = total_of([total[i : i + 5] for i in range(0, span, 5)])
-    lane = iota((1, 128), 1)
-    beside = ((lane < 4) & (mine > 0)) | ((lane >= 4) & (mine < parts - 1))
-    edge = jnp.broadcast_to(jnp.where(beside, edge_ref[0:1], total[4:5]), (8, 128))
-    table = jnp.where((tile >= 2) & (tile < 6), pltpu.roll(turned_ref[...], 2, 0), 0.0)
-    table = jnp.where(tile == 1, edge, table)
-    table = jnp.where(tile == 6, pltpu.roll(edge, 124, 1), table)
+    edge = jnp.broadcast_to(total[4:5], (8, 128))
+    edge = jnp.where(tile == 6, pltpu.roll(edge, 124, 1), edge)
+    table = table_ref[...] + open_ref[...] * edge
     coef = [jnp.broadcast_to(table[:, d : d + 1], (8, 128)) for d in range(4)]
     total = total[:4]
     x = jnp.concatenate([total, pltpu.roll(total, 64, 1)], axis=0)
@@ -356,10 +351,9 @@
     n_mesh, n_event = lax.axis_size("mesh"), lax.axis_size("event")
     scale = math.sqrt(tile_width / elements) / STEPS
     forward, adjoint = (x.reshape(3, NODES, 1, 128) for x in (forward_start, adjoint_start))
-    place = jnp.stack([lax.axis_index("mesh"), jnp.int32(n_mesh), lax.axis_index("event")]).astype(I32)
     up = [(i, (i + 1) % n_mesh) for i in range(n_mesh)]
     down = [(j, i) for i, j in up]
-    first_mesh, first_event = 5 * n_mesh // 8, 3 * n_event // 4
+    first_mesh, first_event = 5 * n_mesh // 8, n_event // 2
     mesh_group = [(i + first_mesh) % n_mesh for i in range(n_mesh)]
     event_group = [(i + first_event) % n_event for i in range(n_event)]
 
@@ -389,11 +383,11 @@
             shape(FACES, 1, 128, dtype=I32),
             shape(1, 128),
         ),
-        2,
+        1,
         2,
         5,
         [pltpu.VMEM(x.shape, x.dtype) for x in (stiffness, project, destinations)] + [pltpu.SemaphoreType.DMA((5,))],
-    )(counts, place, fields, smooth_in, *inputs[3:])
+    )(counts, fields, smooth_in, *inputs[3:])
 
     def one_step(*refs):
         step_kernel(scale, n_mesh, *refs)
@@ -401,30 +395,26 @@
     one, strain, rim_one, edge, chunk = call(
         one_step,
         (shape(3, 128, 128), shape(3, 128, 128), shape(128, 128), shape(8, 128), shape(n_mesh, 72, 128)),
-        2,
+        1,
         10,
-    )(counts, place, partial, kernel, before, after, near, stiff, pick, lift, project, wanted)
+    )(counts, partial, kernel, before, after, near, stiff, pick, lift, project, wanted)
     parts = lax.all_to_all(chunk, "mesh", 0, 0, tiled=True, axis_index_groups=[mesh_group])
+
+    before, after = lax.ppermute(rim_one, "mesh", up), lax.ppermute(rim_one, "mesh", down)
 
     def dense(*refs):
         dense_kernel(n_event, n_mesh, tile_width, first_event, *refs)
 
-    partial = call(dense, shape(5 * n_event, 128), 1, 2)(place, parts, edge)
+    partial = call(dense, shape(5 * n_event, 128), 0, 4)(parts, edge, before, after)
     pieces = lax.all_to_all(partial.reshape(-1, 1, 128), "event", 0, 0, tiled=True, axis_index_groups=[event_group])
-    pieces = pieces.reshape(-1, 128)
-    rim_one, one, _ = lax.optimization_barrier((rim_one, one, partial))
-    before, after = lax.ppermute(rim_one, "mesh", up), lax.ppermute(rim_one, "mesh", down)
-    partial = call(last_own_kernel, shape(3, 128, 128), 2, 7)(
-        counts, place, fields, one, strain, near, material, pick, lift
-    )
-    final = call(last_kernel, shape(3, NODES, 1, 128), 2, 6)(
-        counts, place, partial, before, after, near, pick, lift
+    final, table, is_open = call(last_kernel, (shape(3, NODES, 1, 128), shape(8, 128), shape(8, 128)), 1, 11)(
+        counts, fields, one, strain, before, after, near, material, pick, lift, turned, edge
     )
 
     def smooth(*refs):
         smooth_kernel(n_event, *refs)
 
-    tiles = call(smooth, shape(tile_width, 64), 1, 3)(place, pieces, turned, edge)
+    tiles = call(smooth, shape(tile_width, 64), 0, 3)(pieces.reshape(-1, 128), table, is_open)
     return final.reshape(1, 3, NODES, 128), tiles.T
 
 

time: 70.8 us -> 68.5 us (0.968)
  blocking collectives: 11.4 us -> 0 us
  starting transfers between devices: 36.3 us -> 44.2 us
  waiting for transfers between devices: 9.97 us -> 14 us
  Pallas kernels: 11.4 us -> 8.44 us
    all_to_all x1 -> x0, blocking collectives: 11.4 us -> none  [per_device(): lax.all_to_all(chunk, 'mesh', 0, 0, tiled=True, axis_index_groups=[mesh_g...]
    all_to_all x0 -> x1, starting transfers between devices: none -> 6.66 us  [per_device(): lax.all_to_all(chunk, 'mesh', 0, 0, tiled=True, axis_index_groups=[mesh_g...]
    all_to_all x1, waiting for transfers between devices: 0.01 us -> 3.6 us  [per_device(): lax.all_to_all(partial.reshape(-1, 1, 128), 'event', 0, 0, tiled=True, ax...]
    all_to_all x1, starting transfers between devices: 19.3 us -> 22.7 us  [per_device(): lax.all_to_all(partial.reshape(-1, 1, 128), 'event', 0, 0, tiled=True, ax...]
    ppermute x1, waiting for transfers between devices: 5.31 us -> 1.86 us  [per_device(): lax.ppermute(rim_one, 'mesh', up)]
    ppermute x1, starting transfers between devices: 5.55 us -> 2.18 us  [per_device(): lax.ppermute(rim_one, 'mesh', down)]
    ppermute x1, waiting for transfers between devices: 0.01 us -> 3.37 us  [per_device(): lax.ppermute(rim_one, 'mesh', down)]
    pallas_call x4 -> x3, Pallas kernels: 6.13 us -> 3.47 us  [the longest x1 1.42 us: per_device(): call(last_kernel, (shape(3, NODES, 1, 128), shape(8, 128), shape(8, 128))...]
  transfers between devices with their start and end apart: 5 -> 6, of which waited for: 2 -> 4; matrix products, arithmetic and copies ran while one was open for 0% -> 0% of each run, Pallas kernels for 7% -> 4%
where the time goes in v8:
time: 68.5 us; the launch traced here: 68 us
  starting transfers between devices  44.2 us (65%)
  waiting for transfers between devices  14 us (20%)
  Pallas kernels  8.44 us (12%)
  between operations  1.34 us (2%)
    all_to_all x1, starting transfers between devices, per_device(): lax.all_to_all(partial.reshape(-1, 1, 128), 'event', 0, 0, tiled=True, ax...  22.7 us
    ppermute x1, starting transfers between devices, per_device(): lax.ppermute(rim, 'mesh', down)  7.67 us
    all_to_all x1, starting transfers between devices, per_device(): lax.all_to_all(chunk, 'mesh', 0, 0, tiled=True, axis_index_groups=[mesh_g...  6.66 us
    ppermute x1, waiting for transfers between devices, per_device(): lax.ppermute(rim, 'mesh', up)  5.18 us
    all_to_all x1, waiting for transfers between devices, per_device(): lax.all_to_all(partial.reshape(-1, 1, 128), 'event', 0, 0, tiled=True, ax...  3.6 us
    ppermute x1, waiting for transfers between devices, per_device(): lax.ppermute(rim_one, 'mesh', down)  3.37 us
    ppermute x1, starting transfers between devices, per_device(): lax.ppermute(rim_one, 'mesh', up)  3.09 us
    ppermute x1, starting transfers between devices, per_device(): lax.ppermute(rim_one, 'mesh', down)  2.18 us
  transfers between devices with their start and end apart: 6, of which 4 were waited for; matrix products, arithmetic and copies ran while one was open for 0% of the time, Pallas kernels for 4%

profile of v8, /device:TPU:1, one launch (start us, length us, event | category | flops | bytes accessed | tf_op | source)
XLA Modules:
  0.0 68.0 jit_solution(3910733131097202223)
XLA Ops:
  1.3 1.3 %shard_map.104 = (f32[200,128]{1,0:T(8,128)S(1)}, f32[6,128,128]{2,1,0:T(8,128)S(1)}, f32[4,4]{1,0:T(4,128)S(1)}) custom-call(s32[1,1]{1,0:T(1,128)S(6)} %copy.12.count_ref.refs_0_, f32[3,125,1,128]{3,2,1,0:T(1,128)} %bitcast.11, f32[3,125,1,128]{3,2,1,0:T(1,128)} %bitcast.12, f32[4,4]{1,0:T(4,128)} %smooth_ref.1), custom_call_target="tpu_custom_call" | custom-call | tf_op jit(solution)/shard_map/pallas_call | solution.py:363
  2.6 7.7 %collective-permute-start.1 = (f32[200,128]{1,0:T(8,128)S(1)}, f32[200,128]{1,0:T(8,128)S(1)}, u32[]{:S(2)}, u32[]{:S(2)}) collective-permute-start(f32[200,128]{1,0:T(8,128)S(1)} %get-tuple-element.27), channel_id=1, source_target_pairs={{1,0},{2,1},{3,2},{4,3},{5,4},{6,5},{7,6},{8,7},{9,8},{10,9},{11,1... | collective-permute-start | bytes 307208 | tf_op jit(solution)/shard_map/ppermute | solution.py:371
  10.2 1.9 %collective-permute-start = (f32[200,128]{1,0:T(8,128)S(1)}, f32[200,128]{1,0:T(8,128)S(1)}, u32[]{:S(2)}, u32[]{:S(2)}) collective-permute-start(f32[200,128]{1,0:T(8,128)S(1)} %get-tuple-element.27), channel_id=1, source_target_pairs={{0,1},{1,2},{2,3},{3,4},{4,5},{5,6},{6,7},{7,8},{8,9},{9,10},{10,1... | collective-permute-start | bytes 307208 | tf_op jit(solution)/shard_map/ppermute | solution.py:371
  12.2 1.6 %shard_map.105 = (f32[6,128,128]{2,1,0:T(8,128)S(1)}, f32[128,128]{1,0:T(8,128)S(1)}, f32[8,128]{1,0:T(8,128)S(1)}, bf16[2,128,128]{2,1,0:T(8,128)(2,1)S(1)}, bf...) custom-call(s32[1,1]{1,0:T(1,128)S(6)} %copy.12.count_ref.refs_0_, ...), custom_call_target="tpu_custom_call" | custom-call | tf_op jit(solution)/shard_map/pallas_call | solution.py:372
  13.8 0.0 collective-permute-done.1.refs_4_
  13.8 5.2 %collective-permute-done.refs_3_ = f32[200,128]{1,0:T(8,128)S(1)} collective-permute-done((f32[200,128]{1,0:T(8,128)S(1)}, f32[200,128]{1,0:T(8,128)S(1)}, u32[]{:S(2)}, u32[]{:S(2)}) %collective-permute-start) | collective-permute-done | bytes 102432 | tf_op jit(solution)/shard_map/ppermute | solution.py:371
  19.0 2.1 %shard_map.106 = (f32[3,128,128]{2,1,0:T(8,128)S(1)}, f32[3,128,128]{2,1,0:T(8,128)S(1)}, f32[128,128]{1,0:T(8,128)S(1)}, f32[8,128]{1,0:T(8,128)S(1)}, f32[16,72,128]{2,1,0:T(8,128)}) custom-call(s32[1,1]{1,0:T(1,128)S(6)} %copy.12.count_ref.refs_0_, f32[6,128,128]{2,1,0:T(8,128)S(1)} %get-tuple-element.25.refs_1_, ...), custom_call_target="tpu_custom_call" | custom-call | tf_op jit(solution)/shard_map/pallas_call | solution.py:395
  21.1 6.7 %all-to-all-start = ((f32[16,72,128]{2,1,0:T(8,128)}), f32[16,72,128]{2,1,0:T(8,128)S(1)}, u32[]{:S(2)}, u32[]{:S(2)}) async-start(f32[16,72,128]{2,1,0:T(8,128)} %get-tuple-element.41), calls=%async_computation | async-start | bytes 1179648 | tf_op jit(solution)/shard_map/all_to_all | solution.py:401
  27.7 2.2 %collective-permute-start.3 = (f32[128,128]{1,0:T(8,128)S(1)}, f32[128,128]{1,0:T(8,128)S(1)}, u32[]{:S(2)}, u32[]{:S(2)}) collective-permute-start(f32[128,128]{1,0:T(8,128)S(1)} %get-tuple-element.36), channel_id=1, source_target_pairs={{1,0},{2,1},{3,2},{4,3},{5,4},{6,5},{7,6},{8,7},{9,8},{10,9},{11,1... | collective-permute-start | bytes 196616 | tf_op jit(solution)/shard_map/ppermute | solution.py:403
  29.9 3.1 %collective-permute-start.2 = (f32[128,128]{1,0:T(8,128)S(1)}, f32[128,128]{1,0:T(8,128)S(1)}, u32[]{:S(2)}, u32[]{:S(2)}) collective-permute-start(f32[128,128]{1,0:T(8,128)S(1)} %get-tuple-element.36), channel_id=1, source_target_pairs={{0,1},{1,2},{2,3},{3,4},{4,5},{5,6},{6,7},{7,8},{8,9},{9,10},{10,1... | collective-permute-start | bytes 196616 | tf_op jit(solution)/shard_map/ppermute | solution.py:403
  33.0 3.4 %collective-permute-done.3.after_ref.refs_3_ = f32[128,128]{1,0:T(8,128)S(1)} collective-permute-done((f32[128,128]{1,0:T(8,128)S(1)}, f32[128,128]{1,0:T(8,128)S(1)}, u32[]{:S(2)}, u32[]{:S(2)}) %collective-permute-start.3) | collective-permute-done | bytes 65568 | tf_op jit(solution)/shard_map/ppermute | solution.py:403
  36.4 1.9 %collective-permute-done.2.before_ref.refs_2_ = f32[128,128]{1,0:T(8,128)S(1)} collective-permute-done((f32[128,128]{1,0:T(8,128)S(1)}, f32[128,128]{1,0:T(8,128)S(1)}, u32[]{:S(2)}, u32[]{:S(2)}) %collective-permute-start.2) | collective-permute-done | bytes 65568 | tf_op jit(solution)/shard_map/ppermute | solution.py:403
  38.2 0.0 all-to-all-done.refs_0_
  38.2 1.2 %shard_map.108 = f32[160,128]{1,0:T(8,128)} custom-call(f32[16,72,128]{2,1,0:T(8,128)S(1)} %all-to-all-done.refs_0_, f32[8,128]{1,0:T(8,128)S(1)} %get-tuple-element.39.edge_ref.refs_1_, f32[128,128]{1,0:T(8,128)S(1)} %collective-permute-done.2.before_ref.refs_2_, f32[128,128]{1,0:T(8,128)S(1)} %collective-permute-done.3.after_ref.refs_3_), custom_call_target="tpu_custom_call" | custom-call | tf_op jit(solution)/shard_map/pallas_call | solution.py:408
  39.5 22.7 %all-to-all-start.1 = ((f32[160,1,128]{2,1,0:T(1,128)}), f32[160,1,128]{2,1,0:T(1,128)S(1)}, u32[]{:S(2)}, u32[]{:S(2)}) async-start(f32[160,1,128]{2,1,0:T(1,128)} %bitcast.6), calls=%async_computation.1 | async-start | bytes 163840 | tf_op jit(solution)/shard_map/all_to_all | solution.py:409
  62.2 1.4 %shard_map.107 = (f32[3,125,1,128]{3,2,1,0:T(1,128)}, f32[8,128]{1,0:T(8,128)S(1)}, f32[8,128]{1,0:T(8,128)S(1)}) custom-call(s32[1,1]{1,0:T(1,128)S(6)} %copy.12.count_ref.refs_0_, f32[6,128,128]{2,1,0:T(8,128)S(1)} %get-tuple-element.23.field_ref, f32[3,128,128]{2,1,0:T(8,128)S(1)} %get-tuple-element.34.one_ref, ...), custom_call_target="tpu_custom_call" | custom-call | tf_op jit(solution)/shard_map/pallas_call | solution.py:410
  63.6 3.6 %all-to-all-done.1 = f32[160,1,128]{2,1,0:T(1,128)S(1)} async-done(((f32[160,1,128]{2,1,0:T(1,128)}), f32[160,1,128]{2,1,0:T(1,128)S(1)}, u32[]{:S(2)}, u32[]{:S(2)}) %all-to-all-start.1) | async-done | bytes 81952 | tf_op jit(solution)/shard_map/all_to_all | solution.py:409
  67.2 0.8 %shard_map.109 = f32[4,64]{1,0:T(4,128)} custom-call(f32[160,128]{1,0:T(8,128)S(1)} %bitcast.10, f32[8,128]{1,0:T(8,128)S(1)} %get-tuple-element.42.refs_1_, f32[8,128]{1,0:T(8,128)S(1)} %get-tuple-element.43.refs_2_), custom_call_target="tpu_custom_call" | custom-call | tf_op jit(solution)/shard_map/pallas_call | solution.py:417
Async XLA Ops:
  2.6 11.2 %collective-permute-start.1 = (f32[200,128]{1,0:T(8,128)S(1)}, f32[200,128]{1,0:T(8,128)S(1)}, u32[]{:S(2)}, u32[]{:S(2)}) collective-permute-start(f32[200,128]{1,0:T(8,128)S(1)} %get-tuple-element.27), channel_id=1, source_target_pairs={{1,0},{2,1},{3,2},{4,3},{5,4},{6,5},{7,6},{8,7},{9,8},{10,9},{11,1... | collective-permute-start | bytes 307208 | tf_op jit(solution)/shard_map/ppermute | solution.py:371
  10.2 8.7 %collective-permute-start = (f32[200,128]{1,0:T(8,128)S(1)}, f32[200,128]{1,0:T(8,128)S(1)}, u32[]{:S(2)}, u32[]{:S(2)}) collective-permute-start(f32[200,128]{1,0:T(8,128)S(1)} %get-tuple-element.27), channel_id=1, source_target_pairs={{0,1},{1,2},{2,3},{3,4},{4,5},{5,6},{6,7},{7,8},{8,9},{9,10},{10,1... | collective-permute-start | bytes 307208 | tf_op jit(solution)/shard_map/ppermute | solution.py:371
  21.1 17.2 %all-to-all-start = ((f32[16,72,128]{2,1,0:T(8,128)}), f32[16,72,128]{2,1,0:T(8,128)S(1)}, u32[]{:S(2)}, u32[]{:S(2)}) async-start(f32[16,72,128]{2,1,0:T(8,128)} %get-tuple-element.41), calls=%async_computation | async-start | bytes 1179648 | tf_op jit(solution)/shard_map/all_to_all | solution.py:401
  27.7 8.7 %collective-permute-start.3 = (f32[128,128]{1,0:T(8,128)S(1)}, f32[128,128]{1,0:T(8,128)S(1)}, u32[]{:S(2)}, u32[]{:S(2)}) collective-permute-start(f32[128,128]{1,0:T(8,128)S(1)} %get-tuple-element.36), channel_id=1, source_target_pairs={{1,0},{2,1},{3,2},{4,3},{5,4},{6,5},{7,6},{8,7},{9,8},{10,9},{11,1... | collective-permute-start | bytes 196616 | tf_op jit(solution)/shard_map/ppermute | solution.py:403
  29.9 8.3 %collective-permute-start.2 = (f32[128,128]{1,0:T(8,128)S(1)}, f32[128,128]{1,0:T(8,128)S(1)}, u32[]{:S(2)}, u32[]{:S(2)}) collective-permute-start(f32[128,128]{1,0:T(8,128)S(1)} %get-tuple-element.36), channel_id=1, source_target_pairs={{0,1},{1,2},{2,3},{3,4},{4,5},{5,6},{6,7},{7,8},{8,9},{9,10},{10,1... | collective-permute-start | bytes 196616 | tf_op jit(solution)/shard_map/ppermute | solution.py:403
  39.5 27.8 %all-to-all-start.1 = ((f32[160,1,128]{2,1,0:T(1,128)}), f32[160,1,128]{2,1,0:T(1,128)S(1)}, u32[]{:S(2)}, u32[]{:S(2)}) async-start(f32[160,1,128]{2,1,0:T(1,128)} %bitcast.6), calls=%async_computation.1 | async-start | bytes 163840 | tf_op jit(solution)/shard_map/all_to_all | solution.py:409

commit v9 on v8

--- a/solution.py
+++ b/solution.py
@@ -225,7 +225,7 @@
 
 def step_kernel(
     scale, n_mesh,
-    count_ref, partial_ref, kernel_ref, before_ref, after_ref, near_ref, stiff_ref, pick_ref, lift_ref,
+    count_ref, partial_ref, kernel_ref, after_ref, before_ref, near_ref, stiff_ref, pick_ref, lift_ref,
     project_ref, wanted_ref,
     forward_ref, strain_ref, rim_ref, edge_ref, chunk_ref,
 ):
@@ -251,7 +251,7 @@
         strain_ref[c] = strain[c]
 
 
-def dense_kernel(n_event, n_mesh, tile_width, first, parts_ref, edge_ref, before_ref, after_ref, out_ref):
+def dense_kernel(n_event, n_mesh, tile_width, first, parts_ref, edge_ref, after_ref, before_ref, out_ref):
     rows = 8 * n_event
     row = iota((rows, 128), 0)
     tile = (row % n_event + first) % n_event * (n_mesh * tile_width) + row // n_event - 2
@@ -368,7 +368,7 @@
         3,
         [pltpu.VMEM(x.shape, F32) for x in (forward, adjoint)] + [pltpu.SemaphoreType.DMA((3,))],
     )(counts, *inputs[:3])
-    before, after = lax.ppermute(rim, "mesh", up), lax.ppermute(rim, "mesh", down)
+    after, before = lax.ppermute(rim, "mesh", down), lax.ppermute(rim, "mesh", up)
     partial, kernel, turned, stiff, pick, lift, project, wanted, near, material = call(
         own_kernel,
         (
@@ -397,15 +397,15 @@
         (shape(3, 128, 128), shape(3, 128, 128), shape(128, 128), shape(8, 128), shape(n_mesh, 72, 128)),
         1,
         10,
-    )(counts, partial, kernel, before, after, near, stiff, pick, lift, project, wanted)
+    )(counts, partial, kernel, after, before, near, stiff, pick, lift, project, wanted)
     parts = lax.all_to_all(chunk, "mesh", 0, 0, tiled=True, axis_index_groups=[mesh_group])
 
-    before, after = lax.ppermute(rim_one, "mesh", up), lax.ppermute(rim_one, "mesh", down)
+    after, before = lax.ppermute(rim_one, "mesh", down), lax.ppermute(rim_one, "mesh", up)
 
     def dense(*refs):
         dense_kernel(n_event, n_mesh, tile_width, first_event, *refs)
 
-    partial = call(dense, shape(5 * n_event, 128), 0, 4)(parts, edge, before, after)
+    partial = call(dense, shape(5 * n_event, 128), 0, 4)(parts, edge, after, before)
     pieces = lax.all_to_all(partial.reshape(-1, 1, 128), "event", 0, 0, tiled=True, axis_index_groups=[event_group])
     final, table, is_open = call(last_kernel, (shape(3, NODES, 1, 128), shape(8, 128), shape(8, 128)), 1, 11)(
         counts, fields, one, strain, before, after, near, material, pick, lift, turned, edge

time: 68.5 us -> 65 us (0.949)
  waiting for transfers between devices: 14 us -> 11.4 us
  starting transfers between devices: 44.2 us -> 43.4 us
    ppermute x1, waiting for transfers between devices: 1.86 us -> 7.76 us  [per_device(): lax.ppermute(rim_one, 'mesh', up)]
    ppermute x1, waiting for transfers between devices: 5.18 us -> 0.01 us  [per_device(): lax.ppermute(rim, 'mesh', up)]
    ppermute x1, waiting for transfers between devices: 3.37 us -> 0.01 us  [per_device(): lax.ppermute(rim_one, 'mesh', down)]
    all_to_all x1, starting transfers between devices: 22.7 us -> 20 us  [per_device(): lax.all_to_all(partial.reshape(-1, 1, 128), 'event', 0, 0, tiled=True, ax...]
    ppermute x1, starting transfers between devices: 1.92 us -> 4.03 us  [per_device(): lax.ppermute(rim, 'mesh', up)]
    ppermute x1, starting transfers between devices: 7.67 us -> 5.55 us  [per_device(): lax.ppermute(rim, 'mesh', down)]
    all_to_all x1, starting transfers between devices: 6.66 us -> 8.52 us  [per_device(): lax.all_to_all(chunk, 'mesh', 0, 0, tiled=True, axis_index_groups=[mesh_g...]
  transfers between devices with their start and end apart: 6 -> 6, of which waited for: 4 -> 2; matrix products, arithmetic and copies ran while one was open for 0% -> 0% of each run, Pallas kernels for 4% -> 5%
where the time goes in v9:
time: 65 us; the launch traced here: 64.6 us
  starting transfers between devices  43.4 us (67%)
  waiting for transfers between devices  11.4 us (18%)
  Pallas kernels  8.43 us (13%)
  between operations  1.35 us (2%)
    all_to_all x1, starting transfers between devices, per_device(): lax.all_to_all(partial.reshape(-1, 1, 128), 'event', 0, 0, tiled=True, ax...  20 us
    all_to_all x1, starting transfers between devices, per_device(): lax.all_to_all(chunk, 'mesh', 0, 0, tiled=True, axis_index_groups=[mesh_g...  8.52 us
    ppermute x1, waiting for transfers between devices, per_device(): lax.ppermute(rim_one, 'mesh', up)  7.76 us
    ppermute x1, starting transfers between devices, per_device(): lax.ppermute(rim, 'mesh', down)  5.55 us
    ppermute x1, starting transfers between devices, per_device(): lax.ppermute(rim, 'mesh', up)  4.03 us
    all_to_all x1, waiting for transfers between devices, per_device(): lax.all_to_all(partial.reshape(-1, 1, 128), 'event', 0, 0, tiled=True, ax...  3.6 us
    ppermute x1, starting transfers between devices, per_device(): lax.ppermute(rim_one, 'mesh', up)  3.09 us
    ppermute x1, starting transfers between devices, per_device(): lax.ppermute(rim_one, 'mesh', down)  2.18 us
  transfers between devices with their start and end apart: 6, of which 2 were waited for; matrix products, arithmetic and copies ran while one was open for 0% of the time, Pallas kernels for 5%

profile of v9, /device:TPU:1, one launch (start us, length us, event | category | flops | bytes accessed | tf_op | source)
XLA Modules:
  0.0 64.6 jit_solution(2069379568856652732)
XLA Ops:
  1.3 1.3 %shard_map.104 = (f32[200,128]{1,0:T(8,128)S(1)}, f32[6,128,128]{2,1,0:T(8,128)S(1)}, f32[4,4]{1,0:T(4,128)S(1)}) custom-call(s32[1,1]{1,0:T(1,128)S(6)} %copy.12.count_ref.refs_0_, f32[3,125,1,128]{3,2,1,0:T(1,128)} %bitcast.11, f32[3,125,1,128]{3,2,1,0:T(1,128)} %bitcast.12, f32[4,4]{1,0:T(4,128)} %smooth_ref.1), custom_call_target="tpu_custom_call" | custom-call | tf_op jit(solution)/shard_map/pallas_call | solution.py:363
  2.6 4.0 %collective-permute-start.1 = (f32[200,128]{1,0:T(8,128)S(1)}, f32[200,128]{1,0:T(8,128)S(1)}, u32[]{:S(2)}, u32[]{:S(2)}) collective-permute-start(f32[200,128]{1,0:T(8,128)S(1)} %get-tuple-element.27), channel_id=1, source_target_pairs={{0,1},{1,2},{2,3},{3,4},{4,5},{5,6},{6,7},{7,8},{8,9},{9,10},{10,1... | collective-permute-start | bytes 307208 | tf_op jit(solution)/shard_map/ppermute | solution.py:371
  6.6 5.6 %collective-permute-start = (f32[200,128]{1,0:T(8,128)S(1)}, f32[200,128]{1,0:T(8,128)S(1)}, u32[]{:S(2)}, u32[]{:S(2)}) collective-permute-start(f32[200,128]{1,0:T(8,128)S(1)} %get-tuple-element.27), channel_id=1, source_target_pairs={{1,0},{2,1},{3,2},{4,3},{5,4},{6,5},{7,6},{8,7},{9,8},{10,9},{11,1... | collective-permute-start | bytes 307208 | tf_op jit(solution)/shard_map/ppermute | solution.py:371
  12.2 1.6 %shard_map.105 = (f32[6,128,128]{2,1,0:T(8,128)S(1)}, f32[128,128]{1,0:T(8,128)S(1)}, f32[8,128]{1,0:T(8,128)S(1)}, bf16[2,128,128]{2,1,0:T(8,128)(2,1)S(1)}, bf...) custom-call(s32[1,1]{1,0:T(1,128)S(6)} %copy.12.count_ref.refs_0_, ...), custom_call_target="tpu_custom_call" | custom-call | tf_op jit(solution)/shard_map/pallas_call | solution.py:372
  13.8 0.0 collective-permute-done.1.refs_4_
  13.8 0.0 collective-permute-done.refs_3_
  13.8 2.1 %shard_map.106 = (f32[3,128,128]{2,1,0:T(8,128)S(1)}, f32[3,128,128]{2,1,0:T(8,128)S(1)}, f32[128,128]{1,0:T(8,128)S(1)}, f32[8,128]{1,0:T(8,128)S(1)}, f32[16,72,128]{2,1,0:T(8,128)}) custom-call(s32[1,1]{1,0:T(1,128)S(6)} %copy.12.count_ref.refs_0_, f32[6,128,128]{2,1,0:T(8,128)S(1)} %get-tuple-element.25.refs_1_, ...), custom_call_target="tpu_custom_call" | custom-call | tf_op jit(solution)/shard_map/pallas_call | solution.py:395
  15.9 8.5 %all-to-all-start = ((f32[16,72,128]{2,1,0:T(8,128)}), f32[16,72,128]{2,1,0:T(8,128)S(1)}, u32[]{:S(2)}, u32[]{:S(2)}) async-start(f32[16,72,128]{2,1,0:T(8,128)} %get-tuple-element.41), calls=%async_computation | async-start | bytes 1179648 | tf_op jit(solution)/shard_map/all_to_all | solution.py:401
  24.4 2.2 %collective-permute-start.3 = (f32[128,128]{1,0:T(8,128)S(1)}, f32[128,128]{1,0:T(8,128)S(1)}, u32[]{:S(2)}, u32[]{:S(2)}) collective-permute-start(f32[128,128]{1,0:T(8,128)S(1)} %get-tuple-element.36), channel_id=1, source_target_pairs={{1,0},{2,1},{3,2},{4,3},{5,4},{6,5},{7,6},{8,7},{9,8},{10,9},{11,1... | collective-permute-start | bytes 196616 | tf_op jit(solution)/shard_map/ppermute | solution.py:403
  26.6 3.1 %collective-permute-start.2 = (f32[128,128]{1,0:T(8,128)S(1)}, f32[128,128]{1,0:T(8,128)S(1)}, u32[]{:S(2)}, u32[]{:S(2)}) collective-permute-start(f32[128,128]{1,0:T(8,128)S(1)} %get-tuple-element.36), channel_id=1, source_target_pairs={{0,1},{1,2},{2,3},{3,4},{4,5},{5,6},{6,7},{7,8},{8,9},{9,10},{10,1... | collective-permute-start | bytes 196616 | tf_op jit(solution)/shard_map/ppermute | solution.py:403
  29.7 0.0 collective-permute-done.3.after_ref.refs_2_
  29.7 7.8 %collective-permute-done.2.before_ref.refs_3_ = f32[128,128]{1,0:T(8,128)S(1)} collective-permute-done((f32[128,128]{1,0:T(8,128)S(1)}, f32[128,128]{1,0:T(8,128)S(1)}, u32[]{:S(2)}, u32[]{:S(2)}) %collective-permute-start.2) | collective-permute-done | bytes 65568 | tf_op jit(solution)/shard_map/ppermute | solution.py:403
  37.5 0.0 all-to-all-done.refs_0_
  37.5 1.2 %shard_map.108 = f32[160,128]{1,0:T(8,128)} custom-call(f32[16,72,128]{2,1,0:T(8,128)S(1)} %all-to-all-done.refs_0_, f32[8,128]{1,0:T(8,128)S(1)} %get-tuple-element.39.edge_ref.refs_1_, f32[128,128]{1,0:T(8,128)S(1)} %collective-permute-done.3.after_ref.refs_2_, f32[128,128]{1,0:T(8,128)S(1)} %collective-permute-done.2.before_ref.refs_3_), custom_call_target="tpu_custom_call" | custom-call | tf_op jit(solution)/shard_map/pallas_call | solution.py:408
  38.7 20.0 %all-to-all-start.1 = ((f32[160,1,128]{2,1,0:T(1,128)}), f32[160,1,128]{2,1,0:T(1,128)S(1)}, u32[]{:S(2)}, u32[]{:S(2)}) async-start(f32[160,1,128]{2,1,0:T(1,128)} %bitcast.6), calls=%async_computation.1 | async-start | bytes 163840 | tf_op jit(solution)/shard_map/all_to_all | solution.py:409
  58.8 1.4 %shard_map.107 = (f32[3,125,1,128]{3,2,1,0:T(1,128)}, f32[8,128]{1,0:T(8,128)S(1)}, f32[8,128]{1,0:T(8,128)S(1)}) custom-call(s32[1,1]{1,0:T(1,128)S(6)} %copy.12.count_ref.refs_0_, f32[6,128,128]{2,1,0:T(8,128)S(1)} %get-tuple-element.23.field_ref, f32[3,128,128]{2,1,0:T(8,128)S(1)} %get-tuple-element.34.one_ref, ...), custom_call_target="tpu_custom_call" | custom-call | tf_op jit(solution)/shard_map/pallas_call | solution.py:410
  60.2 3.6 %all-to-all-done.1 = f32[160,1,128]{2,1,0:T(1,128)S(1)} async-done(((f32[160,1,128]{2,1,0:T(1,128)}), f32[160,1,128]{2,1,0:T(1,128)S(1)}, u32[]{:S(2)}, u32[]{:S(2)}) %all-to-all-start.1) | async-done | bytes 81952 | tf_op jit(solution)/shard_map/all_to_all | solution.py:409
  63.8 0.8 %shard_map.109 = f32[4,64]{1,0:T(4,128)} custom-call(f32[160,128]{1,0:T(8,128)S(1)} %bitcast.10, f32[8,128]{1,0:T(8,128)S(1)} %get-tuple-element.42.refs_1_, f32[8,128]{1,0:T(8,128)S(1)} %get-tuple-element.43.refs_2_), custom_call_target="tpu_custom_call" | custom-call | tf_op jit(solution)/shard_map/pallas_call | solution.py:417
Async XLA Ops:
  2.6 11.2 %collective-permute-start.1 = (f32[200,128]{1,0:T(8,128)S(1)}, f32[200,128]{1,0:T(8,128)S(1)}, u32[]{:S(2)}, u32[]{:S(2)}) collective-permute-start(f32[200,128]{1,0:T(8,128)S(1)} %get-tuple-element.27), channel_id=1, source_target_pairs={{0,1},{1,2},{2,3},{3,4},{4,5},{5,6},{6,7},{7,8},{8,9},{9,10},{10,1... | collective-permute-start | bytes 307208 | tf_op jit(solution)/shard_map/ppermute | solution.py:371
  6.6 7.2 %collective-permute-start = (f32[200,128]{1,0:T(8,128)S(1)}, f32[200,128]{1,0:T(8,128)S(1)}, u32[]{:S(2)}, u32[]{:S(2)}) collective-permute-start(f32[200,128]{1,0:T(8,128)S(1)} %get-tuple-element.27), channel_id=1, source_target_pairs={{1,0},{2,1},{3,2},{4,3},{5,4},{6,5},{7,6},{8,7},{9,8},{10,9},{11,1... | collective-permute-start | bytes 307208 | tf_op jit(solution)/shard_map/ppermute | solution.py:371
  15.9 21.6 %all-to-all-start = ((f32[16,72,128]{2,1,0:T(8,128)}), f32[16,72,128]{2,1,0:T(8,128)S(1)}, u32[]{:S(2)}, u32[]{:S(2)}) async-start(f32[16,72,128]{2,1,0:T(8,128)} %get-tuple-element.41), calls=%async_computation | async-start | bytes 1179648 | tf_op jit(solution)/shard_map/all_to_all | solution.py:401
  24.4 5.3 %collective-permute-start.3 = (f32[128,128]{1,0:T(8,128)S(1)}, f32[128,128]{1,0:T(8,128)S(1)}, u32[]{:S(2)}, u32[]{:S(2)}) collective-permute-start(f32[128,128]{1,0:T(8,128)S(1)} %get-tuple-element.36), channel_id=1, source_target_pairs={{1,0},{2,1},{3,2},{4,3},{5,4},{6,5},{7,6},{8,7},{9,8},{10,9},{11,1... | collective-permute-start | bytes 196616 | tf_op jit(solution)/shard_map/ppermute | solution.py:403
  26.6 10.9 %collective-permute-start.2 = (f32[128,128]{1,0:T(8,128)S(1)}, f32[128,128]{1,0:T(8,128)S(1)}, u32[]{:S(2)}, u32[]{:S(2)}) collective-permute-start(f32[128,128]{1,0:T(8,128)S(1)} %get-tuple-element.36), channel_id=1, source_target_pairs={{0,1},{1,2},{2,3},{3,4},{4,5},{5,6},{6,7},{7,8},{8,9},{9,10},{10,1... | collective-permute-start | bytes 196616 | tf_op jit(solution)/shard_map/ppermute | solution.py:403
  38.7 25.1 %all-to-all-start.1 = ((f32[160,1,128]{2,1,0:T(1,128)}), f32[160,1,128]{2,1,0:T(1,128)S(1)}, u32[]{:S(2)}, u32[]{:S(2)}) async-start(f32[160,1,128]{2,1,0:T(1,128)} %bitcast.6), calls=%async_computation.1 | async-start | bytes 163840 | tf_op jit(solution)/shard_map/all_to_all | solution.py:409

commit v10 on v9

--- a/solution.py
+++ b/solution.py
@@ -276,7 +276,7 @@
 
 
 def last_kernel(
-    count_ref, field_ref, one_ref, strain_ref, before_ref, after_ref, near_ref, material_ref, pick_ref, lift_ref,
+    count_ref, field_ref, one_ref, strain_ref, after_ref, before_ref, near_ref, material_ref, pick_ref, lift_ref,
     turned_ref, edge_ref,
     final_ref, table_ref, open_ref,
 ):
@@ -408,7 +408,7 @@
     partial = call(dense, shape(5 * n_event, 128), 0, 4)(parts, edge, after, before)
     pieces = lax.all_to_all(partial.reshape(-1, 1, 128), "event", 0, 0, tiled=True, axis_index_groups=[event_group])
     final, table, is_open = call(last_kernel, (shape(3, NODES, 1, 128), shape(8, 128), shape(8, 128)), 1, 11)(
-        counts, fields, one, strain, before, after, near, material, pick, lift, turned, edge
+        counts, fields, one, strain, after, before, near, material, pick, lift, turned, edge
     )
 
     def smooth(*refs):

time: 65 us -> 64.1 us (0.986)
  waiting for transfers between devices: 11.4 us -> 6.31 us
  starting transfers between devices: 43.4 us -> 47.6 us
    ppermute x1, waiting for transfers between devices: 7.76 us -> 0.01 us  [per_device(): lax.ppermute(rim_one, 'mesh', up)]
    ppermute x1, starting transfers between devices: 2.18 us -> 6.68 us  [per_device(): lax.ppermute(rim_one, 'mesh', down)]
    ppermute x1, waiting for transfers between devices: 0.01 us -> 2.66 us  [per_device(): lax.ppermute(rim_one, 'mesh', down)]
    ppermute x1, starting transfers between devices: 3.09 us -> 1.91 us  [per_device(): lax.ppermute(rim_one, 'mesh', up)]
    all_to_all x1, starting transfers between devices: 20 us -> 20.9 us  [per_device(): lax.all_to_all(partial.reshape(-1, 1, 128), 'event', 0, 0, tiled=True, ax...]
where the time goes in v10:
time: 64.1 us; the launch traced here: 63.7 us
  starting transfers between devices  47.6 us (74%)
  Pallas kernels  8.43 us (13%)
  waiting for transfers between devices  6.31 us (10%)
  between operations  1.35 us (2%)
    all_to_all x1, starting transfers between devices, per_device(): lax.all_to_all(partial.reshape(-1, 1, 128), 'event', 0, 0, tiled=True, ax...  20.9 us
    all_to_all x1, starting transfers between devices, per_device(): lax.all_to_all(chunk, 'mesh', 0, 0, tiled=True, axis_index_groups=[mesh_g...  8.52 us
    ppermute x1, starting transfers between devices, per_device(): lax.ppermute(rim_one, 'mesh', down)  6.68 us
    ppermute x1, starting transfers between devices, per_device(): lax.ppermute(rim, 'mesh', down)  5.55 us
    ppermute x1, starting transfers between devices, per_device(): lax.ppermute(rim, 'mesh', up)  4.03 us
    all_to_all x1, waiting for transfers between devices, per_device(): lax.all_to_all(partial.reshape(-1, 1, 128), 'event', 0, 0, tiled=True, ax...  3.6 us
    ppermute x1, waiting for transfers between devices, per_device(): lax.ppermute(rim_one, 'mesh', down)  2.66 us
    pallas_call x1, Pallas kernels, per_device(): call(one_step, (shape(3, 128, 128), shape(3, 128, 128), shape(128, 128),...  2.09 us
  transfers between devices with their start and end apart: 6, of which 2 were waited for; matrix products, arithmetic and copies ran while one was open for 0% of the time, Pallas kernels for 5%

profile of v10, /device:TPU:1, one launch (start us, length us, event | category | flops | bytes accessed | tf_op | source)
XLA Modules:
  0.0 63.7 jit_solution(15302393748987673460)
XLA Ops:
  1.3 1.3 %shard_map.104 = (f32[200,128]{1,0:T(8,128)S(1)}, f32[6,128,128]{2,1,0:T(8,128)S(1)}, f32[4,4]{1,0:T(4,128)S(1)}) custom-call(s32[1,1]{1,0:T(1,128)S(6)} %copy.12.count_ref.refs_0_, f32[3,125,1,128]{3,2,1,0:T(1,128)} %bitcast.11, f32[3,125,1,128]{3,2,1,0:T(1,128)} %bitcast.12, f32[4,4]{1,0:T(4,128)} %smooth_ref.1), custom_call_target="tpu_custom_call" | custom-call | tf_op jit(solution)/shard_map/pallas_call | solution.py:363
  2.6 4.0 %collective-permute-start.1 = (f32[200,128]{1,0:T(8,128)S(1)}, f32[200,128]{1,0:T(8,128)S(1)}, u32[]{:S(2)}, u32[]{:S(2)}) collective-permute-start(f32[200,128]{1,0:T(8,128)S(1)} %get-tuple-element.27), channel_id=1, source_target_pairs={{0,1},{1,2},{2,3},{3,4},{4,5},{5,6},{6,7},{7,8},{8,9},{9,10},{10,1... | collective-permute-start | bytes 307208 | tf_op jit(solution)/shard_map/ppermute | solution.py:371
  6.6 5.6 %collective-permute-start = (f32[200,128]{1,0:T(8,128)S(1)}, f32[200,128]{1,0:T(8,128)S(1)}, u32[]{:S(2)}, u32[]{:S(2)}) collective-permute-start(f32[200,128]{1,0:T(8,128)S(1)} %get-tuple-element.27), channel_id=1, source_target_pairs={{1,0},{2,1},{3,2},{4,3},{5,4},{6,5},{7,6},{8,7},{9,8},{10,9},{11,1... | collective-permute-start | bytes 307208 | tf_op jit(solution)/shard_map/ppermute | solution.py:371
  12.2 1.6 %shard_map.105 = (f32[6,128,128]{2,1,0:T(8,128)S(1)}, f32[128,128]{1,0:T(8,128)S(1)}, f32[8,128]{1,0:T(8,128)S(1)}, bf16[2,128,128]{2,1,0:T(8,128)(2,1)S(1)}, bf...) custom-call(s32[1,1]{1,0:T(1,128)S(6)} %copy.12.count_ref.refs_0_, ...), custom_call_target="tpu_custom_call" | custom-call | tf_op jit(solution)/shard_map/pallas_call | solution.py:372
  13.8 0.0 collective-permute-done.1.refs_4_
  13.8 0.0 collective-permute-done.refs_3_
  13.8 2.1 %shard_map.106 = (f32[3,128,128]{2,1,0:T(8,128)S(1)}, f32[3,128,128]{2,1,0:T(8,128)S(1)}, f32[128,128]{1,0:T(8,128)S(1)}, f32[8,128]{1,0:T(8,128)S(1)}, f32[16,72,128]{2,1,0:T(8,128)}) custom-call(s32[1,1]{1,0:T(1,128)S(6)} %copy.12.count_ref.refs_0_, f32[6,128,128]{2,1,0:T(8,128)S(1)} %get-tuple-element.25.refs_1_, ...), custom_call_target="tpu_custom_call" | custom-call | tf_op jit(solution)/shard_map/pallas_call | solution.py:395
  15.9 8.5 %all-to-all-start = ((f32[16,72,128]{2,1,0:T(8,128)}), f32[16,72,128]{2,1,0:T(8,128)S(1)}, u32[]{:S(2)}, u32[]{:S(2)}) async-start(f32[16,72,128]{2,1,0:T(8,128)} %get-tuple-element.41), calls=%async_computation | async-start | bytes 1179648 | tf_op jit(solution)/shard_map/all_to_all | solution.py:401
  24.4 1.9 %collective-permute-start.3 = (f32[128,128]{1,0:T(8,128)S(1)}, f32[128,128]{1,0:T(8,128)S(1)}, u32[]{:S(2)}, u32[]{:S(2)}) collective-permute-start(f32[128,128]{1,0:T(8,128)S(1)} %get-tuple-element.36), channel_id=1, source_target_pairs={{0,1},{1,2},{2,3},{3,4},{4,5},{5,6},{6,7},{7,8},{8,9},{9,10},{10,1... | collective-permute-start | bytes 196616 | tf_op jit(solution)/shard_map/ppermute | solution.py:403
  26.3 6.7 %collective-permute-start.2 = (f32[128,128]{1,0:T(8,128)S(1)}, f32[128,128]{1,0:T(8,128)S(1)}, u32[]{:S(2)}, u32[]{:S(2)}) collective-permute-start(f32[128,128]{1,0:T(8,128)S(1)} %get-tuple-element.36), channel_id=1, source_target_pairs={{1,0},{2,1},{3,2},{4,3},{5,4},{6,5},{7,6},{8,7},{9,8},{10,9},{11,1... | collective-permute-start | bytes 196616 | tf_op jit(solution)/shard_map/ppermute | solution.py:403
  33.0 0.0 collective-permute-done.3.before_ref.refs_3_
  33.0 2.7 %collective-permute-done.2.after_ref.refs_2_ = f32[128,128]{1,0:T(8,128)S(1)} collective-permute-done((f32[128,128]{1,0:T(8,128)S(1)}, f32[128,128]{1,0:T(8,128)S(1)}, u32[]{:S(2)}, u32[]{:S(2)}) %collective-permute-start.2) | collective-permute-done | bytes 65568 | tf_op jit(solution)/shard_map/ppermute | solution.py:403
  35.7 0.0 all-to-all-done.refs_0_
  35.7 1.2 %shard_map.108 = f32[160,128]{1,0:T(8,128)} custom-call(f32[16,72,128]{2,1,0:T(8,128)S(1)} %all-to-all-done.refs_0_, f32[8,128]{1,0:T(8,128)S(1)} %get-tuple-element.39.edge_ref.refs_1_, f32[128,128]{1,0:T(8,128)S(1)} %collective-permute-done.2.after_ref.refs_2_, f32[128,128]{1,0:T(8,128)S(1)} %collective-permute-done.3.before_ref.refs_3_), custom_call_target="tpu_custom_call" | custom-call | tf_op jit(solution)/shard_map/pallas_call | solution.py:408
  36.9 20.9 %all-to-all-start.1 = ((f32[160,1,128]{2,1,0:T(1,128)}), f32[160,1,128]{2,1,0:T(1,128)S(1)}, u32[]{:S(2)}, u32[]{:S(2)}) async-start(f32[160,1,128]{2,1,0:T(1,128)} %bitcast.6), calls=%async_computation.1 | async-start | bytes 163840 | tf_op jit(solution)/shard_map/all_to_all | solution.py:409
  57.9 1.4 %shard_map.107 = (f32[3,125,1,128]{3,2,1,0:T(1,128)}, f32[8,128]{1,0:T(8,128)S(1)}, f32[8,128]{1,0:T(8,128)S(1)}) custom-call(s32[1,1]{1,0:T(1,128)S(6)} %copy.12.count_ref.refs_0_, f32[6,128,128]{2,1,0:T(8,128)S(1)} %get-tuple-element.23.field_ref, f32[3,128,128]{2,1,0:T(8,128)S(1)} %get-tuple-element.34.one_ref, ...), custom_call_target="tpu_custom_call" | custom-call | tf_op jit(solution)/shard_map/pallas_call | solution.py:410
  59.3 3.6 %all-to-all-done.1 = f32[160,1,128]{2,1,0:T(1,128)S(1)} async-done(((f32[160,1,128]{2,1,0:T(1,128)}), f32[160,1,128]{2,1,0:T(1,128)S(1)}, u32[]{:S(2)}, u32[]{:S(2)}) %all-to-all-start.1) | async-done | bytes 81952 | tf_op jit(solution)/shard_map/all_to_all | solution.py:409
  62.9 0.8 %shard_map.109 = f32[4,64]{1,0:T(4,128)} custom-call(f32[160,128]{1,0:T(8,128)S(1)} %bitcast.10, f32[8,128]{1,0:T(8,128)S(1)} %get-tuple-element.42.refs_1_, f32[8,128]{1,0:T(8,128)S(1)} %get-tuple-element.43.refs_2_), custom_call_target="tpu_custom_call" | custom-call | tf_op jit(solution)/shard_map/pallas_call | solution.py:417
Async XLA Ops:
  2.6 11.2 %collective-permute-start.1 = (f32[200,128]{1,0:T(8,128)S(1)}, f32[200,128]{1,0:T(8,128)S(1)}, u32[]{:S(2)}, u32[]{:S(2)}) collective-permute-start(f32[200,128]{1,0:T(8,128)S(1)} %get-tuple-element.27), channel_id=1, source_target_pairs={{0,1},{1,2},{2,3},{3,4},{4,5},{5,6},{6,7},{7,8},{8,9},{9,10},{10,1... | collective-permute-start | bytes 307208 | tf_op jit(solution)/shard_map/ppermute | solution.py:371
  6.6 7.2 %collective-permute-start = (f32[200,128]{1,0:T(8,128)S(1)}, f32[200,128]{1,0:T(8,128)S(1)}, u32[]{:S(2)}, u32[]{:S(2)}) collective-permute-start(f32[200,128]{1,0:T(8,128)S(1)} %get-tuple-element.27), channel_id=1, source_target_pairs={{1,0},{2,1},{3,2},{4,3},{5,4},{6,5},{7,6},{8,7},{9,8},{10,9},{11,1... | collective-permute-start | bytes 307208 | tf_op jit(solution)/shard_map/ppermute | solution.py:371
  15.9 19.8 %all-to-all-start = ((f32[16,72,128]{2,1,0:T(8,128)}), f32[16,72,128]{2,1,0:T(8,128)S(1)}, u32[]{:S(2)}, u32[]{:S(2)}) async-start(f32[16,72,128]{2,1,0:T(8,128)} %get-tuple-element.41), calls=%async_computation | async-start | bytes 1179648 | tf_op jit(solution)/shard_map/all_to_all | solution.py:401
  24.4 8.6 %collective-permute-start.3 = (f32[128,128]{1,0:T(8,128)S(1)}, f32[128,128]{1,0:T(8,128)S(1)}, u32[]{:S(2)}, u32[]{:S(2)}) collective-permute-start(f32[128,128]{1,0:T(8,128)S(1)} %get-tuple-element.36), channel_id=1, source_target_pairs={{0,1},{1,2},{2,3},{3,4},{4,5},{5,6},{6,7},{7,8},{8,9},{9,10},{10,1... | collective-permute-start | bytes 196616 | tf_op jit(solution)/shard_map/ppermute | solution.py:403
  26.3 9.4 %collective-permute-start.2 = (f32[128,128]{1,0:T(8,128)S(1)}, f32[128,128]{1,0:T(8,128)S(1)}, u32[]{:S(2)}, u32[]{:S(2)}) collective-permute-start(f32[128,128]{1,0:T(8,128)S(1)} %get-tuple-element.36), channel_id=1, source_target_pairs={{1,0},{2,1},{3,2},{4,3},{5,4},{6,5},{7,6},{8,7},{9,8},{10,9},{11,1... | collective-permute-start | bytes 196616 | tf_op jit(solution)/shard_map/ppermute | solution.py:403
  36.9 25.9 %all-to-all-start.1 = ((f32[160,1,128]{2,1,0:T(1,128)}), f32[160,1,128]{2,1,0:T(1,128)S(1)}, u32[]{:S(2)}, u32[]{:S(2)}) async-start(f32[160,1,128]{2,1,0:T(1,128)} %bitcast.6), calls=%async_computation.1 | async-start | bytes 163840 | tf_op jit(solution)/shard_map/all_to_all | solution.py:409

commit v11 on v10

--- a/solution.py
+++ b/solution.py
@@ -251,7 +251,7 @@
         strain_ref[c] = strain[c]
 
 
-def dense_kernel(n_event, n_mesh, tile_width, first, parts_ref, edge_ref, after_ref, before_ref, out_ref):
+def dense_kernel(n_event, n_mesh, tile_width, first, parts_ref, edge_ref, before_ref, out_ref):
     rows = 8 * n_event
     row = iota((rows, 128), 0)
     tile = (row % n_event + first) % n_event * (n_mesh * tile_width) + row // n_event - 2
@@ -400,13 +400,15 @@
     )(counts, partial, kernel, after, before, near, stiff, pick, lift, project, wanted)
     parts = lax.all_to_all(chunk, "mesh", 0, 0, tiled=True, axis_index_groups=[mesh_group])
 
-    after, before = lax.ppermute(rim_one, "mesh", down), lax.ppermute(rim_one, "mesh", up)
+    before = lax.ppermute(rim_one, "mesh", up)
 
     def dense(*refs):
         dense_kernel(n_event, n_mesh, tile_width, first_event, *refs)
 
-    partial = call(dense, shape(5 * n_event, 128), 0, 4)(parts, edge, after, before)
+    partial = call(dense, shape(5 * n_event, 128), 0, 3)(parts, edge, before)
     pieces = lax.all_to_all(partial.reshape(-1, 1, 128), "event", 0, 0, tiled=True, axis_index_groups=[event_group])
+    rim_one, _ = lax.optimization_barrier((rim_one, partial))
+    after = lax.ppermute(rim_one, "mesh", down)
     final, table, is_open = call(last_kernel, (shape(3, NODES, 1, 128), shape(8, 128), shape(8, 128)), 1, 11)(
         counts, fields, one, strain, after, before, near, material, pick, lift, turned, edge
     )

time: 64.1 us -> 64 us (level)
  starting transfers between devices: 47.6 us -> 44.6 us
  waiting for transfers between devices: 6.31 us -> 9.19 us
    ppermute x2, waiting for transfers between devices: 2.67 us -> 9.14 us  [the longest x1 6.4 us: per_device(): before = lax.ppermute(rim_one, 'mesh', up)]
    ppermute x2, starting transfers between devices: 8.59 us -> 4.18 us  [the longest x1 2.27 us: per_device(): after = lax.ppermute(rim_one, 'mesh', down)]
    all_to_all x1, waiting for transfers between devices: 3.6 us -> 0.01 us  [per_device(): lax.all_to_all(partial.reshape(-1, 1, 128), 'event', 0, 0, tiled=True, ax...]
    all_to_all x1, starting transfers between devices: 20.9 us -> 22.3 us  [per_device(): lax.all_to_all(partial.reshape(-1, 1, 128), 'event', 0, 0, tiled=True, ax...]
where the time goes in v11:
time: 64 us; the launch traced here: 63.5 us
  starting transfers between devices  44.6 us (70%)
  waiting for transfers between devices  9.19 us (14%)
  Pallas kernels  8.43 us (13%)
  between operations  1.34 us (2%)
    all_to_all x1, starting transfers between devices, per_device(): lax.all_to_all(partial.reshape(-1, 1, 128), 'event', 0, 0, tiled=True, ax...  22.3 us
    all_to_all x1, starting transfers between devices, per_device(): lax.all_to_all(chunk, 'mesh', 0, 0, tiled=True, axis_index_groups=[mesh_g...  8.52 us
    ppermute x1, waiting for transfers between devices, per_device(): before = lax.ppermute(rim_one, 'mesh', up)  6.4 us
    ppermute x1, starting transfers between devices, per_device(): lax.ppermute(rim, 'mesh', down)  5.55 us
    ppermute x1, starting transfers between devices, per_device(): lax.ppermute(rim, 'mesh', up)  4.03 us
    ppermute x1, waiting for transfers between devices, per_device(): after = lax.ppermute(rim_one, 'mesh', down)  2.74 us
    ppermute x1, starting transfers between devices, per_device(): after = lax.ppermute(rim_one, 'mesh', down)  2.27 us
    pallas_call x1, Pallas kernels, per_device(): call(one_step, (shape(3, 128, 128), shape(3, 128, 128), shape(128, 128),...  2.09 us
  transfers between devices with their start and end apart: 6, of which 2 were waited for; matrix products, arithmetic and copies ran while one was open for 0% of the time, Pallas kernels for 5%

profile of v11, /device:TPU:1, one launch (start us, length us, event | category | flops | bytes accessed | tf_op | source)
XLA Modules:
  0.0 63.5 jit_solution(1947155111488328753)
XLA Ops:
  1.3 1.3 %shard_map.104 = (f32[200,128]{1,0:T(8,128)S(1)}, f32[6,128,128]{2,1,0:T(8,128)S(1)}, f32[4,4]{1,0:T(4,128)S(1)}) custom-call(s32[1,1]{1,0:T(1,128)S(6)} %copy.12.count_ref.refs_0_, f32[3,125,1,128]{3,2,1,0:T(1,128)} %bitcast.11, f32[3,125,1,128]{3,2,1,0:T(1,128)} %bitcast.12, f32[4,4]{1,0:T(4,128)} %smooth_ref.1), custom_call_target="tpu_custom_call" | custom-call | tf_op jit(solution)/shard_map/pallas_call | solution.py:363
  2.6 4.0 %collective-permute-start.1 = (f32[200,128]{1,0:T(8,128)S(1)}, f32[200,128]{1,0:T(8,128)S(1)}, u32[]{:S(2)}, u32[]{:S(2)}) collective-permute-start(f32[200,128]{1,0:T(8,128)S(1)} %get-tuple-element.28), channel_id=1, source_target_pairs={{0,1},{1,2},{2,3},{3,4},{4,5},{5,6},{6,7},{7,8},{8,9},{9,10},{10,1... | collective-permute-start | bytes 307208 | tf_op jit(solution)/shard_map/ppermute | solution.py:371
  6.6 5.6 %collective-permute-start = (f32[200,128]{1,0:T(8,128)S(1)}, f32[200,128]{1,0:T(8,128)S(1)}, u32[]{:S(2)}, u32[]{:S(2)}) collective-permute-start(f32[200,128]{1,0:T(8,128)S(1)} %get-tuple-element.28), channel_id=1, source_target_pairs={{1,0},{2,1},{3,2},{4,3},{5,4},{6,5},{7,6},{8,7},{9,8},{10,9},{11,1... | collective-permute-start | bytes 307208 | tf_op jit(solution)/shard_map/ppermute | solution.py:371
  12.2 1.6 %shard_map.105 = (f32[6,128,128]{2,1,0:T(8,128)S(1)}, f32[128,128]{1,0:T(8,128)S(1)}, f32[8,128]{1,0:T(8,128)S(1)}, bf16[2,128,128]{2,1,0:T(8,128)(2,1)S(1)}, bf...) custom-call(s32[1,1]{1,0:T(1,128)S(6)} %copy.12.count_ref.refs_0_, ...), custom_call_target="tpu_custom_call" | custom-call | tf_op jit(solution)/shard_map/pallas_call | solution.py:372
  13.8 0.0 collective-permute-done.1.refs_4_
  13.8 0.0 collective-permute-done.refs_3_
  13.8 2.1 %shard_map.106 = (f32[3,128,128]{2,1,0:T(8,128)S(1)}, f32[3,128,128]{2,1,0:T(8,128)S(1)}, f32[128,128]{1,0:T(8,128)S(1)}, f32[8,128]{1,0:T(8,128)S(1)}, f32[16,72,128]{2,1,0:T(8,128)}) custom-call(s32[1,1]{1,0:T(1,128)S(6)} %copy.12.count_ref.refs_0_, f32[6,128,128]{2,1,0:T(8,128)S(1)} %get-tuple-element.26.refs_1_, ...), custom_call_target="tpu_custom_call" | custom-call | tf_op jit(solution)/shard_map/pallas_call | solution.py:395
  15.9 8.5 %all-to-all-start = ((f32[16,72,128]{2,1,0:T(8,128)}), f32[16,72,128]{2,1,0:T(8,128)S(1)}, u32[]{:S(2)}, u32[]{:S(2)}) async-start(f32[16,72,128]{2,1,0:T(8,128)} %get-tuple-element.38), calls=%async_computation | async-start | bytes 1179648 | tf_op jit(solution)/shard_map/all_to_all | solution.py:401
  24.4 1.9 %collective-permute-start.2 = (f32[128,128]{1,0:T(8,128)S(1)}, f32[128,128]{1,0:T(8,128)S(1)}, u32[]{:S(2)}, u32[]{:S(2)}) collective-permute-start(f32[128,128]{1,0:T(8,128)S(1)} %get-tuple-element.40), channel_id=1, source_target_pairs={{0,1},{1,2},{2,3},{3,4},{4,5},{5,6},{6,7},{7,8},{8,9},{9,10},{10,1... | collective-permute-start | bytes 196616 | tf_op jit(solution)/shard_map/ppermute | solution.py:403
  26.3 6.4 %collective-permute-done.2.refs_2_.before_ref = f32[128,128]{1,0:T(8,128)S(1)} collective-permute-done((f32[128,128]{1,0:T(8,128)S(1)}, f32[128,128]{1,0:T(8,128)S(1)}, u32[]{:S(2)}, u32[]{:S(2)}) %collective-permute-start.2) | collective-permute-done | bytes 65568 | tf_op jit(solution)/shard_map/ppermute | solution.py:403
  32.8 0.0 all-to-all-done.refs_0_
  32.8 1.2 %shard_map.107 = f32[160,128]{1,0:T(8,128)} custom-call(f32[16,72,128]{2,1,0:T(8,128)S(1)} %all-to-all-done.refs_0_, f32[8,128]{1,0:T(8,128)S(1)} %get-tuple-element.39.refs_1_.edge_ref, f32[128,128]{1,0:T(8,128)S(1)} %collective-permute-done.2.refs_2_.before_ref), custom_call_target="tpu_custom_call" | custom-call | tf_op jit(solution)/shard_map/pallas_call | solution.py:408
  34.0 22.3 %all-to-all-start.1 = ((f32[160,1,128]{2,1,0:T(1,128)}), f32[160,1,128]{2,1,0:T(1,128)S(1)}, u32[]{:S(2)}, u32[]{:S(2)}) async-start(f32[160,1,128]{2,1,0:T(1,128)} %bitcast.6), calls=%async_computation.1 | async-start | bytes 163840 | tf_op jit(solution)/shard_map/all_to_all | solution.py:409
  56.3 2.3 %collective-permute-start.3 = (f32[128,128]{1,0:T(8,128)S(1)}, f32[128,128]{1,0:T(8,128)S(1)}, u32[]{:S(2)}, u32[]{:S(2)}) collective-permute-start(f32[128,128]{1,0:T(8,128)S(1)} %get-tuple-element.40), channel_id=1, source_target_pairs={{1,0},{2,1},{3,2},{4,3},{5,4},{6,5},{7,6},{8,7},{9,8},{10,9},{11,1... | collective-permute-start | bytes 196616 | tf_op jit(solution)/shard_map/ppermute | solution.py:411
  58.6 2.7 %collective-permute-done.3.after_ref = f32[128,128]{1,0:T(8,128)S(1)} collective-permute-done((f32[128,128]{1,0:T(8,128)S(1)}, f32[128,128]{1,0:T(8,128)S(1)}, u32[]{:S(2)}, u32[]{:S(2)}) %collective-permute-start.3) | collective-permute-done | bytes 65568 | tf_op jit(solution)/shard_map/ppermute | solution.py:411
  61.3 1.4 %shard_map.108 = (f32[3,125,1,128]{3,2,1,0:T(1,128)}, f32[8,128]{1,0:T(8,128)S(1)}, f32[8,128]{1,0:T(8,128)S(1)}) custom-call(s32[1,1]{1,0:T(1,128)S(6)} %copy.12.count_ref.refs_0_, f32[6,128,128]{2,1,0:T(8,128)S(1)} %get-tuple-element.24.field_ref, f32[3,128,128]{2,1,0:T(8,128)S(1)} %get-tuple-element.35.one_ref, ...), custom_call_target="tpu_custom_call" | custom-call | tf_op jit(solution)/shard_map/pallas_call | solution.py:412
  62.7 0.0 all-to-all-done.1
  62.7 0.8 %shard_map.109 = f32[4,64]{1,0:T(4,128)} custom-call(f32[160,128]{1,0:T(8,128)S(1)} %bitcast.10, f32[8,128]{1,0:T(8,128)S(1)} %get-tuple-element.44.refs_1_, f32[8,128]{1,0:T(8,128)S(1)} %get-tuple-element.45.refs_2_), custom_call_target="tpu_custom_call" | custom-call | tf_op jit(solution)/shard_map/pallas_call | solution.py:419
Async XLA Ops:
  2.6 11.2 %collective-permute-start.1 = (f32[200,128]{1,0:T(8,128)S(1)}, f32[200,128]{1,0:T(8,128)S(1)}, u32[]{:S(2)}, u32[]{:S(2)}) collective-permute-start(f32[200,128]{1,0:T(8,128)S(1)} %get-tuple-element.28), channel_id=1, source_target_pairs={{0,1},{1,2},{2,3},{3,4},{4,5},{5,6},{6,7},{7,8},{8,9},{9,10},{10,1... | collective-permute-start | bytes 307208 | tf_op jit(solution)/shard_map/ppermute | solution.py:371
  6.6 7.2 %collective-permute-start = (f32[200,128]{1,0:T(8,128)S(1)}, f32[200,128]{1,0:T(8,128)S(1)}, u32[]{:S(2)}, u32[]{:S(2)}) collective-permute-start(f32[200,128]{1,0:T(8,128)S(1)} %get-tuple-element.28), channel_id=1, source_target_pairs={{1,0},{2,1},{3,2},{4,3},{5,4},{6,5},{7,6},{8,7},{9,8},{10,9},{11,1... | collective-permute-start | bytes 307208 | tf_op jit(solution)/shard_map/ppermute | solution.py:371
  15.9 16.8 %all-to-all-start = ((f32[16,72,128]{2,1,0:T(8,128)}), f32[16,72,128]{2,1,0:T(8,128)S(1)}, u32[]{:S(2)}, u32[]{:S(2)}) async-start(f32[16,72,128]{2,1,0:T(8,128)} %get-tuple-element.38), calls=%async_computation | async-start | bytes 1179648 | tf_op jit(solution)/shard_map/all_to_all | solution.py:401
  24.4 8.3 %collective-permute-start.2 = (f32[128,128]{1,0:T(8,128)S(1)}, f32[128,128]{1,0:T(8,128)S(1)}, u32[]{:S(2)}, u32[]{:S(2)}) collective-permute-start(f32[128,128]{1,0:T(8,128)S(1)} %get-tuple-element.40), channel_id=1, source_target_pairs={{0,1},{1,2},{2,3},{3,4},{4,5},{5,6},{6,7},{7,8},{8,9},{9,10},{10,1... | collective-permute-start | bytes 196616 | tf_op jit(solution)/shard_map/ppermute | solution.py:403
  34.0 28.7 %all-to-all-start.1 = ((f32[160,1,128]{2,1,0:T(1,128)}), f32[160,1,128]{2,1,0:T(1,128)S(1)}, u32[]{:S(2)}, u32[]{:S(2)}) async-start(f32[160,1,128]{2,1,0:T(1,128)} %bitcast.6), calls=%async_computation.1 | async-start | bytes 163840 | tf_op jit(solution)/shard_map/all_to_all | solution.py:409
  56.3 5.0 %collective-permute-start.3 = (f32[128,128]{1,0:T(8,128)S(1)}, f32[128,128]{1,0:T(8,128)S(1)}, u32[]{:S(2)}, u32[]{:S(2)}) collective-permute-start(f32[128,128]{1,0:T(8,128)S(1)} %get-tuple-element.40), channel_id=1, source_target_pairs={{1,0},{2,1},{3,2},{4,3},{5,4},{6,5},{7,6},{8,7},{9,8},{10,9},{11,1... | collective-permute-start | bytes 196616 | tf_op jit(solution)/shard_map/ppermute | solution.py:411

commit v12 on v11

--- a/solution.py
+++ b/solution.py
@@ -353,7 +353,7 @@
     forward, adjoint = (x.reshape(3, NODES, 1, 128) for x in (forward_start, adjoint_start))
     up = [(i, (i + 1) % n_mesh) for i in range(n_mesh)]
     down = [(j, i) for i, j in up]
-    first_mesh, first_event = 5 * n_mesh // 8, n_event // 2
+    first_mesh, first_event = 0, n_event // 2
     mesh_group = [(i + first_mesh) % n_mesh for i in range(n_mesh)]
     event_group = [(i + first_event) % n_event for i in range(n_event)]
 

time: 64 us -> 64.3 us (level)
  starting transfers between devices: 44.6 us -> 45.3 us
    all_to_all x1, starting transfers between devices: 8.52 us -> 6.53 us  [per_device(): lax.all_to_all(chunk, 'mesh', 0, 0, tiled=True, axis_index_groups=[mesh_g...]
    ppermute x1, starting transfers between devices: 1.91 us -> 3.26 us  [per_device(): before = lax.ppermute(rim_one, 'mesh', up)]
    all_to_all x1, starting transfers between devices: 22.3 us -> 23.1 us  [per_device(): lax.all_to_all(partial.reshape(-1, 1, 128), 'event', 0, 0, tiled=True, ax...]
where the time goes in v12:
time: 64.3 us; the launch traced here: 63.9 us
  starting transfers between devices  45.3 us (70%)
  waiting for transfers between devices  8.82 us (14%)
  Pallas kernels  8.43 us (13%)
  between operations  1.35 us (2%)
    all_to_all x1, starting transfers between devices, per_device(): lax.all_to_all(partial.reshape(-1, 1, 128), 'event', 0, 0, tiled=True, ax...  23.1 us
    ppermute x1, waiting for transfers between devices, per_device(): before = lax.ppermute(rim_one, 'mesh', up)  6.53 us
    all_to_all x1, starting transfers between devices, per_device(): lax.all_to_all(chunk, 'mesh', 0, 0, tiled=True, axis_index_groups=[mesh_g...  6.53 us
    ppermute x1, starting transfers between devices, per_device(): lax.ppermute(rim, 'mesh', down)  5.55 us
    ppermute x1, starting transfers between devices, per_device(): lax.ppermute(rim, 'mesh', up)  4.03 us
    ppermute x1, starting transfers between devices, per_device(): before = lax.ppermute(rim_one, 'mesh', up)  3.26 us
    ppermute x1, starting transfers between devices, per_device(): after = lax.ppermute(rim_one, 'mesh', down)  2.78 us
    ppermute x1, waiting for transfers between devices, per_device(): after = lax.ppermute(rim_one, 'mesh', down)  2.24 us
  transfers between devices with their start and end apart: 6, of which 2 were waited for; matrix products, arithmetic and copies ran while one was open for 0% of the time, Pallas kernels for 5%

profile of v12, /device:TPU:1, one launch (start us, length us, event | category | flops | bytes accessed | tf_op | source)
XLA Modules:
  0.0 63.9 jit_solution(12259676269130220750)
XLA Ops:
  1.3 1.3 %shard_map.104 = (f32[200,128]{1,0:T(8,128)S(1)}, f32[6,128,128]{2,1,0:T(8,128)S(1)}, f32[4,4]{1,0:T(4,128)S(1)}) custom-call(s32[1,1]{1,0:T(1,128)S(6)} %copy.12.count_ref.refs_0_, f32[3,125,1,128]{3,2,1,0:T(1,128)} %bitcast.11, f32[3,125,1,128]{3,2,1,0:T(1,128)} %bitcast.12, f32[4,4]{1,0:T(4,128)} %smooth_ref.1), custom_call_target="tpu_custom_call" | custom-call | tf_op jit(solution)/shard_map/pallas_call | solution.py:363
  2.6 4.0 %collective-permute-start.1 = (f32[200,128]{1,0:T(8,128)S(1)}, f32[200,128]{1,0:T(8,128)S(1)}, u32[]{:S(2)}, u32[]{:S(2)}) collective-permute-start(f32[200,128]{1,0:T(8,128)S(1)} %get-tuple-element.28), channel_id=1, source_target_pairs={{0,1},{1,2},{2,3},{3,4},{4,5},{5,6},{6,7},{7,8},{8,9},{9,10},{10,1... | collective-permute-start | bytes 307208 | tf_op jit(solution)/shard_map/ppermute | solution.py:371
  6.6 5.6 %collective-permute-start = (f32[200,128]{1,0:T(8,128)S(1)}, f32[200,128]{1,0:T(8,128)S(1)}, u32[]{:S(2)}, u32[]{:S(2)}) collective-permute-start(f32[200,128]{1,0:T(8,128)S(1)} %get-tuple-element.28), channel_id=1, source_target_pairs={{1,0},{2,1},{3,2},{4,3},{5,4},{6,5},{7,6},{8,7},{9,8},{10,9},{11,1... | collective-permute-start | bytes 307208 | tf_op jit(solution)/shard_map/ppermute | solution.py:371
  12.2 1.6 %shard_map.105 = (f32[6,128,128]{2,1,0:T(8,128)S(1)}, f32[128,128]{1,0:T(8,128)S(1)}, f32[8,128]{1,0:T(8,128)S(1)}, bf16[2,128,128]{2,1,0:T(8,128)(2,1)S(1)}, bf...) custom-call(s32[1,1]{1,0:T(1,128)S(6)} %copy.12.count_ref.refs_0_, ...), custom_call_target="tpu_custom_call" | custom-call | tf_op jit(solution)/shard_map/pallas_call | solution.py:372
  13.8 0.0 collective-permute-done.1.refs_4_
  13.8 0.0 collective-permute-done.refs_3_
  13.8 2.1 %shard_map.106 = (f32[3,128,128]{2,1,0:T(8,128)S(1)}, f32[3,128,128]{2,1,0:T(8,128)S(1)}, f32[128,128]{1,0:T(8,128)S(1)}, f32[8,128]{1,0:T(8,128)S(1)}, f32[16,72,128]{2,1,0:T(8,128)}) custom-call(s32[1,1]{1,0:T(1,128)S(6)} %copy.12.count_ref.refs_0_, f32[6,128,128]{2,1,0:T(8,128)S(1)} %get-tuple-element.26.refs_1_, ...), custom_call_target="tpu_custom_call" | custom-call | tf_op jit(solution)/shard_map/pallas_call | solution.py:395
  15.9 6.5 %all-to-all-start = ((f32[16,72,128]{2,1,0:T(8,128)}), f32[16,72,128]{2,1,0:T(8,128)S(1)}, u32[]{:S(2)}, u32[]{:S(2)}) async-start(f32[16,72,128]{2,1,0:T(8,128)} %get-tuple-element.38), calls=%async_computation | async-start | bytes 1179648 | tf_op jit(solution)/shard_map/all_to_all | solution.py:401
  22.4 3.3 %collective-permute-start.2 = (f32[128,128]{1,0:T(8,128)S(1)}, f32[128,128]{1,0:T(8,128)S(1)}, u32[]{:S(2)}, u32[]{:S(2)}) collective-permute-start(f32[128,128]{1,0:T(8,128)S(1)} %get-tuple-element.40), channel_id=1, source_target_pairs={{0,1},{1,2},{2,3},{3,4},{4,5},{5,6},{6,7},{7,8},{8,9},{9,10},{10,1... | collective-permute-start | bytes 196616 | tf_op jit(solution)/shard_map/ppermute | solution.py:403
  25.7 6.5 %collective-permute-done.2.refs_2_.before_ref = f32[128,128]{1,0:T(8,128)S(1)} collective-permute-done((f32[128,128]{1,0:T(8,128)S(1)}, f32[128,128]{1,0:T(8,128)S(1)}, u32[]{:S(2)}, u32[]{:S(2)}) %collective-permute-start.2) | collective-permute-done | bytes 65568 | tf_op jit(solution)/shard_map/ppermute | solution.py:403
  32.3 0.0 all-to-all-done.refs_0_
  32.3 1.2 %shard_map.107 = f32[160,128]{1,0:T(8,128)} custom-call(f32[16,72,128]{2,1,0:T(8,128)S(1)} %all-to-all-done.refs_0_, f32[8,128]{1,0:T(8,128)S(1)} %get-tuple-element.39.refs_1_.edge_ref, f32[128,128]{1,0:T(8,128)S(1)} %collective-permute-done.2.refs_2_.before_ref), custom_call_target="tpu_custom_call" | custom-call | tf_op jit(solution)/shard_map/pallas_call | solution.py:408
  33.5 23.1 %all-to-all-start.1 = ((f32[160,1,128]{2,1,0:T(1,128)}), f32[160,1,128]{2,1,0:T(1,128)S(1)}, u32[]{:S(2)}, u32[]{:S(2)}) async-start(f32[160,1,128]{2,1,0:T(1,128)} %bitcast.6), calls=%async_computation.1 | async-start | bytes 163840 | tf_op jit(solution)/shard_map/all_to_all | solution.py:409
  56.6 2.8 %collective-permute-start.3 = (f32[128,128]{1,0:T(8,128)S(1)}, f32[128,128]{1,0:T(8,128)S(1)}, u32[]{:S(2)}, u32[]{:S(2)}) collective-permute-start(f32[128,128]{1,0:T(8,128)S(1)} %get-tuple-element.40), channel_id=1, source_target_pairs={{1,0},{2,1},{3,2},{4,3},{5,4},{6,5},{7,6},{8,7},{9,8},{10,9},{11,1... | collective-permute-start | bytes 196616 | tf_op jit(solution)/shard_map/ppermute | solution.py:411
  59.4 2.2 %collective-permute-done.3.after_ref = f32[128,128]{1,0:T(8,128)S(1)} collective-permute-done((f32[128,128]{1,0:T(8,128)S(1)}, f32[128,128]{1,0:T(8,128)S(1)}, u32[]{:S(2)}, u32[]{:S(2)}) %collective-permute-start.3) | collective-permute-done | bytes 65568 | tf_op jit(solution)/shard_map/ppermute | solution.py:411
  61.6 1.4 %shard_map.108 = (f32[3,125,1,128]{3,2,1,0:T(1,128)}, f32[8,128]{1,0:T(8,128)S(1)}, f32[8,128]{1,0:T(8,128)S(1)}) custom-call(s32[1,1]{1,0:T(1,128)S(6)} %copy.12.count_ref.refs_0_, f32[6,128,128]{2,1,0:T(8,128)S(1)} %get-tuple-element.24.field_ref, f32[3,128,128]{2,1,0:T(8,128)S(1)} %get-tuple-element.35.one_ref, ...), custom_call_target="tpu_custom_call" | custom-call | tf_op jit(solution)/shard_map/pallas_call | solution.py:412
  63.0 0.0 all-to-all-done.1
  63.0 0.8 %shard_map.109 = f32[4,64]{1,0:T(4,128)} custom-call(f32[160,128]{1,0:T(8,128)S(1)} %bitcast.10, f32[8,128]{1,0:T(8,128)S(1)} %get-tuple-element.44.refs_1_, f32[8,128]{1,0:T(8,128)S(1)} %get-tuple-element.45.refs_2_), custom_call_target="tpu_custom_call" | custom-call | tf_op jit(solution)/shard_map/pallas_call | solution.py:419
Async XLA Ops:
  2.6 11.2 %collective-permute-start.1 = (f32[200,128]{1,0:T(8,128)S(1)}, f32[200,128]{1,0:T(8,128)S(1)}, u32[]{:S(2)}, u32[]{:S(2)}) collective-permute-start(f32[200,128]{1,0:T(8,128)S(1)} %get-tuple-element.28), channel_id=1, source_target_pairs={{0,1},{1,2},{2,3},{3,4},{4,5},{5,6},{6,7},{7,8},{8,9},{9,10},{10,1... | collective-permute-start | bytes 307208 | tf_op jit(solution)/shard_map/ppermute | solution.py:371
  6.6 7.2 %collective-permute-start = (f32[200,128]{1,0:T(8,128)S(1)}, f32[200,128]{1,0:T(8,128)S(1)}, u32[]{:S(2)}, u32[]{:S(2)}) collective-permute-start(f32[200,128]{1,0:T(8,128)S(1)} %get-tuple-element.28), channel_id=1, source_target_pairs={{1,0},{2,1},{3,2},{4,3},{5,4},{6,5},{7,6},{8,7},{9,8},{10,9},{11,1... | collective-permute-start | bytes 307208 | tf_op jit(solution)/shard_map/ppermute | solution.py:371
  15.9 16.3 %all-to-all-start = ((f32[16,72,128]{2,1,0:T(8,128)}), f32[16,72,128]{2,1,0:T(8,128)S(1)}, u32[]{:S(2)}, u32[]{:S(2)}) async-start(f32[16,72,128]{2,1,0:T(8,128)} %get-tuple-element.38), calls=%async_computation | async-start | bytes 1179648 | tf_op jit(solution)/shard_map/all_to_all | solution.py:401
  22.4 9.8 %collective-permute-start.2 = (f32[128,128]{1,0:T(8,128)S(1)}, f32[128,128]{1,0:T(8,128)S(1)}, u32[]{:S(2)}, u32[]{:S(2)}) collective-permute-start(f32[128,128]{1,0:T(8,128)S(1)} %get-tuple-element.40), channel_id=1, source_target_pairs={{0,1},{1,2},{2,3},{3,4},{4,5},{5,6},{6,7},{7,8},{8,9},{9,10},{10,1... | collective-permute-start | bytes 196616 | tf_op jit(solution)/shard_map/ppermute | solution.py:403
  33.5 29.5 %all-to-all-start.1 = ((f32[160,1,128]{2,1,0:T(1,128)}), f32[160,1,128]{2,1,0:T(1,128)S(1)}, u32[]{:S(2)}, u32[]{:S(2)}) async-start(f32[160,1,128]{2,1,0:T(1,128)} %bitcast.6), calls=%async_computation.1 | async-start | bytes 163840 | tf_op jit(solution)/shard_map/all_to_all | solution.py:409
  56.6 5.0 %collective-permute-start.3 = (f32[128,128]{1,0:T(8,128)S(1)}, f32[128,128]{1,0:T(8,128)S(1)}, u32[]{:S(2)}, u32[]{:S(2)}) collective-permute-start(f32[128,128]{1,0:T(8,128)S(1)} %get-tuple-element.40), channel_id=1, source_target_pairs={{1,0},{2,1},{3,2},{4,3},{5,4},{6,5},{7,6},{8,7},{9,8},{10,9},{11,1... | collective-permute-start | bytes 196616 | tf_op jit(solution)/shard_map/ppermute | solution.py:411

commit v13 on v11

--- a/solution.py
+++ b/solution.py
@@ -251,7 +251,7 @@
         strain_ref[c] = strain[c]
 
 
-def dense_kernel(n_event, n_mesh, tile_width, first, parts_ref, edge_ref, before_ref, out_ref):
+def dense_kernel(n_event, n_mesh, tile_width, first, parts_ref, edge_ref, after_ref, out_ref):
     rows = 8 * n_event
     row = iota((rows, 128), 0)
     tile = (row % n_event + first) % n_event * (n_mesh * tile_width) + row // n_event - 2
@@ -400,15 +400,15 @@
     )(counts, partial, kernel, after, before, near, stiff, pick, lift, project, wanted)
     parts = lax.all_to_all(chunk, "mesh", 0, 0, tiled=True, axis_index_groups=[mesh_group])
 
-    before = lax.ppermute(rim_one, "mesh", up)
+    after = lax.ppermute(rim_one, "mesh", down)
 
     def dense(*refs):
         dense_kernel(n_event, n_mesh, tile_width, first_event, *refs)
 
-    partial = call(dense, shape(5 * n_event, 128), 0, 3)(parts, edge, before)
+    partial = call(dense, shape(5 * n_event, 128), 0, 3)(parts, edge, after)
     pieces = lax.all_to_all(partial.reshape(-1, 1, 128), "event", 0, 0, tiled=True, axis_index_groups=[event_group])
     rim_one, _ = lax.optimization_barrier((rim_one, partial))
-    after = lax.ppermute(rim_one, "mesh", down)
+    before = lax.ppermute(rim_one, "mesh", up)
     final, table, is_open = call(last_kernel, (shape(3, NODES, 1, 128), shape(8, 128), shape(8, 128)), 1, 11)(
         counts, fields, one, strain, after, before, near, material, pick, lift, turned, edge
     )

time: 64 us -> 64.8 us (1.012)
  starting transfers between devices: 44.6 us -> 46.1 us
  waiting for transfers between devices: 9.19 us -> 8.49 us
    all_to_all x1, starting transfers between devices: 22.3 us -> 23.1 us  [per_device(): lax.all_to_all(partial.reshape(-1, 1, 128), 'event', 0, 0, tiled=True, ax...]
    ppermute x1, starting transfers between devices: 1.91 us -> 2.69 us  [per_device(): before = lax.ppermute(rim_one, 'mesh', up)]
    ppermute x1, waiting for transfers between devices: 6.4 us -> 5.63 us  [per_device(): before = lax.ppermute(rim_one, 'mesh', up)]
where the time goes in v13:
time: 64.8 us; the launch traced here: 64.3 us
  starting transfers between devices  46.1 us (71%)
  waiting for transfers between devices  8.49 us (13%)
  Pallas kernels  8.43 us (13%)
  between operations  1.34 us (2%)
    all_to_all x1, starting transfers between devices, per_device(): lax.all_to_all(partial.reshape(-1, 1, 128), 'event', 0, 0, tiled=True, ax...  23.1 us
    all_to_all x1, starting transfers between devices, per_device(): lax.all_to_all(chunk, 'mesh', 0, 0, tiled=True, axis_index_groups=[mesh_g...  8.52 us
    ppermute x1, waiting for transfers between devices, per_device(): before = lax.ppermute(rim_one, 'mesh', up)  5.63 us
    ppermute x1, starting transfers between devices, per_device(): lax.ppermute(rim, 'mesh', down)  5.55 us
    ppermute x1, starting transfers between devices, per_device(): lax.ppermute(rim, 'mesh', up)  4.03 us
    ppermute x1, waiting for transfers between devices, per_device(): after = lax.ppermute(rim_one, 'mesh', down)  2.81 us
    ppermute x1, starting transfers between devices, per_device(): before = lax.ppermute(rim_one, 'mesh', up)  2.69 us
    ppermute x1, starting transfers between devices, per_device(): after = lax.ppermute(rim_one, 'mesh', down)  2.18 us
  transfers between devices with their start and end apart: 6, of which 2 were waited for; matrix products, arithmetic and copies ran while one was open for 0% of the time, Pallas kernels for 5%

profile of v13, /device:TPU:1, one launch (start us, length us, event | category | flops | bytes accessed | tf_op | source)
XLA Modules:
  0.0 64.3 jit_solution(8633876846441437050)
XLA Ops:
  1.3 1.3 %shard_map.104 = (f32[200,128]{1,0:T(8,128)S(1)}, f32[6,128,128]{2,1,0:T(8,128)S(1)}, f32[4,4]{1,0:T(4,128)S(1)}) custom-call(s32[1,1]{1,0:T(1,128)S(6)} %copy.12.count_ref.refs_0_, f32[3,125,1,128]{3,2,1,0:T(1,128)} %bitcast.11, f32[3,125,1,128]{3,2,1,0:T(1,128)} %bitcast.12, f32[4,4]{1,0:T(4,128)} %smooth_ref.1), custom_call_target="tpu_custom_call" | custom-call | tf_op jit(solution)/shard_map/pallas_call | solution.py:363
  2.6 4.0 %collective-permute-start.1 = (f32[200,128]{1,0:T(8,128)S(1)}, f32[200,128]{1,0:T(8,128)S(1)}, u32[]{:S(2)}, u32[]{:S(2)}) collective-permute-start(f32[200,128]{1,0:T(8,128)S(1)} %get-tuple-element.28), channel_id=1, source_target_pairs={{0,1},{1,2},{2,3},{3,4},{4,5},{5,6},{6,7},{7,8},{8,9},{9,10},{10,1... | collective-permute-start | bytes 307208 | tf_op jit(solution)/shard_map/ppermute | solution.py:371
  6.6 5.6 %collective-permute-start = (f32[200,128]{1,0:T(8,128)S(1)}, f32[200,128]{1,0:T(8,128)S(1)}, u32[]{:S(2)}, u32[]{:S(2)}) collective-permute-start(f32[200,128]{1,0:T(8,128)S(1)} %get-tuple-element.28), channel_id=1, source_target_pairs={{1,0},{2,1},{3,2},{4,3},{5,4},{6,5},{7,6},{8,7},{9,8},{10,9},{11,1... | collective-permute-start | bytes 307208 | tf_op jit(solution)/shard_map/ppermute | solution.py:371
  12.2 1.6 %shard_map.105 = (f32[6,128,128]{2,1,0:T(8,128)S(1)}, f32[128,128]{1,0:T(8,128)S(1)}, f32[8,128]{1,0:T(8,128)S(1)}, bf16[2,128,128]{2,1,0:T(8,128)(2,1)S(1)}, bf...) custom-call(s32[1,1]{1,0:T(1,128)S(6)} %copy.12.count_ref.refs_0_, ...), custom_call_target="tpu_custom_call" | custom-call | tf_op jit(solution)/shard_map/pallas_call | solution.py:372
  13.8 0.0 collective-permute-done.1.refs_4_
  13.8 0.0 collective-permute-done.refs_3_
  13.8 2.1 %shard_map.106 = (f32[3,128,128]{2,1,0:T(8,128)S(1)}, f32[3,128,128]{2,1,0:T(8,128)S(1)}, f32[128,128]{1,0:T(8,128)S(1)}, f32[8,128]{1,0:T(8,128)S(1)}, f32[16,72,128]{2,1,0:T(8,128)}) custom-call(s32[1,1]{1,0:T(1,128)S(6)} %copy.12.count_ref.refs_0_, f32[6,128,128]{2,1,0:T(8,128)S(1)} %get-tuple-element.26.refs_1_, ...), custom_call_target="tpu_custom_call" | custom-call | tf_op jit(solution)/shard_map/pallas_call | solution.py:395
  15.9 8.5 %all-to-all-start = ((f32[16,72,128]{2,1,0:T(8,128)}), f32[16,72,128]{2,1,0:T(8,128)S(1)}, u32[]{:S(2)}, u32[]{:S(2)}) async-start(f32[16,72,128]{2,1,0:T(8,128)} %get-tuple-element.38), calls=%async_computation | async-start | bytes 1179648 | tf_op jit(solution)/shard_map/all_to_all | solution.py:401
  24.4 2.2 %collective-permute-start.2 = (f32[128,128]{1,0:T(8,128)S(1)}, f32[128,128]{1,0:T(8,128)S(1)}, u32[]{:S(2)}, u32[]{:S(2)}) collective-permute-start(f32[128,128]{1,0:T(8,128)S(1)} %get-tuple-element.40), channel_id=1, source_target_pairs={{1,0},{2,1},{3,2},{4,3},{5,4},{6,5},{7,6},{8,7},{9,8},{10,9},{11,1... | collective-permute-start | bytes 196616 | tf_op jit(solution)/shard_map/ppermute | solution.py:403
  26.6 2.8 %collective-permute-done.2.refs_2_.after_ref = f32[128,128]{1,0:T(8,128)S(1)} collective-permute-done((f32[128,128]{1,0:T(8,128)S(1)}, f32[128,128]{1,0:T(8,128)S(1)}, u32[]{:S(2)}, u32[]{:S(2)}) %collective-permute-start.2) | collective-permute-done | bytes 65568 | tf_op jit(solution)/shard_map/ppermute | solution.py:403
  29.4 0.0 all-to-all-done.refs_0_
  29.4 1.2 %shard_map.107 = f32[160,128]{1,0:T(8,128)} custom-call(f32[16,72,128]{2,1,0:T(8,128)S(1)} %all-to-all-done.refs_0_, f32[8,128]{1,0:T(8,128)S(1)} %get-tuple-element.39.refs_1_.edge_ref, f32[128,128]{1,0:T(8,128)S(1)} %collective-permute-done.2.refs_2_.after_ref), custom_call_target="tpu_custom_call" | custom-call | tf_op jit(solution)/shard_map/pallas_call | solution.py:408
  30.7 23.1 %all-to-all-start.1 = ((f32[160,1,128]{2,1,0:T(1,128)}), f32[160,1,128]{2,1,0:T(1,128)S(1)}, u32[]{:S(2)}, u32[]{:S(2)}) async-start(f32[160,1,128]{2,1,0:T(1,128)} %bitcast.6), calls=%async_computation.1 | async-start | bytes 163840 | tf_op jit(solution)/shard_map/all_to_all | solution.py:409
  53.8 2.7 %collective-permute-start.3 = (f32[128,128]{1,0:T(8,128)S(1)}, f32[128,128]{1,0:T(8,128)S(1)}, u32[]{:S(2)}, u32[]{:S(2)}) collective-permute-start(f32[128,128]{1,0:T(8,128)S(1)} %get-tuple-element.40), channel_id=1, source_target_pairs={{0,1},{1,2},{2,3},{3,4},{4,5},{5,6},{6,7},{7,8},{8,9},{9,10},{10,1... | collective-permute-start | bytes 196616 | tf_op jit(solution)/shard_map/ppermute | solution.py:411
  56.5 5.6 %collective-permute-done.3.before_ref = f32[128,128]{1,0:T(8,128)S(1)} collective-permute-done((f32[128,128]{1,0:T(8,128)S(1)}, f32[128,128]{1,0:T(8,128)S(1)}, u32[]{:S(2)}, u32[]{:S(2)}) %collective-permute-start.3) | collective-permute-done | bytes 65568 | tf_op jit(solution)/shard_map/ppermute | solution.py:411
  62.1 1.4 %shard_map.108 = (f32[3,125,1,128]{3,2,1,0:T(1,128)}, f32[8,128]{1,0:T(8,128)S(1)}, f32[8,128]{1,0:T(8,128)S(1)}) custom-call(s32[1,1]{1,0:T(1,128)S(6)} %copy.12.count_ref.refs_0_, f32[6,128,128]{2,1,0:T(8,128)S(1)} %get-tuple-element.24.field_ref, f32[3,128,128]{2,1,0:T(8,128)S(1)} %get-tuple-element.35.one_ref, ...), custom_call_target="tpu_custom_call" | custom-call | tf_op jit(solution)/shard_map/pallas_call | solution.py:412
  63.5 0.0 all-to-all-done.1
  63.5 0.8 %shard_map.109 = f32[4,64]{1,0:T(4,128)} custom-call(f32[160,128]{1,0:T(8,128)S(1)} %bitcast.10, f32[8,128]{1,0:T(8,128)S(1)} %get-tuple-element.44.refs_1_, f32[8,128]{1,0:T(8,128)S(1)} %get-tuple-element.45.refs_2_), custom_call_target="tpu_custom_call" | custom-call | tf_op jit(solution)/shard_map/pallas_call | solution.py:419
Async XLA Ops:
  2.6 11.2 %collective-permute-start.1 = (f32[200,128]{1,0:T(8,128)S(1)}, f32[200,128]{1,0:T(8,128)S(1)}, u32[]{:S(2)}, u32[]{:S(2)}) collective-permute-start(f32[200,128]{1,0:T(8,128)S(1)} %get-tuple-element.28), channel_id=1, source_target_pairs={{0,1},{1,2},{2,3},{3,4},{4,5},{5,6},{6,7},{7,8},{8,9},{9,10},{10,1... | collective-permute-start | bytes 307208 | tf_op jit(solution)/shard_map/ppermute | solution.py:371
  6.6 7.2 %collective-permute-start = (f32[200,128]{1,0:T(8,128)S(1)}, f32[200,128]{1,0:T(8,128)S(1)}, u32[]{:S(2)}, u32[]{:S(2)}) collective-permute-start(f32[200,128]{1,0:T(8,128)S(1)} %get-tuple-element.28), channel_id=1, source_target_pairs={{1,0},{2,1},{3,2},{4,3},{5,4},{6,5},{7,6},{8,7},{9,8},{10,9},{11,1... | collective-permute-start | bytes 307208 | tf_op jit(solution)/shard_map/ppermute | solution.py:371
  15.9 13.5 %all-to-all-start = ((f32[16,72,128]{2,1,0:T(8,128)}), f32[16,72,128]{2,1,0:T(8,128)S(1)}, u32[]{:S(2)}, u32[]{:S(2)}) async-start(f32[16,72,128]{2,1,0:T(8,128)} %get-tuple-element.38), calls=%async_computation | async-start | bytes 1179648 | tf_op jit(solution)/shard_map/all_to_all | solution.py:401
  24.4 5.0 %collective-permute-start.2 = (f32[128,128]{1,0:T(8,128)S(1)}, f32[128,128]{1,0:T(8,128)S(1)}, u32[]{:S(2)}, u32[]{:S(2)}) collective-permute-start(f32[128,128]{1,0:T(8,128)S(1)} %get-tuple-element.40), channel_id=1, source_target_pairs={{1,0},{2,1},{3,2},{4,3},{5,4},{6,5},{7,6},{8,7},{9,8},{10,9},{11,1... | collective-permute-start | bytes 196616 | tf_op jit(solution)/shard_map/ppermute | solution.py:403
  30.7 32.9 %all-to-all-start.1 = ((f32[160,1,128]{2,1,0:T(1,128)}), f32[160,1,128]{2,1,0:T(1,128)S(1)}, u32[]{:S(2)}, u32[]{:S(2)}) async-start(f32[160,1,128]{2,1,0:T(1,128)} %bitcast.6), calls=%async_computation.1 | async-start | bytes 163840 | tf_op jit(solution)/shard_map/all_to_all | solution.py:409
  53.8 8.3 %collective-permute-start.3 = (f32[128,128]{1,0:T(8,128)S(1)}, f32[128,128]{1,0:T(8,128)S(1)}, u32[]{:S(2)}, u32[]{:S(2)}) collective-permute-start(f32[128,128]{1,0:T(8,128)S(1)} %get-tuple-element.40), channel_id=1, source_target_pairs={{0,1},{1,2},{2,3},{3,4},{4,5},{5,6},{6,7},{7,8},{8,9},{9,10},{10,1... | collective-permute-start | bytes 196616 | tf_op jit(solution)/shard_map/ppermute | solution.py:411
